TPU v7x, 32 devices: a whole 2x2x4 slice. The times are simulated.
32 devices in a mesh: dp: 4 (over y, x), seq: 8 (over z, core).
Axes of the slice: x: 2, y: 2, z: 4, core: 2. Of those that a mesh axis runs over, the one named last changes fastest.
Arguments:
- tokens: bfloat16 [4, 2048, 2048], P('dp', 'seq'), may hold values from -6 to 6
- doc_reset: int32 [4, 2048], P('dp', 'seq'), may hold values from 0 to 1, as said below
- cotangent: bfloat16 [4, 2048, 2048], P('dp', 'seq'), may hold values from -6 to 6
- norm_gain: bfloat16 [2048], P(('dp', 'seq')), may hold values from 0.5 to 1.5
- input_proj: bfloat16 [2048, 2560], P(('dp', 'seq')), may hold values from -0.125 to 0.125
- branch_proj: bfloat16 [2048, 2560], P(('dp', 'seq')), may hold values from -0.125 to 0.125
- conv_kernel: bfloat16 [4, 2560], P(None, ('dp', 'seq')), may hold values from -3 to 3
- conv_bias: bfloat16 [2560], P(('dp', 'seq')), may hold values from -3 to 3
- gate_weight: bfloat16 [2, 2560, 256], P(None, ('dp', 'seq')), may hold values from -0.375 to 0.375
- gate_bias: bfloat16 [2, 2560], P(None, ('dp', 'seq')), may hold values from -4 to 4
- decay_param: bfloat16 [2560], P(('dp', 'seq')), may hold values from 4 to 10
- output_proj: bfloat16 [2560, 2048], P(None, ('dp', 'seq')), may hold values from -0.25 to 0.25
- ffn_gain: bfloat16 [2048], P(('dp', 'seq')), may hold values from 0.5 to 1.5
- ffn_gate: bfloat16 [2048, 6144], P(('dp', 'seq')), may hold values from -0.125 to 0.125
- ffn_up: bfloat16 [2048, 6144], P(('dp', 'seq')), may hold values from -0.125 to 0.125
- ffn_down: bfloat16 [6144, 2048], P(('dp', 'seq')), may hold values from -0.109375 to 0.109375
Outputs:
- layer_out: float32 [4, 2048, 2048], P('dp', 'seq')
- input_grad: float32 [4, 2048, 2048], P('dp', 'seq')
- gain_grad: float32 [2048], P(('dp', 'seq'))
- input_proj_grad: float32 [2048, 2560], P(('dp', 'seq'))
- branch_proj_grad: float32 [2048, 2560], P(('dp', 'seq'))
- kernel_grad: float32 [4, 2560], P(None, ('dp', 'seq'))
- conv_bias_grad: float32 [2560], P(('dp', 'seq'))
- gate_weight_grad: float32 [2, 2560, 256], P(None, ('dp', 'seq'))
- gate_bias_grad: float32 [2, 2560], P(None, ('dp', 'seq'))
- decay_grad: float32 [2560], P(('dp', 'seq'))
- output_proj_grad: float32 [2560, 2048], P(None, ('dp', 'seq'))
- ffn_gain_grad: float32 [2048], P(('dp', 'seq'))
- ffn_gate_grad: float32 [2048, 6144], P(('dp', 'seq'))
- ffn_up_grad: float32 [2048, 6144], P(('dp', 'seq'))
- ffn_down_grad: float32 [6144, 2048], P(('dp', 'seq'))
Inputs may be any that keep to these rules, and one draw needn't show every extreme that they name: `doc_reset`: every sequence's first position is 1.
All inputs are finite; a program needn't handle non-finite values.
Results may differ from a plain program's by a relative error of at most 0.0095.
Values may be sent and summed in bfloat16 or wider, within the bound.
No kernel may reach another device: no remote copies, remote signals or barrier semaphores. Data moves between devices by JAX's collectives and lax.ppermute only.
A program may use at most 448 MiB of HBM per device.

v0:
```python
import jax
import jax.numpy as jnp
from jax import lax
from jax.sharding import PartitionSpec as P

EPSILON = 1e-06
POWER = 8.0


def passed_along(block, axis, distance):
    devices = range(lax.axis_size(axis))
    route = [(i - distance, i) for i in devices if i - distance in devices]
    return lax.ppermute(block, axis, route)


def carried_in(part, axis, combine, identity):
    place = lax.axis_index(axis)
    gathered = jax.tree.map(lambda a: lax.all_gather(a, axis), part)
    state = jax.tree.map(lambda a, e: jnp.zeros_like(a) + jnp.asarray(e, a.dtype), part, identity)

    def one(lap, state):
        return combine(
            state, jax.tree.map(lambda a: lax.dynamic_index_in_dim(a, lap, 0, False), gathered)
        )

    return lax.fori_loop(0, place, one, state)


def carried_in_2(x, axis, combine, identity):
    peers, position = (lax.axis_size(axis), lax.axis_index(axis))
    everything = jax.tree.map(
        lambda part, kind: lax.all_gather(part.astype(kind), axis), x, (jnp.bfloat16, jnp.bfloat16)
    )
    start = jax.tree.map(
        lambda part, zero: jnp.broadcast_to(jnp.asarray(zero, part.dtype), part.shape), x, identity
    )

    def lap(k, before):
        at = peers - 1 - k
        reached = at > position
        new = combine(
            before, jax.tree.map(lambda part, own: part[at].astype(own.dtype), everything, x)
        )
        return jax.tree.map(lambda a, b: jnp.where(reached, a, b), new, before)

    return lax.fori_loop(0, peers, lap, start)


def combine(earlier, latter):
    return (earlier[0] * latter[0], latter[0] * earlier[1] + latter[1])


def rglru_terms(rate_pre, open_pre, conved, lam_vals, keeping):
    rate_val = jax.nn.sigmoid(rate_pre)
    open_val = jax.nn.sigmoid(open_pre)
    log_decay = -POWER * rate_val * jax.nn.softplus(-lam_vals)
    decay_val = jnp.exp(log_decay)
    scaling = keeping * jnp.sqrt(-jnp.expm1(2.0 * log_decay)) + (1.0 - keeping)
    return (decay_val * keeping, scaling * open_val * conved)


def norm_apply(tokens_in, gain_vals):
    mean_square = jnp.mean(tokens_in * tokens_in, axis=-1, keepdims=True)
    return tokens_in * lax.rsqrt(mean_square + EPSILON) * gain_vals


def contract_rows(left_side, right_side):
    return lax.dot_general(
        left_side, right_side, (((0,), (0,)), ((), ())), preferred_element_type=jnp.float32
    )


def contract_cols(left_side, right_side):
    return lax.dot_general(
        left_side, right_side, (((1,), (1,)), ((), ())), preferred_element_type=jnp.float32
    )


def body(
    tokens,
    doc_reset,
    cotangent,
    norm_gain,
    input_proj,
    branch_proj,
    conv_kernel,
    conv_bias,
    gate_weight,
    gate_bias,
    decay_param,
    output_proj,
    ffn_gain,
    ffn_gate,
    ffn_up,
    ffn_down,
):
    seq_count, span_len, model_width = tokens.shape
    row_count = seq_count * span_len
    (
        gain_all,
        inproj_all,
        brproj_all,
        kernel_all,
        cbias_all,
        gatew_all,
        gateb_all,
        decay_all,
        outproj_all,
    ) = (
        lax.all_gather(norm_gain, ("dp", "seq"), axis=0, tiled=True),
        lax.all_gather(input_proj, ("dp", "seq"), axis=0, tiled=True),
        lax.all_gather(branch_proj, ("dp", "seq"), axis=0, tiled=True),
        lax.all_gather(conv_kernel, ("dp", "seq"), axis=1, tiled=True),
        lax.all_gather(conv_bias, ("dp", "seq"), axis=0, tiled=True),
        lax.all_gather(gate_weight, ("dp", "seq"), axis=1, tiled=True),
        lax.all_gather(gate_bias, ("dp", "seq"), axis=1, tiled=True),
        lax.all_gather(decay_param, ("dp", "seq"), axis=0, tiled=True),
        lax.all_gather(output_proj, ("dp", "seq"), axis=1, tiled=True),
    )
    fgain_all, fgate_all, fup_all, fdown_all = (
        lax.all_gather(ffn_gain, ("dp", "seq"), axis=0, tiled=True),
        lax.all_gather(ffn_gate, ("dp", "seq"), axis=0, tiled=True),
        lax.all_gather(ffn_up, ("dp", "seq"), axis=0, tiled=True),
        lax.all_gather(ffn_down, ("dp", "seq"), axis=0, tiled=True),
    )
    rec_width = inproj_all.shape[1]
    ff_width = fgate_all.shape[1]
    block_width = gatew_all.shape[2]
    block_count = rec_width // block_width
    tap_count = kernel_all.shape[0]
    flat_tokens = tokens.reshape(row_count, model_width).astype(jnp.float32)
    gain_vals = gain_all.astype(jnp.float32)
    normed_val, norm_back = jax.vjp(norm_apply, flat_tokens, gain_vals)
    normed = normed_val.astype(jnp.bfloat16)
    inner_val = jnp.dot(normed, inproj_all, preferred_element_type=jnp.float32).astype(jnp.bfloat16)
    inner_val = inner_val.reshape(seq_count, span_len, rec_width)
    branch = jnp.dot(normed, brproj_all, preferred_element_type=jnp.float32)
    activated, gelu_back = jax.vjp(jax.nn.gelu, branch)
    left_rim = passed_along(inner_val[:, span_len - tap_count + 1 :], "seq", 1)
    extended = jnp.concatenate([left_rim, inner_val], axis=1)
    kernel = kernel_all.astype(jnp.float32)
    conved = cbias_all.astype(jnp.float32) + jnp.zeros(
        (seq_count, span_len, rec_width), jnp.float32
    )
    for offset in range(tap_count):
        conved = conved + kernel[offset] * extended[
            :, tap_count - 1 - offset : tap_count - 1 - offset + span_len
        ].astype(jnp.float32)
    rounded = conved.astype(jnp.bfloat16).reshape(row_count, block_count, block_width)
    gate_blocks = gatew_all.reshape(2, block_count, block_width, block_width)
    mixing = jnp.einsum("rhj,khjm->krhm", rounded, gate_blocks, preferred_element_type=jnp.float32)
    mixing = (
        mixing.reshape(2, seq_count, span_len, rec_width)
        + gateb_all.astype(jnp.float32)[:, None, None, :]
    )
    keeping = (1 - doc_reset).astype(jnp.float32)[..., None]
    lam_vals = decay_all.astype(jnp.float32)
    (decay_rate, driven), term_back = jax.vjp(
        lambda rate_in, open_in, conv_in, lam_in: rglru_terms(
            rate_in, open_in, conv_in, lam_in, keeping
        ),
        mixing[0],
        mixing[1],
        conved,
        lam_vals,
    )
    cum_decay, local_state = lax.associative_scan(combine, (decay_rate, driven), axis=1)
    identity_pair = (jnp.ones_like(cum_decay[:, -1]), jnp.zeros_like(local_state[:, -1]))
    prefix = carried_in((cum_decay[:, -1], local_state[:, -1]), "seq", combine, identity_pair)
    start_state = prefix[1]
    hidden = local_state + cum_decay * start_state[:, None, :]
    previous = jnp.concatenate([start_state[:, None, :], hidden[:, :-1]], axis=1)
    mixed_out = (hidden.reshape(row_count, rec_width) * activated).astype(jnp.bfloat16)
    middle = flat_tokens + jnp.dot(mixed_out, outproj_all, preferred_element_type=jnp.float32)
    fgain_vals = fgain_all.astype(jnp.float32)
    fnormed_val, ffn_norm_back = jax.vjp(norm_apply, middle, fgain_vals)
    ffn_normed = fnormed_val.astype(jnp.bfloat16)
    ffn_pre = jnp.dot(ffn_normed, fgate_all, preferred_element_type=jnp.float32)
    ffn_lin = jnp.dot(ffn_normed, fup_all, preferred_element_type=jnp.float32)
    gelu_pre, ffn_gelu_back = jax.vjp(jax.nn.gelu, ffn_pre)
    ffn_hidden = (gelu_pre * ffn_lin).astype(jnp.bfloat16)
    layer_out = middle + jnp.dot(ffn_hidden, fdown_all, preferred_element_type=jnp.float32)
    cot_flat = cotangent.reshape(row_count, model_width)
    hid_grad = contract_cols(cot_flat, fdown_all)
    pre_grad = ffn_gelu_back(hid_grad * ffn_lin)[0].astype(jnp.bfloat16)
    lin_grad = (hid_grad * gelu_pre).astype(jnp.bfloat16)
    ffn_normed_grad = contract_cols(pre_grad, fgate_all) + contract_cols(lin_grad, fup_all)
    mid_part, fgain_grad = ffn_norm_back(ffn_normed_grad)
    mid_grad = cot_flat.astype(jnp.float32) + mid_part
    mid_low = mid_grad.astype(jnp.bfloat16)
    column_block = ffn_normed
    ffn_in_parts = lax.psum_scatter(
        jnp.concatenate(
            [contract_rows(column_block, pre_grad), contract_rows(column_block, lin_grad)], axis=1
        ),
        ("dp", "seq"),
        scatter_dimension=0,
        tiled=True,
    )
    fgate_part = ffn_in_parts[:, :ff_width]
    fup_part = ffn_in_parts[:, ff_width:]
    column_block = ffn_hidden
    fdown_part = lax.psum_scatter(
        contract_rows(column_block, cot_flat), ("dp", "seq"), scatter_dimension=0, tiled=True
    )
    mixed_grad = contract_cols(mid_low, outproj_all)
    outproj_grad = contract_rows(mixed_out, mid_low)
    hidden_grad = (mixed_grad * activated).reshape(seq_count, span_len, rec_width)
    branch_grad = gelu_back(mixed_grad * hidden.reshape(row_count, rec_width))[0].astype(
        jnp.bfloat16
    )
    flipped_decay = jnp.flip(decay_rate, 1)
    back_prod, back_state = lax.associative_scan(
        combine, (flipped_decay, flipped_decay * jnp.flip(hidden_grad, 1)), axis=1
    )
    back_prod = jnp.flip(back_prod, 1)
    back_state = jnp.flip(back_state, 1)
    identity_pair = (jnp.ones_like(back_prod[:, 0]), jnp.zeros_like(back_state[:, 0]))
    suffix = carried_in_2((back_prod[:, 0], back_state[:, 0]), "seq", combine, identity_pair)
    right_carry = suffix[1]
    full_state = back_state + back_prod * right_carry[:, None, :]
    next_state = jnp.concatenate([full_state[:, 1:], right_carry[:, None, :]], axis=1)
    adjoint = hidden_grad + next_state
    rate_grad, open_grad, conved_direct, decay_grad = term_back((adjoint * previous, adjoint))
    mixing_grad = (
        jnp.stack([rate_grad, open_grad])
        .astype(jnp.bfloat16)
        .reshape(2, row_count, block_count, block_width)
    )
    conved_grad = conved_direct + jnp.einsum(
        "krhm,khjm->rhj", mixing_grad, gate_blocks, preferred_element_type=jnp.float32
    ).reshape(seq_count, span_len, rec_width)
    gatew_grad = jnp.einsum(
        "rhj,krhm->khjm", rounded, mixing_grad, preferred_element_type=jnp.float32
    ).reshape(2, rec_width, block_width)
    gateb_grad = jnp.sum(mixing_grad, axis=1, dtype=jnp.float32).reshape(2, rec_width)
    right_rim = passed_along(
        conved_grad[:, : tap_count - 1].astype(jnp.bfloat16), "seq", -1
    ).astype(jnp.float32)
    padded_grad = jnp.concatenate([conved_grad, right_rim], axis=1)
    inner_grad = jnp.zeros((seq_count, span_len, rec_width), jnp.float32)
    kernel_terms = []
    for offset in range(tap_count):
        inner_grad = inner_grad + kernel[offset] * padded_grad[:, offset : offset + span_len]
        window = extended[:, tap_count - 1 - offset : tap_count - 1 - offset + span_len]
        kernel_terms.append(jnp.sum(window * conved_grad, axis=(0, 1)))
    kernel_grad = jnp.stack(kernel_terms)
    cbias_grad = jnp.sum(conved_grad, axis=(0, 1))
    inner_low = inner_grad.astype(jnp.bfloat16).reshape(row_count, rec_width)
    normed_grad = contract_cols(inner_low, inproj_all) + contract_cols(branch_grad, brproj_all)
    token_grad, gain_grad = norm_back(normed_grad)
    input_grad = mid_grad + token_grad
    inproj_grad = contract_rows(normed, inner_low)
    brproj_grad = contract_rows(normed, branch_grad)
    summed = (
        lax.psum_scatter(gain_grad, ("dp", "seq"), scatter_dimension=0, tiled=True),
        lax.psum_scatter(inproj_grad, ("dp", "seq"), scatter_dimension=0, tiled=True),
        lax.psum_scatter(brproj_grad, ("dp", "seq"), scatter_dimension=0, tiled=True),
        lax.psum_scatter(kernel_grad, ("dp", "seq"), scatter_dimension=1, tiled=True),
        lax.psum_scatter(cbias_grad, ("dp", "seq"), scatter_dimension=0, tiled=True),
        lax.psum_scatter(gatew_grad, ("dp", "seq"), scatter_dimension=1, tiled=True),
        lax.psum_scatter(gateb_grad, ("dp", "seq"), scatter_dimension=1, tiled=True),
        lax.psum_scatter(decay_grad, ("dp", "seq"), scatter_dimension=0, tiled=True),
        lax.psum_scatter(outproj_grad, ("dp", "seq"), scatter_dimension=1, tiled=True),
        lax.psum_scatter(fgain_grad, ("dp", "seq"), scatter_dimension=0, tiled=True),
    )
    (
        gain_part,
        inproj_part,
        brproj_part,
        kernel_part,
        cbias_part,
        gatew_part,
        gateb_part,
        decay_part,
        outproj_part,
        fgain_part,
    ) = summed
    return (
        layer_out.reshape(seq_count, span_len, model_width),
        input_grad.reshape(seq_count, span_len, model_width),
        gain_part,
        inproj_part,
        brproj_part,
        kernel_part,
        cbias_part,
        gatew_part,
        gateb_part,
        decay_part,
        outproj_part,
        fgain_part,
        fgate_part,
        fup_part,
        fdown_part,
    )


def solution(mesh):
    placed = (
        P("dp", "seq", None),
        P("dp", "seq"),
        P("dp", "seq", None),
        P(("dp", "seq")),
        P(("dp", "seq"), None),
        P(("dp", "seq"), None),
        P(None, ("dp", "seq")),
        P(("dp", "seq")),
        P(None, ("dp", "seq"), None),
        P(None, ("dp", "seq")),
        P(("dp", "seq")),
        P(None, ("dp", "seq")),
        P(("dp", "seq")),
        P(("dp", "seq"), None),
        P(("dp", "seq"), None),
        P(("dp", "seq"), None),
    )
    return jax.shard_map(
        body,
        mesh=mesh,
        in_specs=placed,
        out_specs=(
            P("dp", "seq", None),
            P("dp", "seq", None),
            P(("dp", "seq")),
            P(("dp", "seq"), None),
            P(("dp", "seq"), None),
            P(None, ("dp", "seq")),
            P(("dp", "seq")),
            P(None, ("dp", "seq"), None),
            P(None, ("dp", "seq")),
            P(("dp", "seq")),
            P(None, ("dp", "seq")),
            P(("dp", "seq")),
            P(("dp", "seq"), None),
            P(("dp", "seq"), None),
            P(("dp", "seq"), None),
        ),
        check_vma=False,
    )
```

profile of v0, /device:TPU:0, one launch (start us, length us, event | category | flops | bytes accessed | tf_op | source)
XLA Modules:
  0.0 3502.1 jit_solution(3724003910627106649)
XLA Ops:
  13.1 42.7 %all-reduce.73 = (bf16[2560]{0:T(1024)(128)(2,1)S(1)}, bf16[2048]{0:T(1024)(128)(2,1)S(1)}, bf16[2560]{0:T(1024)(128)(2,1)S(1)}, bf16[2048]{0:T(1024)(128)(2,1)S(1)}) all-reduce(bf16[2560]{0:T(1024)(128)(2,1)S(1)} %dynamic-update-slice.2, bf16[2048]{0:T(1024)(128)(2,1)S(1)} %dynamic-update-slice.1, ...), channel_id=1, replica_groups=mesh['dp'=4,'seq'=8] {'dp','seq'}, use_global_device_ids=true, to_apply=%add.66 | all-reduce | flops 9216 | bytes 36864
  55.8 41.1 %all-gather = bf16[32,80,4]{1,2,0:T(4,128)(2,1)S(1)} all-gather(bf16[1,80,4]{1,2,0:T(4,128)(2,1)S(1)} %bitcast.270), channel_id=1, replica_groups=mesh['dp'=4,'seq'=8] {'dp','seq'}, dimensions={0}, use_global_device_ids=true | all-gather | bytes 21120 | tf_op jit(solution)/shard_map/all_gather | solution.py:113
  97.0 36.5 %all-gather.1 = bf16[32,80,2]{1,2,0:T(2,128)(2,1)S(1)} all-gather(bf16[1,80,2]{1,2,0:T(2,128)(2,1)S(1)} %bitcast.271), channel_id=1, replica_groups=mesh['dp'=4,'seq'=8] {'dp','seq'}, dimensions={0}, use_global_device_ids=true | all-gather | bytes 10560 | tf_op jit(solution)/shard_map/all_gather | solution.py:116
  280.6 13.2 rev.13
  401.4 14.1 all_gather.60
  416.4 14.2 all_gather.61
  454.1 39.8 %all-gather.20.cloned.1.call-done = bf16[2048,6144]{1,0:T(8,128)(2,1)} async-done(((bf16[64,6144]{1,0:T(8,128)(2,1)}), bf16[2048,6144]{1,0:T(8,128)(2,1)}) %all-gather.20.cloned.1.call-update) | async-done | bytes 25165840 | tf_op jit(solution)/shard_map/all_gather | solution.py:123
  493.9 14.2 fusion.140
  508.1 141.6 %all-gather.18.cloned.1.call-done = bf16[2048,6144]{1,0:T(8,128)(2,1)} async-done(((bf16[64,6144]{1,0:T(8,128)(2,1)}), bf16[2048,6144]{1,0:T(8,128)(2,1)}) %all-gather.18.cloned.1.call-update) | async-done | bytes 25165840 | tf_op jit(solution)/shard_map/all_gather | solution.py:122
  649.6 14.3 fusion.139
  663.9 141.6 %all-gather.22.cloned.1.call-done = bf16[6144,2048]{1,0:T(8,128)(2,1)} async-done(((bf16[192,2048]{1,0:T(8,128)(2,1)}), bf16[6144,2048]{1,0:T(8,128)(2,1)}) %all-gather.22.cloned.1.call-update) | async-done | bytes 25165840 | tf_op jit(solution)/shard_map/all_gather | solution.py:124
  805.5 21.8 multiply_convert_fusion
  827.3 13.5 fusion.141
  840.8 15.3 multiply_reduce_fusion
  870.1 13.1 reverse.9
  969.6 20.8 rev.15
  990.4 13.9 all_gather.69
  1004.3 20.9 rev.16
  1025.3 13.9 all_gather.68
  1070.2 21.2 fusion.144
  1091.5 21.6 fusion.143
  1128.9 65.1 %pad_maximum_fusion = f32[2048,12288]{1,0:T(8,128)} fusion(f32[2048,6144]{1,0:T(8,128)} %fusion.144, f32[2048,6144]{1,0:T(8,128)} %fusion.143), kind=kLoop, calls=%fused_computation.6 | loop fusion | flops 25165824 | bytes 201326592 | tf_op jit(solution)/shard_map/concatenate | solution.py:193
  1241.4 20.7 fusion.89
  1269.2 13.4 fusion.63
  1291.3 41.4 %all-reduce.72 = (f32[2048]{0:T(1024)S(1)}, f32[2560]{0:T(1024)S(1)}, f32[2560]{0:T(1024)S(1)}, f32[2048]{0:T(1024)S(1)}) all-reduce(f32[2048]{0:T(1024)S(1)} %get-tuple-element.216, f32[2560]{0:T(1024)S(1)} %copy-done.69, f32[2560]{0:T(1024)S(1)} %copy-done.68, ...), channel_id=2, replica_groups=mesh['dp'=4,'seq'=8] {'dp','seq'}, use_global_device_ids=true, to_apply=%region_9.10.clone | all-reduce | flops 9216 | bytes 73728
  1339.9 55.0 %reduce-scatter.25.cloned.1.call-done = f32[80,4]{1,0:T(8,128)} async-done(((f32[2560,4]{1,0:T(8,128)}), f32[80,4]{1,0:T(8,128)}) %reduce-scatter.25.cloned.1.call-update) | async-done | bytes 1296
  1396.3 828.0 %reduce-scatter.21.cloned.1.call-done = f32[64,12288]{1,0:T(8,128)} async-done(((f32[2048,12288]{1,0:T(8,128)}), f32[64,12288]{1,0:T(8,128)}) %reduce-scatter.21.cloned.1.call-update) | async-done | bytes 3145744 | tf_op jit(solution)/shard_map/reduce_scatter | solution.py:192
  2228.2 143.0 %reduce-scatter.17.cloned.1.call-done = f32[2,80,256]{2,1,0:T(8,128)} async-done(((f32[2,2560,256]{2,1,0:T(8,128)}), f32[2,80,256]{2,1,0:T(8,128)}) %reduce-scatter.17.cloned.1.call-update) | async-done | bytes 163856 | tf_op jit(solution)/shard_map/reduce_scatter | solution.py:261
  2371.2 230.0 %reduce-scatter.19.cloned.1.call-done = f32[2560,64]{0,1:T(8,128)} async-done(((f32[2560,2048]{0,1:T(8,128)}), f32[2560,64]{0,1:T(8,128)}) %reduce-scatter.19.cloned.1.call-update) | async-done | bytes 655376 | tf_op jit(solution)/shard_map/reduce_scatter | solution.py:264
  2601.1 229.7 %reduce-scatter.15.cloned.1.call-done = f32[64,2560]{1,0:T(8,128)} async-done(((f32[2048,2560]{1,0:T(8,128)}), f32[64,2560]{1,0:T(8,128)}) %reduce-scatter.15.cloned.1.call-update) | async-done | bytes 655376 | tf_op jit(solution)/shard_map/reduce_scatter | solution.py:258
  2830.9 229.6 %reduce-scatter.13.cloned.1.call-done = f32[64,2560]{1,0:T(8,128)} async-done(((f32[2048,2560]{1,0:T(8,128)}), f32[64,2560]{1,0:T(8,128)}) %reduce-scatter.13.cloned.1.call-update) | async-done | bytes 655376 | tf_op jit(solution)/shard_map/reduce_scatter | solution.py:257
  3060.5 434.9 %reduce-scatter.23.cloned.1.call-done = f32[192,2048]{1,0:T(8,128)} async-done(((f32[6144,2048]{1,0:T(8,128)}), f32[192,2048]{1,0:T(8,128)}) %reduce-scatter.23.cloned.1.call-update) | async-done | bytes 1572880 | tf_op jit(solution)/shard_map/reduce_scatter | solution.py:203
  (566 shorter events, 506.1 us)
Async XLA Ops:
  7.2 48.6 %copy-start.83 = (bf16[4,80]{1,0:T(4,128)(2,1)S(1)}, bf16[4,80]{1,0:T(4,128)(2,1)}, u32[]{:S(2)}) copy-start(bf16[4,80]{1,0:T(4,128)(2,1)} %param.26) | copy-start | bytes 1924
  7.2 89.7 %copy-start.85 = (bf16[2,80]{1,0:T(2,128)(2,1)S(1)}, bf16[2,80]{1,0:T(2,128)(2,1)}, u32[]{:S(2)}) copy-start(bf16[2,80]{1,0:T(2,128)(2,1)} %param.29) | copy-start | bytes 964
  7.2 126.2 %copy-start.3 = (bf16[1,256,2048]{2,1,0:T(8,128)(2,1)S(1)}, bf16[1,256,2048]{2,1,0:T(8,128)(2,1)}, u32[]{:S(2)}) copy-start(bf16[1,256,2048]{2,1,0:T(8,128)(2,1)} %param.20) | copy-start | bytes 3145732
  7.3 126.5 %copy-start.84 = (s32[1,256]{1,0:T(1,128)S(1)}, s32[1,256]{1,0:T(1,128)}, u32[]{:S(2)}) copy-start(s32[1,256]{1,0:T(1,128)} %param.21) | copy-start | bytes 3076
  7.3 127.1 %all-gather.10.cloned.1.call-start = ((), (), s32[]{:S(2)}) async-start(), calls=%async_computation.8 | async-start | bytes 10813440 | tf_op jit(solution)/shard_map/all_gather | solution.py:111
  8.0 152.5 %all-gather.12.cloned.1.call-start = ((), (), s32[]{:S(2)}) async-start(), calls=%async_computation.9 | async-start | bytes 2703360 | tf_op jit(solution)/shard_map/all_gather | solution.py:115
  8.7 422.0 %all-gather.14.cloned.1.call-start = ((), (), s32[]{:S(2)}) async-start(), calls=%async_computation.10 | async-start | bytes 10813440 | tf_op jit(solution)/shard_map/all_gather | solution.py:112
  9.5 433.8 %all-gather.16.cloned.1.call-start = ((), (), s32[]{:S(2)}) async-start(), calls=%async_computation.11 | async-start | bytes 10813440 | tf_op jit(solution)/shard_map/all_gather | solution.py:118
  10.1 483.8 %all-gather.20.cloned.1.call-start = ((), (), s32[]{:S(2)}) async-start(), calls=%async_computation.13 | async-start | bytes 25952256 | tf_op jit(solution)/shard_map/all_gather | solution.py:123
  10.6 639.0 %all-gather.18.cloned.1.call-start = ((), (), s32[]{:S(2)}) async-start(), calls=%async_computation.12 | async-start | bytes 25952256 | tf_op jit(solution)/shard_map/all_gather | solution.py:122
  11.2 794.3 %all-gather.22.cloned.1.call-start = ((), (), s32[]{:S(2)}) async-start(), calls=%async_computation.14 | async-start | bytes 25952256 | tf_op jit(solution)/shard_map/all_gather | solution.py:124
  12.0 1326.5 %reduce-scatter.27.cloned.1.call-start = ((), (), s32[]{:S(2)}) async-start(), calls=%async_computation.22 | async-start | bytes 1351680
  55.8 78.1 %copy-start.76 = (bf16[2560]{0:T(1024)(128)(2,1)}, bf16[2560]{0:T(1024)(128)(2,1)S(1)}, u32[]{:S(2)}) copy-start(bf16[2560]{0:T(1024)(128)(2,1)S(1)} %get-tuple-element.248) | copy-start | bytes 15364
  55.8 374.9 %copy-start.47 = (f32[2048]{0:T(1024)}, f32[2048]{0:T(1024)S(1)}, u32[]{:S(2)}) copy-start(f32[2048]{0:T(1024)S(1)} %convert_element_type.157) | copy-start | bytes 24580
  133.8 297.0 %copy-start.62 = (f32[256]{0:T(256)}, f32[256]{0:T(256)S(1)}, u32[]{:S(2)}) copy-start(f32[256]{0:T(256)S(1)} %fusion.121) | copy-start | bytes 3076
  133.8 41.3 %copy-start.66 = (f32[1,256]{1,0:T(1,128)}, f32[1,256]{1,0:T(1,128)S(1)}, u32[]{:S(2)}) copy-start(f32[1,256]{1,0:T(1,128)S(1)} %subtract_convert_fusion) | copy-start | bytes 3076
  133.8 41.3 %copy-start.78 = (f32[256]{0:T(256)}, f32[256]{0:T(256)S(1)}, u32[]{:S(2)}) copy-start(f32[256]{0:T(256)S(1)} %broadcast_subtract_fusion) | copy-start | bytes 3076
  134.3 40.8 %copy-start.52 = (f32[2560]{0:T(1024)}, f32[2560]{0:T(1024)S(1)}, u32[]{:S(2)}) copy-start(f32[2560]{0:T(1024)S(1)} %broadcast_multiply_fusion) | copy-start | bytes 30724
  141.3 3.0 collective-permute-start
  449.5 406.6 %copy-start.22 = (f32[256,2048]{1,0:T(8,128)}, f32[256,2048]{1,0:T(8,128)S(1)}, u32[]{:S(2)}) copy-start(f32[256,2048]{1,0:T(8,128)S(1)} %get-tuple-element.345) | copy-start | bytes 6291460
  449.8 199.8 %copy-start.13 = (bf16[256,2048]{1,0:T(8,128)(2,1)}, bf16[256,2048]{1,0:T(8,128)(2,1)S(1)}, u32[]{:S(2)}) copy-start(bf16[256,2048]{1,0:T(8,128)(2,1)S(1)} %multiply_convert_fusion.2) | copy-start | bytes 3145732
  1004.3 38.7 %slice-start = ((s8[5242880]{0:T(1024)(128)(4,1)}), s8[1048576]{0:T(1024)(128)(4,1)S(1)}, s32[]{:S(2)}) async-start(s8[5242880]{0:T(1024)(128)(4,1)} %bitcast.242), calls=%async_computation.23 | async-start | bytes 2097152
  1127.2 267.7 %reduce-scatter.25.cloned.1.call-start = ((), (), s32[]{:S(2)}) async-start(), calls=%async_computation.21 | async-start | bytes 1351680
  1128.9 1095.4 %reduce-scatter.21.cloned.1.call-start = ((), (), s32[]{:S(2)}) async-start(), calls=%async_computation.19 | async-start | bytes 103809024 | tf_op jit(solution)/shard_map/reduce_scatter | solution.py:192
  1194.1 1177.1 %reduce-scatter.17.cloned.1.call-start = ((), (), s32[]{:S(2)}) async-start(), calls=%async_computation.17 | async-start | bytes 5406720 | tf_op jit(solution)/shard_map/reduce_scatter | solution.py:261
  1199.9 1401.3 %reduce-scatter.19.cloned.1.call-start = ((), (), s32[]{:S(2)}) async-start(), calls=%async_computation.18 | async-start | bytes 21626880 | tf_op jit(solution)/shard_map/reduce_scatter | solution.py:264
  1211.9 1619.0 %reduce-scatter.15.cloned.1.call-start = ((), (), s32[]{:S(2)}) async-start(), calls=%async_computation.16 | async-start | bytes 21626880 | tf_op jit(solution)/shard_map/reduce_scatter | solution.py:258
  1224.3 1836.2 %reduce-scatter.13.cloned.1.call-start = ((), (), s32[]{:S(2)}) async-start(), calls=%async_computation.15 | async-start | bytes 21626880 | tf_op jit(solution)/shard_map/reduce_scatter | solution.py:257
  1224.4 3.8 collective-permute-start.1
  1239.5 2255.9 %reduce-scatter.23.cloned.1.call-start = ((), (), s32[]{:S(2)}) async-start(), calls=%async_computation.20 | async-start | bytes 51904512 | tf_op jit(solution)/shard_map/reduce_scatter | solution.py:203
  1282.6 52.4 %copy-start.81 = (f32[256]{0:T(256)S(1)}, f32[256]{0:T(256)}, u32[]{:S(2)}) copy-start(f32[256]{0:T(256)} %copy-done.80) | copy-start | bytes 3076
  1282.7 52.4 %copy-start.12 = (f32[256,2048]{1,0:T(8,128)S(1)}, f32[256,2048]{1,0:T(8,128)}, u32[]{:S(2)}) copy-start(f32[256,2048]{1,0:T(8,128)} %copy-done.11) | copy-start | bytes 6291460
  (77 other events, 437.8 us)
Sparse Core Ops, SparseCore 0:
  11.0 90.0 all-gather.9
  103.9 56.5 all-gather.11
  163.4 85.7 all-gather.13
  251.9 85.3 all-gather.15
  340.1 153.7 all-gather.19
  496.7 152.8 all-gather.17
  652.6 152.8 all-gather.21
  1127.3 133.3 reduce-scatter.26
  1263.1 131.7 reduce-scatter.24
  1401.1 823.1 reduce-scatter.20
  2227.2 143.9 reduce-scatter.16
  2373.9 227.2 reduce-scatter.18
  2604.0 226.8 reduce-scatter.14
  2833.6 226.8 reduce-scatter.12
  3067.3 428.0 reduce-scatter.22
where the time goes:
time: 3520 us; the launch traced here: 3500 us
  waiting for transfers between devices  2490 us (71%)
  local copies, waits for them, and re-layouts  343 us (10%)
  matrix products  248 us (7%)
  blocking collectives  218 us (6%)
  other arithmetic  180 us (5%)
    reduce_scatter x1, waiting for transfers between devices, body(): lax.psum_scatter(jnp.concatenate([contract_rows(column_block, pre_grad),...  828 us
    reduce_scatter x1, waiting for transfers between devices, body(): lax.psum_scatter(contract_rows(column_block, cot_flat), ('dp', 'seq'), sc...  435 us
    reduce_scatter x1, waiting for transfers between devices, body(): lax.psum_scatter(outproj_grad, ('dp', 'seq'), scatter_dimension=1, tiled=...  230 us
    reduce_scatter x1, waiting for transfers between devices, body(): lax.psum_scatter(brproj_grad, ('dp', 'seq'), scatter_dimension=0, tiled=T...  230 us
    reduce_scatter x1, waiting for transfers between devices, body(): lax.psum_scatter(inproj_grad, ('dp', 'seq'), scatter_dimension=0, tiled=T...  230 us
    reduce_scatter x1, waiting for transfers between devices, body(): lax.psum_scatter(gatew_grad, ('dp', 'seq'), scatter_dimension=1, tiled=True)  143 us
    all_gather x1, waiting for transfers between devices, body(): lax.all_gather(ffn_down, ('dp', 'seq'), axis=0, tiled=True)  142 us
    all_gather x1, waiting for transfers between devices, body(): lax.all_gather(ffn_gate, ('dp', 'seq'), axis=0, tiled=True)  142 us
  transfers between devices with their start and end apart: 17, of which 13 were waited for; matrix products, arithmetic and copies ran while one was open for 13% of the time, Pallas kernels for 0%

commit v1 on v0

v1 whole, which is shorter than its diff:
```python
import functools

import jax
import jax.numpy as jnp
from jax import lax
from jax.experimental import pallas as pl
from jax.experimental.pallas import tpu as pltpu
from jax.sharding import Mesh
from jax.sharding import PartitionSpec as P

EPSILON = 1e-06
POWER = 8.0
BF = jnp.bfloat16
F32 = jnp.float32
GROUP = ("dp", "core")
EVERY = ("dp", "z", "core")
GELU_A = 0.7978845608028654
GELU_B = 0.044715
HALO = 16
VMEM_BYTES = 48 * 1024 * 1024


def gelu_pair(x):
    x2 = x * x
    th = jnp.tanh(GELU_A * (x + GELU_B * x2 * x))
    half = 0.5 * (1.0 + th)
    slope = half + 0.5 * x * (1.0 - th * th) * (GELU_A * (1.0 + 3.0 * GELU_B * x2))
    return x * half, slope


def gelu_only(x):
    return 0.5 * x * (1.0 + jnp.tanh(GELU_A * (x + GELU_B * x * x * x)))


def dot(a, b):
    return lax.dot_general(a, b, (((1,), (0,)), ((), ())), preferred_element_type=F32)


def dot_rows(a, b):
    return lax.dot_general(a, b, (((0,), (0,)), ((), ())), preferred_element_type=F32)


def dot_cols(a, b):
    return lax.dot_general(a, b, (((1,), (1,)), ((), ())), preferred_element_type=F32)


def minus_expm1(x):
    series = -x * (1.0 + x * (1 / 2) * (1.0 + x * (1 / 3) * (1.0 + x * (1 / 4) * (1.0 + x * (1 / 5) * (1.0 + x * (1 / 6))))))
    return jnp.where(x > -0.125, series, 1.0 - jnp.exp(x))


def conv_and_gates(inner_ref, prev, vec, gwf_ref, gws_ref, ext, block, own):
    rows = inner_ref.shape[0]
    ext[0:HALO, :] = prev.astype(F32)
    ext[HALO : HALO + rows, :] = inner_ref[...].astype(F32)
    conved = vec[4:5, :] + vec[0:1, :] * ext[HALO : HALO + rows, :]
    for tap in range(1, 4):
        conved = conved + vec[tap : tap + 1, :] * ext[HALO - tap : HALO - tap + rows, :]
    rounded = conved.astype(BF)
    gf = dot(rounded[:, :block], gwf_ref[...])
    gs = dot(rounded[:, block:], gws_ref[...])
    part = own - block
    rate_pre = jnp.concatenate([gf[:, :block], gs[:, :part]], axis=1) + vec[5:6, :own]
    open_pre = jnp.concatenate([gf[:, block:], gs[:, part:]], axis=1) + vec[6:7, :own]
    return conved, rounded, rate_pre, open_pre


def scan_groups(a_ref, b_ref, out_h, out_c, h, c, rows, width):
    place = lax.broadcasted_iota(jnp.int32, (8, width), 0)

    def one(g, carry):
        h, c = carry
        at = pl.ds(pl.multiple_of(g * 8, 8), 8)
        a, b = a_ref[at, :], b_ref[at, :]
        for shift in (1, 2, 4):
            keep = place >= shift
            pa = jnp.where(keep, pltpu.roll(a, shift, 0), 1.0)
            pb = jnp.where(keep, pltpu.roll(b, shift, 0), 0.0)
            b = a * pb + b
            a = a * pa
        b = b + a * h
        a = a * c
        out_h[at, :] = b
        out_c[at, :] = a
        return b[7:8, :], a[7:8, :]

    return lax.fori_loop(0, rows // 8, one, (h, c), unroll=4)


def forward_kernel(
    inner_ref, prev_ref, halo_ref, keep_ref, vec_ref, gwf_ref, gws_ref,
    decay_ref, local_ref, cum_ref, last_ref, ext, b_ref, carry, *, block, own,
):
    c = pl.program_id(2)
    rows = inner_ref.shape[0]
    prev = jnp.where(c == 0, halo_ref[...].astype(F32), prev_ref[...].astype(F32))
    vec = vec_ref[...]
    conved, _, rate_pre, open_pre = conv_and_gates(inner_ref, prev, vec, gwf_ref, gws_ref, ext, block, own)
    keep = keep_ref[...]
    rate = jax.nn.sigmoid(rate_pre)
    opening = jax.nn.sigmoid(open_pre)
    log_decay = vec[7:8, :own] * rate
    scale = keep * jnp.sqrt(minus_expm1(2.0 * log_decay)) + (1.0 - keep)
    decay_ref[...] = jnp.exp(log_decay) * keep
    b_ref[...] = scale * opening * conved[:, :own]

    @pl.when(c == 0)
    def _():
        carry[0:1, :] = jnp.zeros((1, own), F32)
        carry[1:2, :] = jnp.ones((1, own), F32)

    h, p = scan_groups(decay_ref, b_ref, local_ref, cum_ref, carry[0:1, :], carry[1:2, :], rows, own)
    carry[0:1, :] = h
    carry[1:2, :] = p
    last_ref[...] = carry[...]


def reverse_kernel(decay_ref, grad_ref, branch_ref, adj_ref, prod_ref, first_ref, carry, *, own):
    c = pl.program_id(2)
    rows = decay_ref.shape[0]
    place = lax.broadcasted_iota(jnp.int32, (8, own), 0)

    @pl.when(c == 0)
    def _():
        carry[0:1, :] = jnp.zeros((1, own), F32)
        carry[1:2, :] = jnp.ones((1, own), F32)

    def one(i, state):
        s, p = state
        at = pl.ds(pl.multiple_of((rows // 8 - 1 - i) * 8, 8), 8)
        a = decay_ref[at, :]
        hg = grad_ref[at, :] * gelu_only(branch_ref[at, :])
        b = a * hg
        for shift in (1, 2, 4):
            keep = place < 8 - shift
            na = jnp.where(keep, pltpu.roll(a, 8 - shift, 0), 1.0)
            nb = jnp.where(keep, pltpu.roll(b, 8 - shift, 0), 0.0)
            b = a * nb + b
            a = a * na
        b = b + a * s
        a = a * p
        last = place == 7
        adj_ref[at, :] = hg + jnp.where(last, s, pltpu.roll(b, 7, 0))
        prod_ref[at, :] = jnp.where(last, p, pltpu.roll(a, 7, 0))
        return b[0:1, :], a[0:1, :]

    s, p = lax.fori_loop(0, rows // 8, one, (carry[0:1, :], carry[1:2, :]), unroll=4)
    carry[0:1, :] = s
    carry[1:2, :] = p
    first_ref[...] = carry[...]


def backward_kernel(
    inner_ref, prev_ref, halo_ref, keep_ref, vec_ref, gwf_ref, gws_ref, hidden_ref, before_ref, start_ref,
    adj_ref, prod_ref, suffix_ref,
    igrad_ref, tail_ref, head_ref, dgf_ref, dgs_ref, sums_ref, ext, hext, cext, *, block, own,
):
    c = pl.program_id(2)
    peers = pl.num_programs(2)
    first = (pl.program_id(0) == 0) & (pl.program_id(1) == 0) & (c == 0)
    at_start = c == peers - 1
    rows = inner_ref.shape[0]
    part = own - block
    window = vec_ref.shape[1]

    @pl.when(first)
    def _():
        dgf_ref[...] = jnp.zeros_like(dgf_ref)
        dgs_ref[...] = jnp.zeros_like(dgs_ref)
        sums_ref[...] = jnp.zeros_like(sums_ref)

    @pl.when(c == 0)
    def _():
        cext[rows : rows + 8, :] = jnp.zeros((8, window), F32)

    @pl.when(c > 0)
    def _():
        cext[rows : rows + 8, :] = cext[0:8, :]

    prev = jnp.where(at_start, halo_ref[...].astype(F32), prev_ref[...].astype(F32))
    vec = vec_ref[...]
    conved, rounded, rate_pre, open_pre = conv_and_gates(inner_ref, prev, vec, gwf_ref, gws_ref, ext, block, own)
    keep = keep_ref[...]
    conv = conved[:, :own]
    rate = jax.nn.sigmoid(rate_pre)
    opening = jax.nn.sigmoid(open_pre)
    factor = vec[7:8, :own]
    log_decay = factor * rate
    e = jnp.exp(log_decay)
    root = jnp.sqrt(minus_expm1(2.0 * log_decay))
    scale = keep * root + (1.0 - keep)

    adj = adj_ref[...] + prod_ref[...] * suffix_ref[0:1, :]
    hext[0:8, :] = jnp.where(at_start, jnp.broadcast_to(start_ref[0:1, :], (8, own)), before_ref[...])
    hext[8 : 8 + rows, :] = hidden_ref[...]
    before = hext[7 : 7 + rows, :]
    d_log = keep * (adj * before * e - adj * opening * conv * (e * e) / root)
    direct = adj * scale * opening
    g_rate = (d_log * factor * rate * (1.0 - rate)).astype(BF)
    g_open = (adj * scale * conv * opening * (1.0 - opening)).astype(BF)
    gf = jnp.concatenate([g_rate[:, :block], g_open[:, :block]], axis=1)
    gs = jnp.concatenate([g_rate[:, block:], g_open[:, block:]], axis=1)
    cgrad = jnp.concatenate([dot_cols(gf, gwf_ref[...]), dot_cols(gs, gws_ref[...])], axis=1)
    cgrad = cgrad + jnp.concatenate([direct, jnp.zeros((rows, window - own), F32)], axis=1)
    cext[0:rows, :] = cgrad
    dgf_ref[...] += dot_rows(rounded[:, :block], gf)
    dgs_ref[...] += dot_rows(rounded[:, block:], gs)

    igrad = vec[0:1, :] * cgrad
    for tap in range(1, 4):
        igrad = igrad + vec[tap : tap + 1, :] * cext[tap : tap + rows, :]
    igrad_ref[...] = igrad.astype(BF)

    @pl.when(c == 0)
    def _():
        tail_ref[...] = igrad[rows - HALO :, :]

    head_ref[...] = cgrad[0:8, :]

    def total(x):
        return jnp.sum(x, axis=0, keepdims=True)

    for tap in range(4):
        sums_ref[tap : tap + 1, :] += total(ext[HALO - tap : HALO - tap + rows, :] * cgrad)
    sums_ref[4:5, :] += total(cgrad)
    sums_ref[5:6, :own] += total(g_rate.astype(F32))
    sums_ref[6:7, :own] += total(g_open.astype(F32))
    sums_ref[7:8, :own] += total(d_log * rate)


class Blocks:
    def __init__(self, peers, seqs, back):
        self.peers, self.seqs, self.back = peers, seqs, back

    def core(self, c):
        return self.peers - 1 - c if self.back else c

    def rows(self, count, width):
        return pl.BlockSpec((count, width), lambda d, s, c: ((d * self.peers + self.core(c)) * self.seqs + s, 0))

    def before(self, count, width, length):
        each = length // count

        def index(d, s, c):
            c = jnp.maximum(self.core(c) - 1, 0)
            return (((d * self.peers + c) * self.seqs + s) * each + each - 1, 0)

        return pl.BlockSpec((count, width), index)

    def sequence(self, count, width):
        return pl.BlockSpec((count, width), lambda d, s, c: (d * self.seqs + s, 0))

    def whole(self, *shape):
        return pl.BlockSpec(shape, lambda d, s, c: (0,) * len(shape))


def body(
    tokens, doc_reset, cotangent, norm_gain, input_proj, branch_proj, conv_kernel, conv_bias, gate_weight, gate_bias,
    decay_param, output_proj, ffn_gain, ffn_gate, ffn_up, ffn_down,
):
    seqs, span, width = tokens.shape
    rows = seqs * span
    n_dp, n_z, n_core = (lax.axis_size(a) for a in EVERY)
    group = n_dp * n_core
    devices = group * n_z
    zi = lax.axis_index("z")
    me = lax.axis_index("dp") * n_core + lax.axis_index("core")
    rec = input_proj.shape[1]
    ff = ffn_gate.shape[1]
    block = gate_weight.shape[2]
    taps = conv_kernel.shape[0]
    drow = input_proj.shape[0]
    frow = ffn_down.shape[0]
    ff_own = ff // group
    blocks = rec // block
    shared = blocks - group
    sharers = group // shared
    part = block // sharers
    lanes = 128 * (-(-part // 128))
    own = block + lanes
    window = 2 * block
    total_rows = group * rows
    lines = n_dp * seqs

    def d_to_z(x):
        lead = x.shape[:-1]
        y = x.reshape(*lead, n_dp, n_z, n_core * drow)
        return jnp.swapaxes(y, -3, -2).reshape(*lead, width)

    def d_from_z(x):
        lead = x.shape[:-1]
        y = x.reshape(*lead, n_z, n_dp, n_core * drow)
        return jnp.swapaxes(y, -3, -2).reshape(*lead, width)

    def own_columns(w):
        lead = w.shape[0]
        full = w[:, : group * block].reshape(lead, group, block)
        rest = w[:, group * block :].reshape(lead, group, part)
        return jnp.concatenate([full, rest, jnp.zeros((lead, group, lanes - part), w.dtype)], axis=2)

    def window_columns(w):
        lead = w.shape[0]
        full = w[:, : group * block].reshape(lead, group, block)
        rest = w[:, group * block :].reshape(lead, shared, block)
        turned = jnp.stack([jnp.roll(rest, -part * q, axis=2) for q in range(sharers)], axis=2)
        return jnp.concatenate([full, turned.reshape(lead, group, block)], axis=2)

    def exchange(x):
        return lax.all_to_all(x, GROUP, split_axis=0, concat_axis=0, tiled=True)

    def to_members(x):
        y = jnp.swapaxes(x, 0, 1)
        return exchange(y.reshape(group * x.shape[0], x.shape[2]))

    def over_z(x):
        return lax.all_gather(x, "z", axis=0, tiled=True)

    w_in = over_z(to_members(jnp.concatenate([window_columns(input_proj), own_columns(branch_proj)], axis=2)))
    w_out = over_z(to_members(own_columns(output_proj.T)))

    def ff_columns(w):
        y = w.reshape(drow, n_dp, n_z, n_core, frow)
        return jnp.transpose(y, (0, 1, 3, 2, 4)).reshape(drow, group, ff_own)

    w_ff = over_z(to_members(jnp.concatenate([ff_columns(ffn_gate), ff_columns(ffn_up)], axis=2)))
    w_down = over_z(ffn_down)

    rrow = rec // devices
    small = jnp.concatenate(
        [
            gate_weight.reshape(-1), norm_gain, ffn_gain, conv_kernel.reshape(-1), conv_bias, gate_bias.reshape(-1),
            decay_param,
        ]
    )
    small_len = small.shape[0]
    small = jnp.pad(small, (0, -small_len % (16 * 256))).reshape(-1, 256)
    small = lax.all_gather(small, EVERY, axis=0, tiled=False).reshape(devices, -1)
    gates_len = 2 * rrow * block
    gates_all = small[:, :gates_len].reshape(devices, 2, rrow, block)
    gates_all = jnp.swapaxes(gates_all, 0, 1).reshape(2, rec, block)
    rest = small[:, gates_len:small_len].astype(F32)
    gain = rest[:, :drow].reshape(width)
    fgain = rest[:, drow : 2 * drow].reshape(width)
    chan = rest[:, 2 * drow :].reshape(devices, taps + 4, rrow)
    chan = jnp.swapaxes(chan, 0, 1).reshape(taps + 4, rec)
    lam = chan[taps + 3 :]
    chan = jnp.concatenate([chan[: taps + 3], -POWER * jax.nn.softplus(-lam)], axis=0)

    quarter = me % sharers
    shared_at = (group + me // sharers) * block

    def my_window(x, axis):
        full = lax.dynamic_slice_in_dim(x, me * block, block, axis)
        other = lax.dynamic_slice_in_dim(x, shared_at, block, axis)
        turned = lax.dynamic_slice_in_dim(jnp.concatenate([other, other], axis), quarter * part, block, axis)
        return full, turned

    vec = jnp.concatenate(my_window(chan, 1), axis=1)
    gw_full, gw_shared = my_window(gates_all, 1)
    gw_shared = lax.dynamic_slice_in_dim(gw_shared, quarter * part, part, 2)
    gw_shared = jnp.pad(gw_shared, ((0, 0), (0, 0), (0, lanes - part)))
    gwf = jnp.concatenate([gw_full[0], gw_full[1]], axis=1)
    gws = jnp.concatenate([gw_shared[0], gw_shared[1]], axis=1)

    tok = d_to_z(tokens.reshape(rows, width)).astype(F32)
    cot = cotangent.reshape(rows, width)
    gain_z = d_to_z(gain)
    fgain_z = d_to_z(fgain)
    inv = lax.rsqrt(jnp.mean(tok * tok, axis=1, keepdims=True) + EPSILON)
    normed_own = (tok * inv * gain_z).astype(BF)

    def over_group(x):
        return lax.all_gather(x, GROUP, axis=0, tiled=True)

    def sum_group(x):
        return lax.psum_scatter(x.astype(BF), GROUP, scatter_dimension=0, tiled=True).astype(F32)

    normed = over_group(normed_own)
    keep = over_group((1 - doc_reset).astype(BF).reshape(rows)).astype(F32).reshape(total_rows, 1)
    cot_all = over_group(cot)

    both = dot(normed, w_in)
    inner = both[:, :window].astype(BF)
    branch = both[:, window:]
    ends = inner.reshape(n_dp, n_core, seqs, span, window)[:, n_core - 1, :, span - HALO :].reshape(lines * HALO, window)
    halo = lax.ppermute(ends, "z", [(i, i + 1) for i in range(n_z - 1)])

    grid = (n_dp, seqs, n_core)
    at = Blocks(n_core, seqs, False)
    params = pltpu.CompilerParams(vmem_limit_bytes=VMEM_BYTES)
    seq_in = [
        lambda b: b.rows(span, window), lambda b: b.before(HALO, window, span), lambda b: b.sequence(HALO, window),
        lambda b: b.rows(span, 1), lambda b: b.whole(8, window), lambda b: b.whole(block, window),
        lambda b: b.whole(block, 2 * lanes),
    ]
    row_f32 = jax.ShapeDtypeStruct((total_rows, own), F32)
    decay, local, cum, last = pl.pallas_call(
        functools.partial(forward_kernel, block=block, own=own),
        grid=grid,
        in_specs=[f(at) for f in seq_in],
        out_specs=[at.rows(span, own)] * 3 + [at.sequence(8, own)],
        out_shape=[row_f32] * 3 + [jax.ShapeDtypeStruct((lines * 8, own), F32)],
        scratch_shapes=[
            pltpu.VMEM((span + HALO, window), F32), pltpu.VMEM((span, own), F32), pltpu.VMEM((8, own), F32),
        ],
        compiler_params=params,
    )(inner, inner, halo, keep, vec, gwf, gws)

    def carried(x, order, reached):
        every = lax.all_gather(x.reshape(lines, 8, own)[:, :2], "z", axis=0, tiled=False)
        state = jnp.zeros((lines, own), F32)
        for k in order:
            state = jnp.where(reached(k), every[k, :, 1] * state + every[k, :, 0], state)
        return state

    start = carried(last, range(n_z), lambda k: k < zi)

    def by_line(x):
        return x.reshape(n_dp, 1, seqs, 1, own)

    def spread(x):
        return x.reshape(n_dp, n_core, seqs, span, own)

    hidden = (spread(local) + spread(cum) * by_line(start)).reshape(total_rows, own)
    mixed_out = (hidden * gelu_only(branch)).astype(BF)
    mid = tok + sum_group(dot_cols(mixed_out, w_out))

    finv = lax.rsqrt(jnp.mean(mid * mid, axis=1, keepdims=True) + EPSILON)
    fnormed = over_group((mid * finv * fgain_z).astype(BF))
    pre_lin = dot(fnormed, w_ff)
    act, slope = gelu_pair(pre_lin[:, :ff_own])
    lin = pre_lin[:, ff_own:]
    fhidden = (act * lin).astype(BF)
    hid_grad = dot_cols(cot_all, w_down)
    fgrad = jnp.concatenate([(hid_grad * lin * slope).astype(BF), (hid_grad * act).astype(BF)], axis=1)
    fnormed_grad = sum_group(dot_cols(fgrad, w_ff))
    layer_out = d_from_z(mid) + sum_group(dot(fhidden, w_down))

    fg = fgain_z * fnormed_grad
    ffn_gain_part = jnp.sum(fnormed_grad * mid * finv, axis=0)
    mid_grad = (
        d_to_z(cot).astype(F32) + finv * fg - mid * (finv * finv * finv) * jnp.mean(mid * fg, axis=1, keepdims=True)
    )
    mid_low = over_group(mid_grad.astype(BF))

    def sum_z(x):
        return lax.psum_scatter(x.astype(BF), "z", scatter_dimension=0, tiled=True)

    down_out = sum_z(dot_rows(fhidden, cot_all)).astype(F32)
    ff_part = exchange(sum_z(dot_rows(fnormed, fgrad))).reshape(group, drow, 2, ff_own)

    def ff_natural(x):
        y = x.reshape(n_dp, n_core, drow, n_z, frow)
        return jnp.transpose(y, (2, 0, 3, 1, 4)).reshape(drow, ff).astype(F32)

    mixed_grad = dot(mid_low, w_out)
    act_r, slope_r = gelu_pair(branch)
    branch_grad = (mixed_grad * hidden * slope_r).astype(BF)
    back = Blocks(n_core, seqs, True)
    adj, prod, front = pl.pallas_call(
        functools.partial(reverse_kernel, own=own),
        grid=grid,
        in_specs=[back.rows(span, own)] * 3,
        out_specs=[back.rows(span, own)] * 2 + [back.sequence(8, own)],
        out_shape=[row_f32] * 2 + [jax.ShapeDtypeStruct((lines * 8, own), F32)],
        scratch_shapes=[pltpu.VMEM((8, own), F32)],
        compiler_params=params,
    )(decay, mixed_grad, branch)
    suffix = carried(front, reversed(range(n_z)), lambda k: k > zi)

    def eight(x):
        return jnp.broadcast_to(x[:, None, :], (lines, 8, own)).reshape(lines * 8, own)

    igrad, tail, head, dgf, dgs, sums = pl.pallas_call(
        functools.partial(backward_kernel, block=block, own=own),
        grid=grid,
        in_specs=[f(back) for f in seq_in]
        + [
            back.rows(span, own), back.before(8, own, span), back.sequence(8, own), back.rows(span, own),
            back.rows(span, own), back.sequence(8, own),
        ],
        out_specs=[
            back.rows(span, window), back.sequence(HALO, window), back.sequence(8, window), back.whole(block, window),
            back.whole(block, 2 * lanes), back.whole(8, window),
        ],
        out_shape=[
            jax.ShapeDtypeStruct((total_rows, window), BF), jax.ShapeDtypeStruct((lines * HALO, window), F32),
            jax.ShapeDtypeStruct((lines * 8, window), F32), jax.ShapeDtypeStruct((block, window), F32),
            jax.ShapeDtypeStruct((block, 2 * lanes), F32), jax.ShapeDtypeStruct((8, window), F32),
        ],
        scratch_shapes=[
            pltpu.VMEM((span + HALO, window), F32), pltpu.VMEM((span + 8, own), F32), pltpu.VMEM((span + 8, window), F32),
        ],
        compiler_params=params,
    )(inner, inner, halo, keep, vec, gwf, gws, hidden, hidden, eight(start), adj, prod, eight(suffix))

    after = lax.ppermute(head.astype(BF), "z", [(i + 1, i) for i in range(n_z - 1)]).astype(F32).reshape(lines, 8, window)
    fix = jnp.zeros((lines, HALO, window), F32)
    for tap in range(1, taps):
        fix = fix.at[:, HALO - tap :, :].add(vec[tap] * after[:, :tap])
    tail = (tail.reshape(lines, HALO, window) + fix).astype(BF).reshape(n_dp, 1, seqs, HALO, window)
    igrad = lax.dynamic_update_slice(
        igrad.reshape(n_dp, n_core, seqs, span, window), tail, (0, n_core - 1, 0, span - HALO, 0)
    ).reshape(total_rows, window)
    rgrad = jnp.concatenate([igrad, branch_grad], axis=1)
    normed_grad = sum_group(dot_cols(rgrad, w_in))

    g = gain_z * normed_grad
    gain_part = jnp.sum(normed_grad * tok * inv, axis=0)
    input_grad = mid_grad + inv * g - tok * (inv * inv * inv) * jnp.mean(tok * g, axis=1, keepdims=True)
    input_grad = d_from_z(input_grad)

    out_part = exchange(sum_z(dot_rows(mid_low, mixed_out))).reshape(group, drow, own)
    in_part = exchange(sum_z(dot_rows(normed, rgrad))).reshape(group, drow, window + own)

    def own_natural(x):
        full = jnp.swapaxes(x[:, :, :block], 0, 1).reshape(drow, group * block)
        rest = jnp.swapaxes(x[:, :, block : block + part], 0, 1).reshape(drow, group * part)
        return jnp.concatenate([full, rest], axis=1).astype(F32)

    full = jnp.swapaxes(in_part[:, :, :block], 0, 1).reshape(drow, group * block).astype(F32)
    turned = in_part[:, :, block:window].astype(F32).reshape(shared, sharers, drow, block)
    other = sum(jnp.roll(turned[:, q], part * q, axis=2) for q in range(sharers))
    input_proj_grad = jnp.concatenate([full, jnp.swapaxes(other, 0, 1).reshape(drow, shared * block)], axis=1)
    branch_proj_grad = own_natural(in_part[:, :, window:])
    output_proj_grad = own_natural(out_part).T

    def place_window(x, axis_len):
        lead = x.shape[:-1]
        other = x[..., block:]
        turned = lax.dynamic_slice_in_dim(
            jnp.concatenate([other, other], -1), lax.rem(block - quarter * part, block), block, x.ndim - 1
        )
        y = jnp.zeros((*lead, axis_len), x.dtype)
        y = lax.dynamic_update_slice_in_dim(y, x[..., :block], me * block, x.ndim - 1)
        return lax.dynamic_update_slice_in_dim(y, turned, shared_at, x.ndim - 1)

    lane = jnp.arange(window)
    mine = lane < block + part
    sums = jnp.where(jnp.concatenate([jnp.ones((5, window), bool), jnp.broadcast_to(mine, (3, window))], axis=0), sums, 0.0)
    sums = place_window(sums, rec)
    sums = jnp.concatenate([sums[:7], sums[7:8] * (POWER * jax.nn.sigmoid(-lam))], axis=0)
    vectors = jnp.concatenate(
        [
            d_from_z(gain_part).reshape(devices, drow), d_from_z(ffn_gain_part).reshape(devices, drow),
            jnp.swapaxes(sums.reshape(8, devices, rrow), 0, 1).reshape(devices, 8 * rrow),
        ],
        axis=1,
    )
    vec_len = vectors.shape[1]
    vectors = lax.all_to_all(vectors, EVERY, split_axis=0, concat_axis=0, tiled=True)
    vectors = jnp.sum(vectors.reshape(devices, vec_len), axis=0)
    gain_out = vectors[:drow]
    fgain_out = vectors[drow : 2 * drow]
    chan_out = vectors[2 * drow :].reshape(8, rrow)

    dg_full = jnp.stack([dgf[:, :block], dgf[:, block:]])
    dg_shared = jnp.stack([dgs[:, :part], dgs[:, lanes : lanes + part]])
    dg_shared = lax.dynamic_slice_in_dim(
        jnp.concatenate([dg_shared, dg_shared], 1), lax.rem(block - quarter * part, block), block, 1
    )
    gates = jnp.zeros((2, rec, block), BF)
    gates = lax.dynamic_update_slice(gates, dg_full.astype(BF), (0, me * block, 0))
    gates = lax.dynamic_update_slice(gates, dg_shared.astype(BF), (0, shared_at, quarter * part))
    gates = jnp.swapaxes(gates.reshape(2, devices, rrow, block), 0, 1).reshape(devices * 2 * rrow, block)
    gates = lax.all_to_all(gates, EVERY, split_axis=0, concat_axis=0, tiled=True)
    gates_out = jnp.sum(gates.reshape(devices, 2, rrow, block).astype(F32), axis=0)

    return (
        layer_out.reshape(seqs, span, width),
        input_grad.reshape(seqs, span, width),
        gain_out,
        input_proj_grad,
        branch_proj_grad,
        chan_out[:taps],
        chan_out[taps],
        gates_out,
        chan_out[taps + 1 : taps + 3],
        chan_out[taps + 3],
        output_proj_grad,
        fgain_out,
        ff_natural(ff_part[:, :, 0]),
        ff_natural(ff_part[:, :, 1]),
        down_out,
    )


def solution(mesh):
    n_dp, n_seq = mesh.shape["dp"], mesh.shape["seq"]
    split = Mesh(mesh.devices.reshape(n_dp, n_seq // 2, 2), EVERY)
    seq = ("z", "core")
    line = P("dp", seq, None)
    first = P(EVERY)
    rows = P(EVERY, None)
    cols = P(None, EVERY)
    mids = P(None, EVERY, None)
    return jax.shard_map(
        body,
        mesh=split,
        in_specs=(
            line, P("dp", seq), line, first, rows, rows, cols, first, mids, cols, first, cols, first, rows, rows, rows,
        ),
        out_specs=(
            line, line, first, rows, rows, cols, first, mids, cols, first, cols, first, rows, rows, rows,
        ),
        check_vma=False,
    )
```

time: 3520 us -> 1340 us (0.38)
  waiting for transfers between devices: 2490 us -> 781 us
  local copies, waits for them, and re-layouts: 343 us -> 132 us
  other arithmetic: 180 us -> 56.6 us
  blocking collectives: 218 us -> 106 us
  matrix products: 248 us -> 166 us
  Pallas kernels: 0 us -> 42.6 us
    reduce_scatter x6 -> x8, waiting for transfers between devices: 2100 us -> 313 us  [the longest x4 217 us: sum_group(): lax.psum_scatter(x.astype(BF), GROUP, scatter_dimension=0, tiled=True)]
    slice x108 -> x36, local copies, waits for them, and re-layouts: 123 us -> 12.2 us  [the longest x1 3.41 us: body(): gates_all = small[:, :gates_len].reshape(devices, 2, rrow, block)]
    pad x56 -> x1, local copies, waits for them, and re-layouts: 101 us -> 0.01 us  [body(): small = jnp.pad(small, (0, -small_len % (16 * 256))).reshape(-1, 256)]
    all_gather x7 -> x9, waiting for transfers between devices: 334 us -> 427 us  [the longest x4 201 us: over_group(): return lax.all_gather(x, GROUP, axis=0, tiled=True)]
    all_gather x6 -> x3, blocking collectives: 134 us -> 44.8 us  [the longest x2 33.5 us: carried(): lax.all_gather(x.reshape(lines, 8, own)[:, :2], 'z', axis=0, tiled=False)]
    unnamed x2 -> x0, blocking collectives: 84.1 us -> none
    dot_general x21 -> x12, matrix products: 248 us -> 166 us  [the longest x4 61.6 us: dot_cols(): lax.dot_general(a, b, (((1,), (1,)), ((), ())), preferred_element_type=F32)]
    concatenate x29 -> x9, other arithmetic: 79.8 us -> 1.67 us  [the longest x1 0.88 us: body(): jnp.concatenate([full, jnp.swapaxes(other, 0, 1).reshape(drow, shared * b...]
  transfers between devices with their start and end apart: 17 -> 25, of which waited for: 13 -> 18; matrix products, arithmetic and copies ran while one was open for 13% -> 21% of each run, Pallas kernels for 0% -> 3%
where the time goes in v1:
time: 1340 us; the launch traced here: 1330 us
  waiting for transfers between devices  781 us (58%)
  matrix products  166 us (12%)
  local copies, waits for them, and re-layouts  132 us (10%)
  blocking collectives  106 us (8%)
  other arithmetic  56.6 us (4%)
  Pallas kernels  42.6 us (3%)
  starting transfers between devices  29.8 us (2%)
  between operations  15.8 us (1%)
    reduce_scatter x4, waiting for transfers between devices, sum_group(): lax.psum_scatter(x.astype(BF), GROUP, scatter_dimension=0, tiled=True)  217 us
    all_gather x4, waiting for transfers between devices, over_group(): return lax.all_gather(x, GROUP, axis=0, tiled=True)  201 us
    all_gather x4, waiting for transfers between devices, over_z(): return lax.all_gather(x, 'z', axis=0, tiled=True)  193 us
    reduce_scatter x4, waiting for transfers between devices, sum_z(): return lax.psum_scatter(x.astype(BF), 'z', scatter_dimension=0, tiled=True)  95.8 us
    dot_general x4, matrix products, dot_cols(): lax.dot_general(a, b, (((1,), (1,)), ((), ())), preferred_element_type=F32)  61.6 us
    all_to_all x2, blocking collectives, exchange(): return lax.all_to_all(x, GROUP, split_axis=0, concat_axis=0, tiled=True)  61 us
    dot_general x4, matrix products, dot_rows(): lax.dot_general(a, b, (((0,), (0,)), ((), ())), preferred_element_type=F32)  54.6 us
    dot_general x4, matrix products, dot(): lax.dot_general(a, b, (((1,), (0,)), ((), ())), preferred_element_type=F32)  49.8 us
  transfers between devices with their start and end apart: 25, of which 18 were waited for; matrix products, arithmetic and copies ran while one was open for 21% of the time, Pallas kernels for 3%

profile of v1, /device:TPU:0, one launch (start us, length us, event | category | flops | bytes accessed | tf_op | source)
XLA Modules:
  0.0 1328.5 jit_solution(13083376761634667600)
XLA Ops:
  16.6 19.7 %all_to_all.72 = bf16[8,64,896]{2,1,0:T(8,128)(2,1)} all-to-all(bf16[8,64,896]{2,1,0:T(8,128)(2,1)S(1)} %copy.329), channel_id=1, replica_groups=mesh['dp'=4,'z'=4,'core'=2] {'dp','core'}, dimensions={0} | all-to-all | bytes 1835008 | tf_op jit(solution)/shard_map/all_to_all | solution.py:309
  43.3 32.2 %all-gather.14.cloned.1.call-done = bf16[32,176,256]{2,1,0:T(8,128)(2,1)} async-done(((bf16[1,176,256]{2,1,0:T(8,128)(2,1)}), bf16[32,176,256]{2,1,0:T(8,128)(2,1)}) %all-gather.14.cloned.1.call-update) | async-done | bytes 2883600 | tf_op jit(solution)/shard_map/all_gather | solution.py:337
  86.9 11.2 all-gather
  111.4 36.5 %all-gather.18.cloned.1.call-done = bf16[2048,896]{1,0:T(8,128)(2,1)} async-done(((bf16[512,896]{1,0:T(8,128)(2,1)}), bf16[2048,896]{1,0:T(8,128)(2,1)}) %all-gather.18.cloned.1.call-update) | async-done | bytes 3670032 | tf_op jit(solution)/shard_map/all_gather | solution.py:316
  147.9 55.5 %all-gather.16.cloned.1.call-done = bf16[2048,2048]{1,0:T(8,128)(2,1)} async-done(((bf16[256,2048]{1,0:T(8,128)(2,1)}), bf16[2048,2048]{1,0:T(8,128)(2,1)}) %all-gather.16.cloned.1.call-update) | async-done | bytes 8388624 | tf_op jit(solution)/shard_map/all_gather | solution.py:373
  203.4 12.3 fusion.99
  223.0 12.3 shard_map.271
  236.6 16.0 %all-gather.1 = f32[16,2,384]{2,1,0:T(2,128)S(1)} all-gather(f32[4,2,384]{2,1,0:T(2,128)S(1)} %slice.463), channel_id=3, replica_groups=mesh['dp'=4,'z'=4,'core'=2] {'z'}, dimensions={0}, use_global_device_ids=true | all-gather | bytes 61440 | tf_op jit(solution)/shard_map/all_gather | solution.py:410
  291.9 41.3 %all_to_all.73 = bf16[8,64,1536]{2,1,0:T(8,128)(2,1)} all-to-all(bf16[8,64,1536]{2,1,0:T(8,128)(2,1)S(1)} %copy.346), channel_id=1, replica_groups=mesh['dp'=4,'z'=4,'core'=2] {'dp','core'}, dimensions={0} | all-to-all | bytes 3145728 | tf_op jit(solution)/shard_map/all_to_all | solution.py:309
  334.6 22.9 %reduce-scatter.9.cloned.1.call-done = bf16[256,2048]{1,0:T(8,128)(2,1)} async-done(((bf16[2048,2048]{1,0:T(8,128)(2,1)}), bf16[256,2048]{1,0:T(8,128)(2,1)}) %reduce-scatter.9.cloned.1.call-update) | async-done | bytes 1048592 | tf_op jit(solution)/shard_map/reduce_scatter | solution.py:376
  363.6 110.8 %all-gather.24.cloned.1.call-done = bf16[2048,1536]{1,0:T(8,128)(2,1)} async-done(((bf16[512,1536]{1,0:T(8,128)(2,1)}), bf16[2048,1536]{1,0:T(8,128)(2,1)}) %all-gather.24.cloned.1.call-update) | async-done | bytes 6291472 | tf_op jit(solution)/shard_map/all_gather | solution.py:316
  474.4 55.3 %all-gather.22.cloned.1.call-done = bf16[2048,2048]{1,0:T(8,128)(2,1)} async-done(((bf16[256,2048]{1,0:T(8,128)(2,1)}), bf16[2048,2048]{1,0:T(8,128)(2,1)}) %all-gather.22.cloned.1.call-update) | async-done | bytes 8388624 | tf_op jit(solution)/shard_map/all_gather | solution.py:373
  529.7 19.1 %fusion.100 = f32[2048,1536]{0,1:T(8,128)} fusion(bf16[2048,2048]{1,0:T(8,128)(2,1)} %all-gather.22.cloned.1.call-done, bf16[2048,1536]{1,0:T(8,128)(2,1)} %all-gather.24.cloned.1.call-done), kind=kOutput, calls=%fused_computation.226 | convolution fusion | flops 12884901888 | bytes 27262976 | tf_op jit(solution)/shard_map/dot_general | solution.py:36
  548.8 46.1 %all-gather.26.cloned.1.call-done = bf16[768,2048]{1,0:T(8,128)(2,1)} async-done(((bf16[192,2048]{1,0:T(8,128)(2,1)}), bf16[768,2048]{1,0:T(8,128)(2,1)}) %all-gather.26.cloned.1.call-update) | async-done | bytes 3145744 | tf_op jit(solution)/shard_map/all_gather | solution.py:316
  594.9 55.1 %all-gather.30.cloned.1.call-done = bf16[1,2048,2048]{2,1,0:T(8,128)(2,1)} async-done(((bf16[1,256,2048]{2,1,0:T(8,128)(2,1)}), bf16[1,2048,2048]{2,1,0:T(8,128)(2,1)}) %all-gather.30.cloned.1.call-update) | async-done | bytes 8388624 | tf_op jit(solution)/shard_map/all_gather | solution.py:373
  650.0 19.4 %multiply_convert_fusion.1 = (bf16[2048,768]{0,1:T(8,128)(2,1)S(1)}, bf16[2048,768]{0,1:T(8,128)(2,1)}, bf16[2048,768]{0,1:T(8,128)(2,1)}) fusion(f32[2048,1536]{0,1:T(8,128)} %fusion.100, bf16[768,2048]{1,0:T(8,128)(2,1)} %all-gather.26.cloned.1.call-done, bf16[1,2048,2048]{2,1,0:T(8,128)(2,1)} %all-gather.30.cloned.1.call-done), kind=kOutput, calls=%fused_computation.14 | convolution fusion | flops 6480199680 | bytes 33554432 | tf_op jit(solution)/shard_map/dot_general | solution.py:44
  671.1 18.6 %convolution_convert_fusion.1 = bf16[2048,2048]{1,0:T(8,128)(2,1)} fusion(bf16[2048,1536]{1,0:T(8,128)(2,1)} %all-gather.24.cloned.1.call-done, bf16[2048,768]{0,1:T(8,128)(2,1)} %get-tuple-element.90, bf16[2048,768]{0,1:T(8,128)(2,1)S(1)} %get-tuple-element.89), kind=kOutput, calls=%fused_computation.6 | convolution fusion | flops 12901679104 | bytes 20971520 | tf_op jit(solution)/shard_map/dot_general | solution.py:44
  698.1 63.2 %reduce-scatter.13.cloned.1.call-done = bf16[256,2048]{1,0:T(8,128)(2,1)} async-done(((bf16[2048,2048]{1,0:T(8,128)(2,1)}), bf16[256,2048]{1,0:T(8,128)(2,1)}) %reduce-scatter.13.cloned.1.call-update) | async-done | bytes 1048592 | tf_op jit(solution)/shard_map/reduce_scatter | solution.py:376
  766.2 19.4 %convolution_convert_fusion.4 = bf16[2048,1536]{1,0:T(8,128)(2,1)} fusion(bf16[2048,2048]{1,0:T(8,128)(2,1)} %all-gather.22.cloned.1.call-done, bf16[2048,768]{0,1:T(8,128)(2,1)} %get-tuple-element.90, bf16[2048,768]{0,1:T(8,128)(2,1)} %copy-done.47), kind=kOutput, calls=%fused_computation.9 | convolution fusion | flops 12900630528 | bytes 20971520 | tf_op jit(solution)/shard_map/dot_general | solution.py:40
  785.7 35.0 %all-gather.28.cloned.1.call-done = bf16[2048,2048]{1,0:T(8,128)(2,1)} async-done(((bf16[256,2048]{1,0:T(8,128)(2,1)}), bf16[2048,2048]{1,0:T(8,128)(2,1)}) %all-gather.28.cloned.1.call-update) | async-done | bytes 8388624 | tf_op jit(solution)/shard_map/all_gather | solution.py:373
  829.9 12.3 fusion.7
  842.2 11.4 convolution_convert_fusion.2
  879.7 17.5 %all-gather.3 = f32[16,2,384]{2,1,0:T(2,128)S(1)} all-gather(f32[4,2,384]{2,1,0:T(2,128)S(1)} %slice.478), channel_id=5, replica_groups=mesh['dp'=4,'z'=4,'core'=2] {'z'}, dimensions={0}, use_global_device_ids=true | all-gather | bytes 61440 | tf_op jit(solution)/shard_map/all_gather | solution.py:410
  897.4 20.3 %shard_map.273 = (bf16[2048,512]{1,0:T(8,128)(2,1)S(1)}, f32[64,512]{1,0:T(8,128)S(1)}, f32[32,512]{1,0:T(8,128)S(1)}, f32[256,512]{1,0:T(8,128)S(1)}, f32[256,256]{1,0:T(8,128)S(1)}, /*index=5*/f32[8,512]{1,0:T(8,128)S(1)}) custom-call(bf16[2048,512]{1,0:T(8,128)(2,1)} %copy-done, bf16[2048,512]{1,0:T(8,128)(2,1)} %copy-done, ...), custom_call_target="tpu_custom_call" | custom-call | tf_op jit(solution)/shard_map/pallas_call | solution.py:474
  926.7 13.8 %convolution_convert_fusion.5 = bf16[2048,896]{1,0:T(8,128)(2,1)} fusion(bf16[2048,2048]{1,0:T(8,128)(2,1)} %all-gather.16.cloned.1.call-done, bf16[2048,384]{1,0:T(8,128)(2,1)} %get-tuple-element.93, bf16[2048,512]{1,0:T(8,128)(2,1)} %bitcast.305), kind=kOutput, calls=%fused_computation.23 | convolution fusion | flops 7525367808 | bytes 15728640 | tf_op jit(solution)/shard_map/dot_general | solution.py:40
  940.6 13.8 %convolution_convert_fusion = bf16[2048,2048]{1,0:T(8,128)(2,1)} fusion(bf16[2048,896]{1,0:T(8,128)(2,1)} %all-gather.18.cloned.1.call-done, bf16[2048,384]{1,0:T(8,128)(2,1)} %get-tuple-element.93, bf16[2048,512]{1,0:T(8,128)(2,1)} %bitcast.306), kind=kOutput, calls=%fused_computation.5 | convolution fusion | flops 7527727104 | bytes 15728640 | tf_op jit(solution)/shard_map/dot_general | solution.py:44
  959.1 20.7 %all-to-all-done.7 = bf16[8,64,1536]{2,1,0:T(8,128)(2,1)} async-done(((bf16[8,64,1536]{2,1,0:T(8,128)(2,1)}), bf16[8,64,1536]{2,1,0:T(8,128)(2,1)}, u32[]{:S(2)}, u32[]{:S(2)}) %all-to-all-start.7) | async-done | bytes 1572896 | tf_op jit(solution)/shard_map/all_to_all | solution.py:309
  1004.8 62.4 %reduce-scatter.23.cloned.1.call-done = bf16[192,2048]{1,0:T(8,128)(2,1)} async-done(((bf16[768,2048]{1,0:T(8,128)(2,1)}), bf16[192,2048]{1,0:T(8,128)(2,1)}) %reduce-scatter.23.cloned.1.call-update) | async-done | bytes 786448 | tf_op jit(solution)/shard_map/reduce_scatter | solution.py:447
  1070.3 83.6 %reduce-scatter.11.cloned.1.call-done = bf16[256,2048]{1,0:T(8,128)(2,1)} async-done(((bf16[2048,2048]{1,0:T(8,128)(2,1)}), bf16[256,2048]{1,0:T(8,128)(2,1)}) %reduce-scatter.11.cloned.1.call-update) | async-done | bytes 1048592 | tf_op jit(solution)/shard_map/reduce_scatter | solution.py:376
  1191.2 33.4 %reduce-scatter.17.cloned.1.call-done = bf16[512,896]{1,0:T(8,128)(2,1)} async-done(((bf16[2048,896]{1,0:T(8,128)(2,1)}), bf16[512,896]{1,0:T(8,128)(2,1)}) %reduce-scatter.17.cloned.1.call-update) | async-done | bytes 917520 | tf_op jit(solution)/shard_map/reduce_scatter | solution.py:447
  1232.2 10.1 all-to-all-done.4
  1252.6 47.4 %reduce-scatter.15.cloned.1.call-done = bf16[256,2048]{1,0:T(8,128)(2,1)} async-done(((bf16[2048,2048]{1,0:T(8,128)(2,1)}), bf16[256,2048]{1,0:T(8,128)(2,1)}) %reduce-scatter.15.cloned.1.call-update) | async-done | bytes 1048592 | tf_op jit(solution)/shard_map/reduce_scatter | solution.py:376
  (338 shorter events, 264.3 us)
Async XLA Ops:
  7.2 68.3 %all-gather.14.cloned.1.call-start = ((), (), s32[]{:S(2)}) async-start(), calls=%async_computation.16 | async-start | bytes 2973696 | tf_op jit(solution)/shard_map/all_gather | solution.py:337
  13.3 134.6 %all-gather.18.cloned.1.call-start = ((), (), s32[]{:S(2)}) async-start(), calls=%async_computation.18 | async-start | bytes 4587520 | tf_op jit(solution)/shard_map/all_gather | solution.py:316
  36.3 167.1 %all-gather.16.cloned.1.call-start = ((), (), s32[]{:S(2)}) async-start(), calls=%async_computation.17 | async-start | bytes 9437184 | tf_op jit(solution)/shard_map/all_gather | solution.py:373
  42.2 315.4 %copy-start.7 = (f32[256,2048]{1,0:T(8,128)}, f32[256,2048]{1,0:T(8,128)S(1)}, u32[]{:S(2)}) copy-start(f32[256,2048]{1,0:T(8,128)S(1)} %reshape.670) | copy-start | bytes 6291460
  83.3 15.2 %all-to-all-start.1 = ((bf16[8,64,384]{2,1,0:T(8,128)(2,1)}), bf16[8,64,384]{2,1,0:T(8,128)(2,1)S(1)}, u32[]{:S(2)}, u32[]{:S(2)}) async-start(bf16[8,64,384]{2,1,0:T(8,128)(2,1)} %copy.341), calls=%async_computation.1 | async-start | bytes 786432 | tf_op jit(solution)/shard_map/all_to_all | solution.py:309
  86.7 172.8 %all-gather.20.cloned.1.call-start = ((), (), s32[]{:S(2)}) async-start(), calls=%async_computation.19 | async-start | bytes 1966080 | tf_op jit(solution)/shard_map/all_gather | solution.py:316
  99.3 258.3 %reduce-scatter.9.cloned.1.call-start = ((), (), s32[]{:S(2)}) async-start(), calls=%async_computation.20 | async-start | bytes 9437184 | tf_op jit(solution)/shard_map/reduce_scatter | solution.py:376
  110.3 109.1 %copy-start.34 = (f32[8,256]{1,0:T(8,128)}, f32[8,256]{1,0:T(8,128)S(1)}, u32[]{:S(2)}) copy-start(f32[8,256]{1,0:T(8,128)S(1)} %get-tuple-element.115) | copy-start | bytes 24580
  110.4 109.0 %copy-start.32 = (f32[8,256]{1,0:T(8,128)}, f32[8,256]{1,0:T(8,128)S(1)}, u32[]{:S(2)}) copy-start(f32[8,256]{1,0:T(8,128)S(1)} %fusion.52) | copy-start | bytes 24580
  216.0 7.0 collective-permute-start
  269.3 205.1 %all-gather.24.cloned.1.call-start = ((), (), s32[]{:S(2)}) async-start(), calls=%async_computation.22 | async-start | bytes 7864320 | tf_op jit(solution)/shard_map/all_gather | solution.py:316
  333.2 196.5 %all-gather.22.cloned.1.call-start = ((), (), s32[]{:S(2)}) async-start(), calls=%async_computation.21 | async-start | bytes 9437184 | tf_op jit(solution)/shard_map/all_gather | solution.py:373
  361.7 233.2 %all-gather.26.cloned.1.call-start = ((), (), s32[]{:S(2)}) async-start(), calls=%async_computation.23 | async-start | bytes 3932160 | tf_op jit(solution)/shard_map/all_gather | solution.py:316
  362.5 287.6 %all-gather.30.cloned.1.call-start = ((), (), s32[]{:S(2)}) async-start(), calls=%async_computation.32 | async-start | bytes 9437184 | tf_op jit(solution)/shard_map/all_gather | solution.py:373
  363.2 398.0 %reduce-scatter.13.cloned.1.call-start = ((), (), s32[]{:S(2)}) async-start(), calls=%async_computation.25 | async-start | bytes 9437184 | tf_op jit(solution)/shard_map/reduce_scatter | solution.py:376
  689.8 130.9 %all-gather.28.cloned.1.call-start = ((), (), s32[]{:S(2)}) async-start(), calls=%async_computation.26 | async-start | bytes 9437184 | tf_op jit(solution)/shard_map/all_gather | solution.py:373
  694.5 66.8 %copy-start.10 = (f32[256,2048]{1,0:T(8,128)S(1)}, f32[256,2048]{1,0:T(8,128)}, u32[]{:S(2)}) copy-start(f32[256,2048]{1,0:T(8,128)} %copy-done.9) | copy-start | bytes 6291460
  766.2 188.2 %reduce-scatter.21.cloned.1.call-start = ((), (), s32[]{:S(2)}) async-start(), calls=%async_computation.30 | async-start | bytes 7864320 | tf_op jit(solution)/shard_map/reduce_scatter | solution.py:447
  785.7 194.1 %reduce-scatter.19.cloned.1.call-start = ((), (), s32[]{:S(2)}) async-start(), calls=%async_computation.29 | async-start | bytes 1966080 | tf_op jit(solution)/shard_map/reduce_scatter | solution.py:447
  829.8 237.3 %reduce-scatter.23.cloned.1.call-start = ((), (), s32[]{:S(2)}) async-start(), calls=%async_computation.31 | async-start | bytes 3932160 | tf_op jit(solution)/shard_map/reduce_scatter | solution.py:447
  842.2 311.7 %reduce-scatter.11.cloned.1.call-start = ((), (), s32[]{:S(2)}) async-start(), calls=%async_computation.24 | async-start | bytes 9437184 | tf_op jit(solution)/shard_map/reduce_scatter | solution.py:376
  853.7 370.9 %reduce-scatter.17.cloned.1.call-start = ((), (), s32[]{:S(2)}) async-start(), calls=%async_computation.28 | async-start | bytes 4587520 | tf_op jit(solution)/shard_map/reduce_scatter | solution.py:447
  919.0 6.6 collective-permute-start.1
  940.5 359.5 %reduce-scatter.15.cloned.1.call-start = ((), (), s32[]{:S(2)}) async-start(), calls=%async_computation.27 | async-start | bytes 9437184 | tf_op jit(solution)/shard_map/reduce_scatter | solution.py:376
  954.4 25.4 %all-to-all-start.7 = ((bf16[8,64,1536]{2,1,0:T(8,128)(2,1)}), bf16[8,64,1536]{2,1,0:T(8,128)(2,1)}, u32[]{:S(2)}, u32[]{:S(2)}) async-start(bf16[8,64,1536]{2,1,0:T(8,128)(2,1)} %bitcast.328), calls=%async_computation.14 | async-start | bytes 3145728 | tf_op jit(solution)/shard_map/all_to_all | solution.py:309
  979.8 13.0 all-to-all-start.6
  992.8 198.4 %all-to-all-start.5 = ((bf16[32,160,256]{2,1,0:T(8,128)(2,1)}), bf16[32,160,256]{2,1,0:T(8,128)(2,1)}, u32[]{:S(2)}, u32[]{:S(2)}) async-start(bf16[32,160,256]{2,1,0:T(8,128)(2,1)} %bitcast.309), calls=%async_computation.10 | async-start | bytes 5242880 | tf_op jit(solution)/shard_map/all_to_all | solution.py:566
  1002.7 66.9 %copy-start.41 = (f32[2048]{0:T(1024)S(1)}, f32[2048]{0:T(1024)}, u32[]{:S(2)}) copy-start(f32[2048]{0:T(1024)} %get-tuple-element.79) | copy-start | bytes 24580
  1224.6 17.7 %all-to-all-start.4 = ((bf16[8,64,896]{2,1,0:T(8,128)(2,1)}), bf16[8,64,896]{2,1,0:T(8,128)(2,1)S(1)}, u32[]{:S(2)}, u32[]{:S(2)}) async-start(bf16[8,64,896]{2,1,0:T(8,128)(2,1)} %bitcast.338), calls=%async_computation.9 | async-start | bytes 1835008 | tf_op jit(solution)/shard_map/all_to_all | solution.py:309
  1245.4 54.6 %copy-start.43 = (f32[256]{0:T(256)S(1)}, f32[256]{0:T(256)}, u32[]{:S(2)}) copy-start(f32[256]{0:T(256)} %copy-done.42) | copy-start | bytes 3076
  1249.9 57.8 %copy-start.44 = (f32[256]{0:T(256)S(1)}, f32[256]{0:T(256)}, u32[]{:S(2)}) copy-start(f32[256]{0:T(256)} %get-tuple-element.148) | copy-start | bytes 3076
  1302.9 16.0 %all-to-all-start.3 = ((f32[32,1,768]{2,1,0:T(1,128)}), f32[32,1,768]{2,1,0:T(1,128)S(1)}, u32[]{:S(2)}, u32[]{:S(2)}) async-start(f32[32,1,768]{2,1,0:T(1,128)} %copy.364), calls=%async_computation.7 | async-start | bytes 196608 | tf_op jit(solution)/shard_map/all_to_all | solution.py:551
  (45 other events, 640.1 us)
Sparse Core Ops, SparseCore 0:
  13.4 62.1 all-gather.13
  77.1 70.7 all-gather.17
  150.4 52.9 all-gather.15
  205.4 37.0 all-gather.19
  269.5 88.0 reduce-scatter.8
  359.1 115.3 all-gather.23
  477.1 52.6 all-gather.21
  531.4 63.4 all-gather.25
  597.0 53.0 all-gather.29
  689.9 71.2 reduce-scatter.12
  766.3 54.3 all-gather.27
  822.9 112.2 reduce-scatter.20
  938.0 35.7 reduce-scatter.18
  976.0 91.1 reduce-scatter.22
  1070.5 83.3 reduce-scatter.10
  1156.2 68.3 reduce-scatter.16
  1228.3 71.6 reduce-scatter.14

commit v2 on v1

--- a/solution.py
+++ b/solution.py
@@ -18,6 +18,10 @@
 GELU_B = 0.044715
 HALO = 16
 VMEM_BYTES = 48 * 1024 * 1024
+
+
+def after(x, *others):
+    return lax.optimization_barrier((x, *others))[0]
 
 
 def gelu_pair(x):
@@ -88,7 +92,7 @@
 
 
 def forward_kernel(
-    inner_ref, prev_ref, halo_ref, keep_ref, vec_ref, gwf_ref, gws_ref,
+    core_ref, inner_ref, prev_ref, halo_ref, keep_ref, vec_ref, gwf_ref, gws_ref,
     decay_ref, local_ref, cum_ref, last_ref, ext, b_ref, carry, *, block, own,
 ):
     c = pl.program_id(2)
@@ -115,7 +119,7 @@
     last_ref[...] = carry[...]
 
 
-def reverse_kernel(decay_ref, grad_ref, branch_ref, adj_ref, prod_ref, first_ref, carry, *, own):
+def reverse_kernel(core_ref, decay_ref, grad_ref, branch_ref, adj_ref, prod_ref, first_ref, carry, *, own):
     c = pl.program_id(2)
     rows = decay_ref.shape[0]
     place = lax.broadcasted_iota(jnp.int32, (8, own), 0)
@@ -151,7 +155,7 @@
 
 
 def backward_kernel(
-    inner_ref, prev_ref, halo_ref, keep_ref, vec_ref, gwf_ref, gws_ref, hidden_ref, before_ref, start_ref,
+    core_ref, inner_ref, prev_ref, halo_ref, keep_ref, vec_ref, gwf_ref, gws_ref, hidden_ref, before_ref, start_ref,
     adj_ref, prod_ref, suffix_ref,
     igrad_ref, tail_ref, head_ref, dgf_ref, dgs_ref, sums_ref, ext, hext, cext, *, block, own,
 ):
@@ -228,30 +232,229 @@
     sums_ref[7:8, :own] += total(d_log * rate)
 
 
+def lane_blocks(n_dp, n_z):
+    return [(d * n_z + z, z * n_dp + d) for d in range(n_dp) for z in range(n_z)]
+
+
+def to_z(x, n_dp, n_z):
+    w = x.shape[1] // (n_dp * n_z)
+    pairs = sorted(lane_blocks(n_dp, n_z), key=lambda p: p[1])
+    return jnp.concatenate([x[:, a * w : (a + 1) * w] for a, _ in pairs], axis=1)
+
+
+def from_z(x, n_dp, n_z):
+    w = x.shape[1] // (n_dp * n_z)
+    return jnp.concatenate([x[:, b * w : (b + 1) * w] for _, b in lane_blocks(n_dp, n_z)], axis=1)
+
+
+def total(pieces, i, steps):
+    q, ax, a, bx, b = pieces
+    low = i < steps // 2
+    pick = lambda u, v: jnp.where(low, u[...].astype(F32), v[...].astype(F32))
+    return q[...] + pick(ax, bx) + pick(a, b)
+
+
+def inverse(x):
+    return lax.rsqrt(jnp.mean(x * x, axis=1, keepdims=True) + EPSILON)
+
+
+def norm_kernel(gain_ref, *refs, cuts):
+    out_ref = refs[-1]
+    for k, ref in enumerate(refs[:-1]):
+
+        @pl.when(pl.program_id(0) == k)
+        def _(ref=ref):
+            x = ref[...].astype(F32)
+            out_ref[...] = to_z(x * inverse(x) * gain_ref[...], *cuts).astype(BF)
+
+
+def mid_kernel(q, ax, a, bx, b, tok_ref, gain_ref, mid_ref, normed_ref, *, cuts):
+    i = pl.program_id(0)
+    x = tok_ref[...].astype(F32) + from_z(total((q, ax, a, bx, b), i, pl.num_programs(0)), *cuts)
+    mid_ref[...] = x
+    normed_ref[...] = to_z(x * inverse(x) * gain_ref[...], *cuts).astype(BF)
+
+
+def norm_back(grad, x, gain):
+    inv = inverse(x)
+    g = grad * gain
+    return inv * g - x * (inv * inv * inv) * jnp.mean(x * g, axis=1, keepdims=True), grad * x * inv
+
+
+def add_rows(ref, x):
+    first = pl.program_id(0) == 0
+    terms = jnp.sum(x.reshape(-1, 8, x.shape[1]), axis=0)
+
+    @pl.when(first)
+    def _():
+        ref[...] = terms
+
+    @pl.when(jnp.logical_not(first))
+    def _():
+        ref[...] += terms
+
+
+def mid_back_kernel(q, ax, a, bx, b, mid_ref, cot_ref, gain_ref, grad_ref, low_ref, part_ref, *, cuts):
+    i = pl.program_id(0)
+    g = from_z(total((q, ax, a, bx, b), i, pl.num_programs(0)), *cuts)
+    back, part = norm_back(g, mid_ref[...], gain_ref[...])
+    grad = cot_ref[...].astype(F32) + back
+    grad_ref[...] = grad
+    low_ref[...] = to_z(grad, *cuts).astype(BF)
+    add_rows(part_ref, part)
+
+
+def tok_back_kernel(q, ax, a, bx, b, tok_ref, mid_grad_ref, gain_ref, grad_ref, part_ref, *, cuts):
+    i = pl.program_id(0)
+    g = from_z(total((q, ax, a, bx, b), i, pl.num_programs(0)), *cuts)
+    back, part = norm_back(g, tok_ref[...].astype(F32), gain_ref[...])
+    grad_ref[...] = mid_grad_ref[...] + back
+    add_rows(part_ref, part)
+
+
+def out_kernel(q, ax, a, bx, b, mid_ref, out_ref):
+    out_ref[...] = mid_ref[...] + total((q, ax, a, bx, b), pl.program_id(0), pl.num_programs(0))
+
+
+class OwnRows:
+    def __init__(self, rows, width, steps=4):
+        self.rows, self.width, self.steps = rows, width, steps
+
+    def call(self, kernel, pieces, arrays, gain, outs):
+        n, step = self.steps, self.rows // self.steps
+        tile = pl.BlockSpec((step, self.width), lambda i: (i, 0))
+        low = pl.BlockSpec((step, self.width), lambda i: (jnp.minimum(i, n // 2 - 1), 0))
+        high = pl.BlockSpec((step, self.width), lambda i: (jnp.maximum(i - n // 2, 0), 0))
+        line = pl.BlockSpec((1, self.width), lambda i: (0, 0))
+        part = pl.BlockSpec((8, self.width), lambda i: (0, 0))
+        shape = jax.ShapeDtypeStruct
+        gains = [] if gain is None else [gain.reshape(1, self.width)]
+        return pl.pallas_call(
+            kernel,
+            grid=(n,),
+            in_specs=([tile, low, low, high, high] if pieces else []) + [tile] * len(arrays) + [line] * len(gains),
+            out_specs=[part if t is None else tile for t in outs],
+            out_shape=[
+                shape((8, self.width), F32) if t is None else shape((self.rows, self.width), t) for t in outs
+            ],
+            compiler_params=pltpu.CompilerParams(vmem_limit_bytes=VMEM_BYTES),
+        )(*pieces, *arrays, *gains)
+
+
+def ff_pack_kernel(gate_ref, up_ref, out_ref, *, cuts):
+    n_dp, n_z, n_core = cuts
+    w = gate_ref.shape[1] // (n_dp * n_z * n_core)
+    for d in range(n_dp):
+        for c in range(n_core):
+            for j, ref in enumerate((gate_ref, up_ref)):
+                cols = [((d * n_z + z) * n_core + c) * w for z in range(n_z)]
+                x = jnp.concatenate([ref[:, o : o + w].astype(F32) for o in cols], axis=1)
+                out_ref[d * n_core + c, :, j * n_z * w : (j + 1) * n_z * w] = x.astype(BF)
+
+
+def ff_unpack_kernel(x_ref, gate_ref, up_ref, *, cuts):
+    n_dp, n_z, n_core = cuts
+    w = gate_ref.shape[1] // (n_dp * n_z * n_core)
+    for j, ref in enumerate((gate_ref, up_ref)):
+        for d in range(n_dp):
+            cols = []
+            for z in range(n_z):
+                for c in range(n_core):
+                    o = (j * n_z + z) * w
+                    cols.append(x_ref[d * n_core + c, :, o : o + w].astype(F32))
+            span = n_z * n_core * w
+            ref[:, d * span : (d + 1) * span] = jnp.concatenate(cols, axis=1)
+
+
 class Blocks:
-    def __init__(self, peers, seqs, back):
-        self.peers, self.seqs, self.back = peers, seqs, back
+    def __init__(self, peers, lines, seqs, back):
+        self.peers, self.lines, self.seqs, self.back = peers, lines, seqs, back
 
     def core(self, c):
         return self.peers - 1 - c if self.back else c
 
+    def block(self, d, s, c, core):
+        return (jnp.bitwise_xor(c, core[0]) * self.lines + d) * self.seqs + s
+
     def rows(self, count, width):
-        return pl.BlockSpec((count, width), lambda d, s, c: ((d * self.peers + self.core(c)) * self.seqs + s, 0))
+        return pl.BlockSpec((count, width), lambda d, s, c, core: (self.block(d, s, self.core(c), core), 0))
 
     def before(self, count, width, length):
         each = length // count
 
-        def index(d, s, c):
-            c = jnp.maximum(self.core(c) - 1, 0)
-            return (((d * self.peers + c) * self.seqs + s) * each + each - 1, 0)
+        def index(d, s, c, core):
+            return (self.block(d, s, jnp.maximum(self.core(c) - 1, 0), core) * each + each - 1, 0)
 
         return pl.BlockSpec((count, width), index)
 
     def sequence(self, count, width):
-        return pl.BlockSpec((count, width), lambda d, s, c: (d * self.seqs + s, 0))
+        return pl.BlockSpec((count, width), lambda d, s, c, core: (d * self.seqs + s, 0))
 
     def whole(self, *shape):
-        return pl.BlockSpec(shape, lambda d, s, c: (0,) * len(shape))
+        return pl.BlockSpec(shape, lambda d, s, c, core: (0,) * len(shape))
+
+    def call(self, kernel, in_specs, out_specs, out_shape, scratch, *args):
+        return pl.pallas_call(
+            kernel,
+            grid_spec=pltpu.PrefetchScalarGridSpec(
+                num_scalar_prefetch=1,
+                grid=(self.lines, self.seqs, self.peers),
+                in_specs=in_specs,
+                out_specs=out_specs,
+                scratch_shapes=scratch,
+            ),
+            out_shape=out_shape,
+            compiler_params=pltpu.CompilerParams(vmem_limit_bytes=VMEM_BYTES),
+        )(*args)
+
+
+class Plane:
+    def __init__(self, n_dp, n_core):
+        self.n_dp, self.n_core = n_dp, n_core
+        self.core = lax.axis_index("core")
+        self.dp = lax.axis_index("dp")
+
+    def near(self, x, k):
+        return lax.ppermute(x, "dp", [(i, i ^ k) for i in range(self.n_dp)])
+
+    def twin(self, x):
+        return lax.ppermute(x, "core", [(0, 1), (1, 0)])
+
+    def pieces(self, x):
+        half = x.shape[0] // 2
+        x1, x2 = self.near(x, 1), self.near(x, 2)
+        x3 = jnp.concatenate([self.near(x2[:half], 1), self.near(x1[half:], 2)], axis=0)
+        mine = [x, x1, x2, x3]
+        return mine + [self.twin(m) for m in mine]
+
+    def gather(self, x):
+        return jnp.concatenate(self.pieces(x), axis=0)
+
+    def terms(self, product, rows):
+        n = self.n_dp
+        order = (3, 1, 2, 0)
+        other = {k: self.twin(product((n + k) * rows, (n + k + 1) * rows).astype(BF)) for k in order}
+        q = {k: product(k * rows, (k + 1) * rows) + other[k].astype(F32) for k in order}
+        return [q[k] for k in range(n)]
+
+    def add_up(self, q):
+        half = q[0].shape[0] // 2
+        low = lambda x: x.astype(BF)
+        a3, b3 = self.near(low(q[3][:half]), 1), self.near(low(q[3][half:]), 2)
+        a1, b2 = self.near(low(q[1][:half]), 1), self.near(low(q[2][half:]), 2)
+        a = self.near(low(q[2][:half] + a3.astype(F32)), 2)
+        b = self.near(low(q[1][half:] + b3.astype(F32)), 1)
+        return q[0], a1, a, b2, b
+
+    def scatter(self, product, rows):
+        return self.add_up(self.terms(product, rows))
+
+    def in_order(self, x):
+        x = jnp.where(self.core == 1, x[::-1], x)
+        for bit in (1, 2):
+            y = x.reshape(2, self.n_dp // (2 * bit), 2, bit, *x.shape[2:])
+            x = jnp.where((self.dp & bit) != 0, y[:, :, ::-1], y).reshape(x.shape)
+        return jnp.swapaxes(x, 0, 1)
 
 
 def body(
@@ -282,15 +485,9 @@
     total_rows = group * rows
     lines = n_dp * seqs
 
-    def d_to_z(x):
-        lead = x.shape[:-1]
-        y = x.reshape(*lead, n_dp, n_z, n_core * drow)
-        return jnp.swapaxes(y, -3, -2).reshape(*lead, width)
-
-    def d_from_z(x):
-        lead = x.shape[:-1]
-        y = x.reshape(*lead, n_z, n_dp, n_core * drow)
-        return jnp.swapaxes(y, -3, -2).reshape(*lead, width)
+    plane = Plane(n_dp, n_core)
+    core = plane.core
+    core_id = core.astype(jnp.int32).reshape(1)
 
     def own_columns(w):
         lead = w.shape[0]
@@ -312,19 +509,19 @@
         y = jnp.swapaxes(x, 0, 1)
         return exchange(y.reshape(group * x.shape[0], x.shape[2]))
 
+    def sum_z(x):
+        return lax.psum_scatter(x, "z", scatter_dimension=0, tiled=True)
+
     def over_z(x):
         return lax.all_gather(x, "z", axis=0, tiled=True)
 
-    w_in = over_z(to_members(jnp.concatenate([window_columns(input_proj), own_columns(branch_proj)], axis=2)))
-    w_out = over_z(to_members(own_columns(output_proj.T)))
-
-    def ff_columns(w):
-        y = w.reshape(drow, n_dp, n_z, n_core, frow)
-        return jnp.transpose(y, (0, 1, 3, 2, 4)).reshape(drow, group, ff_own)
-
-    w_ff = over_z(to_members(jnp.concatenate([ff_columns(ffn_gate), ff_columns(ffn_up)], axis=2)))
-    w_down = over_z(ffn_down)
-
+    cuts = (n_dp, n_z)
+    cot = cotangent.reshape(rows, width)
+    tok = tokens.reshape(rows, width)
+    tok_pieces = plane.pieces(tok)
+    sent_in = to_members(window_columns(input_proj))
+    w_in = over_z(sent_in)
+    both = jnp.concatenate([own_columns(branch_proj), own_columns(output_proj.T)], axis=2)
     rrow = rec // devices
     small = jnp.concatenate(
         [
@@ -333,14 +530,35 @@
         ]
     )
     small_len = small.shape[0]
-    small = jnp.pad(small, (0, -small_len % (16 * 256))).reshape(-1, 256)
-    small = lax.all_gather(small, EVERY, axis=0, tiled=False).reshape(devices, -1)
+    marks = (1 - doc_reset).astype(BF).reshape(-1, 256)
+    small = jnp.pad(small, (0, -small_len % 256)).reshape(-1, 256)
+    marks_at = small.shape[0]
+    small = jnp.concatenate([small, marks])
+    small = jnp.pad(small, ((0, -small.shape[0] % 32), (0, 0)))
+    packed = small.shape[0]
+    small = over_z(after(small, sent_in))
+    sent_both = to_members(after(both, small, tok_pieces[1], tok_pieces[2]))
+    w_both = over_z(sent_both)
+    w_branch, w_out = w_both[:, :own], w_both[:, own:]
+    small = plane.gather(small).reshape(n_core, n_dp, n_z, packed, 256)
+    keep = lax.dynamic_index_in_dim(small, zi, 2, False)[:, :, marks_at : marks_at + rows // 256]
+    keep = keep.astype(F32).reshape(total_rows, 1)
+    small = jnp.swapaxes(plane.in_order(small), 1, 2).reshape(devices, packed * 256)
     gates_len = 2 * rrow * block
     gates_all = small[:, :gates_len].reshape(devices, 2, rrow, block)
     gates_all = jnp.swapaxes(gates_all, 0, 1).reshape(2, rec, block)
     rest = small[:, gates_len:small_len].astype(F32)
     gain = rest[:, :drow].reshape(width)
     fgain = rest[:, drow : 2 * drow].reshape(width)
+    ff_packed = pl.pallas_call(
+        functools.partial(ff_pack_kernel, cuts=(n_dp, n_z, n_core)),
+        out_shape=jax.ShapeDtypeStruct((group, drow, 2 * ff_own), BF),
+        compiler_params=pltpu.CompilerParams(vmem_limit_bytes=VMEM_BYTES),
+    )(ffn_gate, ffn_up)
+    sent_ff = exchange(after(ff_packed.reshape(group * drow, 2 * ff_own), tok_pieces[3], gain))
+    w_ff = over_z(sent_ff)
+    w_down = over_z(after(ffn_down, sent_ff))
+
     chan = rest[:, 2 * drow :].reshape(devices, taps + 4, rrow)
     chan = jnp.swapaxes(chan, 0, 1).reshape(taps + 4, rec)
     lam = chan[taps + 3 :]
@@ -362,168 +580,156 @@
     gwf = jnp.concatenate([gw_full[0], gw_full[1]], axis=1)
     gws = jnp.concatenate([gw_shared[0], gw_shared[1]], axis=1)
 
-    tok = d_to_z(tokens.reshape(rows, width)).astype(F32)
-    cot = cotangent.reshape(rows, width)
-    gain_z = d_to_z(gain)
-    fgain_z = d_to_z(fgain)
-    inv = lax.rsqrt(jnp.mean(tok * tok, axis=1, keepdims=True) + EPSILON)
-    normed_own = (tok * inv * gain_z).astype(BF)
-
-    def over_group(x):
-        return lax.all_gather(x, GROUP, axis=0, tiled=True)
-
-    def sum_group(x):
-        return lax.psum_scatter(x.astype(BF), GROUP, scatter_dimension=0, tiled=True).astype(F32)
-
-    normed = over_group(normed_own)
-    keep = over_group((1 - doc_reset).astype(BF).reshape(rows)).astype(F32).reshape(total_rows, 1)
-    cot_all = over_group(cot)
-
-    both = dot(normed, w_in)
-    inner = both[:, :window].astype(BF)
-    branch = both[:, window:]
-    ends = inner.reshape(n_dp, n_core, seqs, span, window)[:, n_core - 1, :, span - HALO :].reshape(lines * HALO, window)
+    mine = OwnRows(rows, width)
+    normed = pl.pallas_call(
+        functools.partial(norm_kernel, cuts=cuts),
+        grid=(group,),
+        in_specs=[pl.BlockSpec((1, width), lambda i: (0, 0))] + [pl.BlockSpec((rows, width), lambda i: (0, 0))] * group,
+        out_specs=pl.BlockSpec((rows, width), lambda i: (i, 0)),
+        out_shape=jax.ShapeDtypeStruct((total_rows, width), BF),
+        compiler_params=pltpu.CompilerParams(vmem_limit_bytes=VMEM_BYTES),
+    )(gain.reshape(1, width), *tok_pieces)
+    cot_all = plane.gather(after(cot, sent_ff))
+
+    inner = dot(normed, w_in).astype(BF)
+    branch = dot(normed, w_branch)
+    ends = inner.reshape(n_core, n_dp, seqs, span, window)[:, :, :, span - HALO :]
+    ends = jnp.where(core == 1, ends[0], ends[1]).reshape(lines * HALO, window)
     halo = lax.ppermute(ends, "z", [(i, i + 1) for i in range(n_z - 1)])
 
-    grid = (n_dp, seqs, n_core)
-    at = Blocks(n_core, seqs, False)
-    params = pltpu.CompilerParams(vmem_limit_bytes=VMEM_BYTES)
+    at = Blocks(n_core, n_dp, seqs, False)
     seq_in = [
         lambda b: b.rows(span, window), lambda b: b.before(HALO, window, span), lambda b: b.sequence(HALO, window),
         lambda b: b.rows(span, 1), lambda b: b.whole(8, window), lambda b: b.whole(block, window),
         lambda b: b.whole(block, 2 * lanes),
     ]
     row_f32 = jax.ShapeDtypeStruct((total_rows, own), F32)
-    decay, local, cum, last = pl.pallas_call(
+    decay, local, cum, last = at.call(
         functools.partial(forward_kernel, block=block, own=own),
-        grid=grid,
-        in_specs=[f(at) for f in seq_in],
-        out_specs=[at.rows(span, own)] * 3 + [at.sequence(8, own)],
-        out_shape=[row_f32] * 3 + [jax.ShapeDtypeStruct((lines * 8, own), F32)],
-        scratch_shapes=[
-            pltpu.VMEM((span + HALO, window), F32), pltpu.VMEM((span, own), F32), pltpu.VMEM((8, own), F32),
-        ],
-        compiler_params=params,
-    )(inner, inner, halo, keep, vec, gwf, gws)
-
-    def carried(x, order, reached):
-        every = lax.all_gather(x.reshape(lines, 8, own)[:, :2], "z", axis=0, tiled=False)
+        [f(at) for f in seq_in],
+        [at.rows(span, own)] * 3 + [at.sequence(8, own)],
+        [row_f32] * 3 + [jax.ShapeDtypeStruct((lines * 8, own), F32)],
+        [pltpu.VMEM((span + HALO, window), F32), pltpu.VMEM((span, own), F32), pltpu.VMEM((8, own), F32)],
+        core_id, inner, inner, halo, keep, vec, gwf, gws,
+    )
+
+    def carried(x, way, beside):
+        x = x.reshape(lines, 8, own)[:, :2]
         state = jnp.zeros((lines, own), F32)
-        for k in order:
-            state = jnp.where(reached(k), every[k, :, 1] * state + every[k, :, 0], state)
+        for k in range(n_z - 1, 0, -1):
+            hops = [(i, i + way * k) for i in range(n_z) if 0 <= i + way * k < n_z]
+            come = after(lax.ppermute(x, "z", hops), *beside)
+            state = come[:, 1] * state + come[:, 0]
         return state
 
-    start = carried(last, range(n_z), lambda k: k < zi)
+    start = carried(last, 1, [branch])
 
     def by_line(x):
-        return x.reshape(n_dp, 1, seqs, 1, own)
+        return x.reshape(1, n_dp, seqs, 1, own)
 
     def spread(x):
-        return x.reshape(n_dp, n_core, seqs, span, own)
+        return x.reshape(n_core, n_dp, seqs, span, own)
 
     hidden = (spread(local) + spread(cum) * by_line(start)).reshape(total_rows, own)
     mixed_out = (hidden * gelu_only(branch)).astype(BF)
-    mid = tok + sum_group(dot_cols(mixed_out, w_out))
-
-    finv = lax.rsqrt(jnp.mean(mid * mid, axis=1, keepdims=True) + EPSILON)
-    fnormed = over_group((mid * finv * fgain_z).astype(BF))
+    terms = plane.scatter(lambda lo, hi: dot_cols(mixed_out[lo:hi], w_out), rows)
+    mid, fnormed = mine.call(functools.partial(mid_kernel, cuts=cuts), terms, [tok], fgain, [F32, BF])
+
+    fnormed = plane.gather(fnormed)
     pre_lin = dot(fnormed, w_ff)
     act, slope = gelu_pair(pre_lin[:, :ff_own])
     lin = pre_lin[:, ff_own:]
     fhidden = (act * lin).astype(BF)
-    hid_grad = dot_cols(cot_all, w_down)
+    down_terms = dot_rows(fhidden, cot_all).astype(BF)
+    hid_grad = dot_cols(after(cot_all, down_terms), w_down)
     fgrad = jnp.concatenate([(hid_grad * lin * slope).astype(BF), (hid_grad * act).astype(BF)], axis=1)
-    fnormed_grad = sum_group(dot_cols(fgrad, w_ff))
-    layer_out = d_from_z(mid) + sum_group(dot(fhidden, w_down))
-
-    fg = fgain_z * fnormed_grad
-    ffn_gain_part = jnp.sum(fnormed_grad * mid * finv, axis=0)
-    mid_grad = (
-        d_to_z(cot).astype(F32) + finv * fg - mid * (finv * finv * finv) * jnp.mean(mid * fg, axis=1, keepdims=True)
-    )
-    mid_low = over_group(mid_grad.astype(BF))
-
-    def sum_z(x):
-        return lax.psum_scatter(x.astype(BF), "z", scatter_dimension=0, tiled=True)
-
-    down_out = sum_z(dot_rows(fhidden, cot_all)).astype(F32)
-    ff_part = exchange(sum_z(dot_rows(fnormed, fgrad))).reshape(group, drow, 2, ff_own)
-
-    def ff_natural(x):
-        y = x.reshape(n_dp, n_core, drow, n_z, frow)
-        return jnp.transpose(y, (2, 0, 3, 1, 4)).reshape(drow, ff).astype(F32)
+    down_sum = sum_z(down_terms)
+    down_out = down_sum.astype(F32)
+    ff_terms = dot_rows(fnormed, fgrad).astype(BF)
+    terms = plane.scatter(lambda lo, hi: dot_cols(fgrad[lo:hi], w_ff), rows)
+    ff_sum = sum_z(after(ff_terms, down_sum))
+    ff_part = exchange(ff_sum).reshape(group, drow, 2 * ff_own)
+    terms = (after(terms[0], down_sum, ff_terms), *terms[1:])
+    mid_grad, mid_low, ffn_gain_part = mine.call(
+        functools.partial(mid_back_kernel, cuts=cuts), terms, [mid, cot], fgain, [F32, BF, None]
+    )
+    mid_low = plane.gather(mid_low)
+    later = after(fhidden, mid_grad)
+    out_terms = plane.terms(lambda lo, hi: dot(later[lo:hi], w_down), rows)
+    mid_low = after(mid_low, *out_terms)
+    out_terms[3] = after(out_terms[3], mid_low)
+    layer_out = mine.call(out_kernel, plane.add_up(out_terms), [mid], None, [F32])[0]
+
+    gate_out, up_out = pl.pallas_call(
+        functools.partial(ff_unpack_kernel, cuts=(n_dp, n_z, n_core)),
+        out_shape=[jax.ShapeDtypeStruct((drow, ff), F32)] * 2,
+        compiler_params=pltpu.CompilerParams(vmem_limit_bytes=VMEM_BYTES),
+    )(ff_part)
 
     mixed_grad = dot(mid_low, w_out)
     act_r, slope_r = gelu_pair(branch)
     branch_grad = (mixed_grad * hidden * slope_r).astype(BF)
-    back = Blocks(n_core, seqs, True)
-    adj, prod, front = pl.pallas_call(
+    back = Blocks(n_core, n_dp, seqs, True)
+    adj, prod, front = back.call(
         functools.partial(reverse_kernel, own=own),
-        grid=grid,
-        in_specs=[back.rows(span, own)] * 3,
-        out_specs=[back.rows(span, own)] * 2 + [back.sequence(8, own)],
-        out_shape=[row_f32] * 2 + [jax.ShapeDtypeStruct((lines * 8, own), F32)],
-        scratch_shapes=[pltpu.VMEM((8, own), F32)],
-        compiler_params=params,
-    )(decay, mixed_grad, branch)
-    suffix = carried(front, reversed(range(n_z)), lambda k: k > zi)
+        [back.rows(span, own)] * 3,
+        [back.rows(span, own)] * 2 + [back.sequence(8, own)],
+        [row_f32] * 2 + [jax.ShapeDtypeStruct((lines * 8, own), F32)],
+        [pltpu.VMEM((8, own), F32)],
+        core_id, after(decay, ff_sum), mixed_grad, branch,
+    )
+    both = jnp.concatenate([dot_rows(normed, branch_grad).astype(BF), dot_rows(mid_low, mixed_out).astype(BF)], axis=1)
+    suffix = carried(front, -1, [both])
 
     def eight(x):
         return jnp.broadcast_to(x[:, None, :], (lines, 8, own)).reshape(lines * 8, own)
 
-    igrad, tail, head, dgf, dgs, sums = pl.pallas_call(
+    igrad, tail, head, dgf, dgs, sums = back.call(
         functools.partial(backward_kernel, block=block, own=own),
-        grid=grid,
-        in_specs=[f(back) for f in seq_in]
+        [f(back) for f in seq_in]
         + [
             back.rows(span, own), back.before(8, own, span), back.sequence(8, own), back.rows(span, own),
             back.rows(span, own), back.sequence(8, own),
         ],
-        out_specs=[
+        [
             back.rows(span, window), back.sequence(HALO, window), back.sequence(8, window), back.whole(block, window),
             back.whole(block, 2 * lanes), back.whole(8, window),
         ],
-        out_shape=[
+        [
             jax.ShapeDtypeStruct((total_rows, window), BF), jax.ShapeDtypeStruct((lines * HALO, window), F32),
             jax.ShapeDtypeStruct((lines * 8, window), F32), jax.ShapeDtypeStruct((block, window), F32),
             jax.ShapeDtypeStruct((block, 2 * lanes), F32), jax.ShapeDtypeStruct((8, window), F32),
         ],
-        scratch_shapes=[
+        [
             pltpu.VMEM((span + HALO, window), F32), pltpu.VMEM((span + 8, own), F32), pltpu.VMEM((span + 8, window), F32),
         ],
-        compiler_params=params,
-    )(inner, inner, halo, keep, vec, gwf, gws, hidden, hidden, eight(start), adj, prod, eight(suffix))
-
-    after = lax.ppermute(head.astype(BF), "z", [(i + 1, i) for i in range(n_z - 1)]).astype(F32).reshape(lines, 8, window)
+        core_id, inner, inner, halo, keep, vec, gwf, gws, hidden, hidden, eight(start), adj, prod, eight(suffix),
+    )
+
+    coming = lax.ppermute(head.astype(BF), "z", [(i + 1, i) for i in range(n_z - 1)]).astype(F32).reshape(lines, 8, window)
     fix = jnp.zeros((lines, HALO, window), F32)
     for tap in range(1, taps):
-        fix = fix.at[:, HALO - tap :, :].add(vec[tap] * after[:, :tap])
-    tail = (tail.reshape(lines, HALO, window) + fix).astype(BF).reshape(n_dp, 1, seqs, HALO, window)
+        fix = fix.at[:, HALO - tap :, :].add(vec[tap] * coming[:, :tap])
+    tail = (tail.reshape(lines, HALO, window) + fix).astype(BF).reshape(1, n_dp, seqs, HALO, window)
     igrad = lax.dynamic_update_slice(
-        igrad.reshape(n_dp, n_core, seqs, span, window), tail, (0, n_core - 1, 0, span - HALO, 0)
+        igrad.reshape(n_core, n_dp, seqs, span, window), tail, (1 - core, 0, 0, span - HALO, 0)
     ).reshape(total_rows, window)
-    rgrad = jnp.concatenate([igrad, branch_grad], axis=1)
-    normed_grad = sum_group(dot_cols(rgrad, w_in))
-
-    g = gain_z * normed_grad
-    gain_part = jnp.sum(normed_grad * tok * inv, axis=0)
-    input_grad = mid_grad + inv * g - tok * (inv * inv * inv) * jnp.mean(tok * g, axis=1, keepdims=True)
-    input_grad = d_from_z(input_grad)
-
-    out_part = exchange(sum_z(dot_rows(mid_low, mixed_out))).reshape(group, drow, own)
-    in_part = exchange(sum_z(dot_rows(normed, rgrad))).reshape(group, drow, window + own)
+    both_sum = sum_z(after(both, ff_sum))
+    igrad = after(igrad, layer_out, both_sum)
+    in_terms = dot_rows(normed, igrad).astype(BF)
+    igrad = after(igrad, in_terms)
+    terms = plane.scatter(
+        lambda lo, hi: dot_cols(igrad[lo:hi], w_in) + dot_cols(branch_grad[lo:hi], w_branch), rows
+    )
+    both_part = exchange(both_sum).reshape(group, drow, 2 * own)
 
     def own_natural(x):
         full = jnp.swapaxes(x[:, :, :block], 0, 1).reshape(drow, group * block)
         rest = jnp.swapaxes(x[:, :, block : block + part], 0, 1).reshape(drow, group * part)
         return jnp.concatenate([full, rest], axis=1).astype(F32)
 
-    full = jnp.swapaxes(in_part[:, :, :block], 0, 1).reshape(drow, group * block).astype(F32)
-    turned = in_part[:, :, block:window].astype(F32).reshape(shared, sharers, drow, block)
-    other = sum(jnp.roll(turned[:, q], part * q, axis=2) for q in range(sharers))
-    input_proj_grad = jnp.concatenate([full, jnp.swapaxes(other, 0, 1).reshape(drow, shared * block)], axis=1)
-    branch_proj_grad = own_natural(in_part[:, :, window:])
-    output_proj_grad = own_natural(out_part).T
+    branch_proj_grad = own_natural(both_part[:, :, :own])
+    output_proj_grad = own_natural(both_part[:, :, own:]).T
 
     def place_window(x, axis_len):
         lead = x.shape[:-1]
@@ -535,6 +741,40 @@
         y = lax.dynamic_update_slice_in_dim(y, x[..., :block], me * block, x.ndim - 1)
         return lax.dynamic_update_slice_in_dim(y, turned, shared_at, x.ndim - 1)
 
+    dg_full = jnp.stack([dgf[:, :block], dgf[:, block:]])
+    dg_shared = jnp.stack([dgs[:, :part], dgs[:, lanes : lanes + part]])
+    dg_shared = lax.dynamic_slice_in_dim(
+        jnp.concatenate([dg_shared, dg_shared], 1), lax.rem(block - quarter * part, block), block, 1
+    )
+    lot = n_core * rrow
+    lots = (block + 2 * lot - 2) // lot
+
+    def by_z(x, row):
+        y = jnp.swapaxes(x, 0, 1).reshape(block, -1).astype(BF)
+        q = row // lot
+        y = lax.dynamic_update_slice(jnp.zeros((n_z * lot, y.shape[1]), BF), y, (row - q * lot, 0))
+        y = y.reshape(n_z, lot, -1)
+        return lax.dynamic_slice_in_dim(jnp.concatenate([y, y]), lax.rem(n_z - lax.rem(q, n_z), n_z), n_z, 0)
+
+    def to_lines(x, row):
+        q = row // lot
+        q = q + lax.rem(zi + n_z - lax.rem(q, n_z), n_z)
+        y = jnp.zeros((n_dp, *x.shape), x.dtype)
+        return lax.dynamic_update_slice(y, x[None], (jnp.minimum(q // n_z, n_dp - 1), 0, 0))
+
+    assert lots <= n_z
+    gates = jnp.concatenate([by_z(dg_full, me * block), by_z(dg_shared, shared_at)], axis=2)
+    gates = sum_z(after(gates.reshape(n_z * lot, 2 * (block + part)), both_sum))
+    in_part = exchange(sum_z(after(in_terms, gates))).reshape(group, drow, window)
+    gates = jnp.concatenate(
+        [to_lines(gates[:, : 2 * block], me * block), to_lines(gates[:, 2 * block :], shared_at)], axis=2
+    )
+    gates = exchange(gates.reshape(group * rrow, 2 * (block + part))).reshape(group, rrow, 2 * (block + part)).astype(F32)
+    terms = (after(terms[0], gates, both_part, gate_out, up_out), *terms[1:])
+    input_grad, gain_part = mine.call(
+        functools.partial(tok_back_kernel, cuts=cuts), terms, [tok, mid_grad], gain, [F32, None]
+    )
+
     lane = jnp.arange(window)
     mine = lane < block + part
     sums = jnp.where(jnp.concatenate([jnp.ones((5, window), bool), jnp.broadcast_to(mine, (3, window))], axis=0), sums, 0.0)
@@ -542,7 +782,7 @@
     sums = jnp.concatenate([sums[:7], sums[7:8] * (POWER * jax.nn.sigmoid(-lam))], axis=0)
     vectors = jnp.concatenate(
         [
-            d_from_z(gain_part).reshape(devices, drow), d_from_z(ffn_gain_part).reshape(devices, drow),
+            jnp.sum(gain_part, axis=0).reshape(devices, drow), jnp.sum(ffn_gain_part, axis=0).reshape(devices, drow),
             jnp.swapaxes(sums.reshape(8, devices, rrow), 0, 1).reshape(devices, 8 * rrow),
         ],
         axis=1,
@@ -554,17 +794,15 @@
     fgain_out = vectors[drow : 2 * drow]
     chan_out = vectors[2 * drow :].reshape(8, rrow)
 
-    dg_full = jnp.stack([dgf[:, :block], dgf[:, block:]])
-    dg_shared = jnp.stack([dgs[:, :part], dgs[:, lanes : lanes + part]])
-    dg_shared = lax.dynamic_slice_in_dim(
-        jnp.concatenate([dg_shared, dg_shared], 1), lax.rem(block - quarter * part, block), block, 1
-    )
-    gates = jnp.zeros((2, rec, block), BF)
-    gates = lax.dynamic_update_slice(gates, dg_full.astype(BF), (0, me * block, 0))
-    gates = lax.dynamic_update_slice(gates, dg_shared.astype(BF), (0, shared_at, quarter * part))
-    gates = jnp.swapaxes(gates.reshape(2, devices, rrow, block), 0, 1).reshape(devices * 2 * rrow, block)
-    gates = lax.all_to_all(gates, EVERY, split_axis=0, concat_axis=0, tiled=True)
-    gates_out = jnp.sum(gates.reshape(devices, 2, rrow, block).astype(F32), axis=0)
+    gates_out = jnp.sum(gates[:, :, : 2 * block], axis=0).reshape(rrow, 2, block)
+    rest = jnp.sum(gates[:, :, 2 * block :].reshape(shared, sharers, rrow, 2, part), axis=0)
+    rest = jnp.transpose(rest, (1, 2, 0, 3)).reshape(rrow, 2, block)
+    gates_out = jnp.swapaxes(gates_out + rest, 0, 1)
+
+    full = jnp.swapaxes(in_part[:, :, :block], 0, 1).reshape(drow, group * block).astype(F32)
+    turned = in_part[:, :, block:window].astype(F32).reshape(shared, sharers, drow, block)
+    other = sum(jnp.roll(turned[:, q], part * q, axis=2) for q in range(sharers))
+    input_proj_grad = jnp.concatenate([full, jnp.swapaxes(other, 0, 1).reshape(drow, shared * block)], axis=1)
 
     return (
         layer_out.reshape(seqs, span, width),
@@ -579,8 +817,8 @@
         chan_out[taps + 3],
         output_proj_grad,
         fgain_out,
-        ff_natural(ff_part[:, :, 0]),
-        ff_natural(ff_part[:, :, 1]),
+        gate_out,
+        up_out,
         down_out,
     )
 

time: 1340 us -> 774 us (0.58)
  waiting for transfers between devices: 781 us -> 167 us
  starting transfers between devices: 29.8 us -> 94.5 us
  matrix products: 166 us -> 210 us
  local copies, waits for them, and re-layouts: 132 us -> 90.7 us
  Pallas kernels: 42.6 us -> 76.7 us
  blocking collectives: 106 us -> 75.1 us
  other arithmetic: 56.6 us -> 37.4 us
    reduce_scatter x8 -> x5, waiting for transfers between devices: 313 us -> 0.03 us  [sum_z(): return lax.psum_scatter(x, 'z', scatter_dimension=0, tiled=True)]
    all_gather x5 -> x0, waiting for transfers between devices: 233 us -> none  [the longest x4 201 us: over_group(): return lax.all_gather(x, GROUP, axis=0, tiled=True)]
    all_gather x4, waiting for transfers between devices: 193 us -> 0.02 us  [over_z(): return lax.all_gather(x, 'z', axis=0, tiled=True)]
    ppermute x0 -> x86, waiting for transfers between devices: none -> 136 us  [the longest x44 132 us: near(): return lax.ppermute(x, 'dp', [(i, i ^ k) for i in range(self.n_dp)])]
    ppermute x0 -> x86, starting transfers between devices: none -> 66.5 us  [the longest x44 41.2 us: near(): return lax.ppermute(x, 'dp', [(i, i ^ k) for i in range(self.n_dp)])]
    dot_general x4 -> x33, matrix products: 61.6 us -> 104 us  [dot_cols(): lax.dot_general(a, b, (((1,), (1,)), ((), ())), preferred_element_type=F32)]
    pallas_call x3 -> x10, Pallas kernels: 42.6 us -> 76.7 us  [the longest x3 43.9 us: call(): pl.pallas_call(kernel, grid_spec=pltpu.PrefetchScalarGridSpec(num_scalar_...]
    convert_element_type x12 -> x4, local copies, waits for them, and re-layouts: 33.6 us -> 0.48 us  [by_z(): y = jnp.swapaxes(x, 0, 1).reshape(block, -1).astype(BF)]
  transfers between devices with their start and end apart: 25 -> 102, of which waited for: 18 -> 28; matrix products, arithmetic and copies ran while one was open for 21% -> 41% of each run, Pallas kernels for 3% -> 10%
where the time goes in v2:
time: 774 us; the launch traced here: 768 us
  matrix products  210 us (27%)
  waiting for transfers between devices  167 us (22%)
  starting transfers between devices  94.5 us (12%)
  local copies, waits for them, and re-layouts  90.7 us (12%)
  Pallas kernels  76.7 us (10%)
  blocking collectives  75.1 us (10%)
  other arithmetic  37.4 us (5%)
  between operations  16.7 us (2%)
    ppermute x44, waiting for transfers between devices, near(): return lax.ppermute(x, 'dp', [(i, i ^ k) for i in range(self.n_dp)])  132 us
    dot_general x33, matrix products, dot_cols(): lax.dot_general(a, b, (((1,), (1,)), ((), ())), preferred_element_type=F32)  104 us
    dot_general x12, matrix products, dot(): lax.dot_general(a, b, (((1,), (0,)), ((), ())), preferred_element_type=F32)  56.4 us
    all_to_all x3, blocking collectives, exchange(): return lax.all_to_all(x, GROUP, split_axis=0, concat_axis=0, tiled=True)  55 us
    dot_general x5, matrix products, dot_rows(): lax.dot_general(a, b, (((0,), (0,)), ((), ())), preferred_element_type=F32)  49.2 us
    pallas_call x3, Pallas kernels, call(): pl.pallas_call(kernel, grid_spec=pltpu.PrefetchScalarGridSpec(num_scalar_...  43.9 us
    unnamed x188, local copies, waits for them, and re-layouts  42.8 us
    ppermute x44, starting transfers between devices, near(): return lax.ppermute(x, 'dp', [(i, i ^ k) for i in range(self.n_dp)])  41.2 us
  transfers between devices with their start and end apart: 102, of which 28 were waited for; matrix products, arithmetic and copies ran while one was open for 41% of the time, Pallas kernels for 10%

profile of v2, /device:TPU:0, one launch (start us, length us, event | category | flops | bytes accessed | tf_op | source)
XLA Modules:
  0.0 767.7 jit_solution(16934076794985326147)
XLA Ops:
  9.9 14.8 %all_to_all.75 = bf16[8,64,512]{2,1,0:T(8,128)(2,1)} all-to-all(bf16[8,64,512]{2,1,0:T(8,128)(2,1)S(1)} %copy.99), channel_id=1, replica_groups=mesh['dp'=4,'z'=4,'core'=2] {'dp','core'}, dimensions={0} | all-to-all | bytes 1048576 | tf_op jit(solution)/shard_map/all_to_all | solution.py:506
  29.8 20.0 %all_gather.15 = bf16[768,256]{1,0:T(8,128)(2,1)S(1)} all-gather(bf16[192,256]{1,0:T(8,128)(2,1)S(1)} %fusion.138), channel_id=1, replica_groups=mesh['dp'=4,'z'=4,'core'=2] {'z'}, dimensions={0}, use_global_device_ids=true | all-gather | bytes 491520 | tf_op jit(solution)/shard_map/all_gather | solution.py:516
  51.1 16.1 %all_to_all.76 = bf16[8,64,768]{2,1,0:T(8,128)(2,1)} all-to-all(bf16[8,64,768]{2,1,0:T(8,128)(2,1)S(1)} %copy.106), channel_id=1, replica_groups=mesh['dp'=4,'z'=4,'core'=2] {'dp','core'}, dimensions={0} | all-to-all | bytes 1572864 | tf_op jit(solution)/shard_map/all_to_all | solution.py:506
  71.2 9.2 %collective-permute-done.10 = bf16[128,2048]{1,0:T(8,128)(2,1)S(1)} collective-permute-done((bf16[128,2048]{1,0:T(8,128)(2,1)S(1)}, bf16[128,2048]{1,0:T(8,128)(2,1)S(1)}, u32[]{:S(2)}, u32[]{:S(2)}) %collective-permute-start.10) | collective-permute-done | bytes 524320 | tf_op jit(solution)/shard_map/ppermute | solution.py:418
  83.5 24.1 %all_to_all.77 = bf16[8,64,1536]{2,1,0:T(8,128)(2,1)} all-to-all(bf16[8,64,1536]{2,1,0:T(8,128)(2,1)S(1)} %shard_map.274), channel_id=1, replica_groups=mesh['dp'=4,'z'=4,'core'=2] {'dp','core'}, dimensions={0} | all-to-all | bytes 3145728 | tf_op jit(solution)/shard_map/all_to_all | solution.py:506
  109.9 8.5 %collective-permute-done.1 = bf16[768,256]{1,0:T(8,128)(2,1)S(1)} collective-permute-done((bf16[768,256]{1,0:T(8,128)(2,1)S(1)}, bf16[768,256]{1,0:T(8,128)(2,1)S(1)}, u32[]{:S(2)}, u32[]{:S(2)}) %collective-permute-start.1) | collective-permute-done | bytes 393248 | tf_op jit(solution)/shard_map/ppermute | solution.py:418
  147.1 9.7 %shard_map.271 = bf16[2048,2048]{1,0:T(8,128)(2,1)} custom-call(f32[1,2048]{1,0:T(1,128)S(1)} %copy-done.10, bf16[256,2048]{1,0:T(8,128)(2,1)S(1)} %bitcast.219, bf16[256,2048]{1,0:T(8,128)(2,1)} %collective-permute-done.8.refs_1_, bf16[256,2048]{1,0:T(8,128)(2,1)S(1)} %collective-permute-done.9.refs_2_, ...), custom_call_target="tpu_custom_call" | custom-call | tf_op jit(solution)/shard_map/pallas_call | solution.py:584
  158.6 8.5 %convolution_convert_fusion.3.inner_ref.prev_ref = bf16[2048,512]{1,0:T(8,128)(2,1)S(1)} fusion(bf16[2048,2048]{1,0:T(8,128)(2,1)} %shard_map.271, bf16[2048,512]{1,0:T(8,128)(2,1)} %all-gather.5.cloned.1.call-done), kind=kOutput, calls=%fused_computation.46 | convolution fusion | flops 4296015872 | bytes 12582912 | tf_op jit(solution)/shard_map/dot_general | solution.py:40
  174.4 13.2 %shard_map.272 = (f32[2048,384]{1,0:T(8,128)}, f32[2048,384]{1,0:T(8,128)}, f32[2048,384]{1,0:T(8,128)}, f32[32,384]{1,0:T(8,128)S(1)}) custom-call(s32[1]{0:T(128)} %bitcast.core_ref, bf16[2048,512]{1,0:T(8,128)(2,1)S(1)} %convolution_convert_fusion.3.inner_ref.prev_ref, bf16[2048,512]{1,0:T(8,128)(2,1)S(1)} %convolution_convert_fusion.3.inner_ref.prev_ref, ...), custom_call_target="tpu_custom_call" | custom-call | tf_op jit(solution)/shard_map/pallas_call | solution.py:397
  187.6 10.2 %collective-permute-start.19 = (f32[4,2,384]{2,1,0:T(2,128)S(1)}, f32[4,2,384]{2,1,0:T(2,128)S(1)}, u32[]{:S(2)}, u32[]{:S(2)}) collective-permute-start(f32[4,2,384]{2,1,0:T(2,128)S(1)} %slice.785), channel_id=1, source_target_pairs={{0,6},{1,7},{8,14},{9,15},{16,22},{17,23},{24,30},{25,31}} | collective-permute-start | bytes 36872 | tf_op jit(solution)/shard_map/ppermute | solution.py:621
  212.1 7.7 %fusion.157.branch_ref = f32[2048,384]{1,0:T(8,128)S(1)} fusion(bf16[2048,2048]{1,0:T(8,128)(2,1)} %shard_map.271, bf16[2048,768]{1,0:T(8,128)(2,1)} %all-gather.7.cloned.1.call-done), kind=kOutput, calls=%fused_computation.257 | convolution fusion | flops 3221225472 | bytes 13107200 | tf_op jit(solution)/shard_map/dot_general | solution.py:40
  234.7 10.4 %collective-permute-done.28 = bf16[128,2048]{1,0:T(8,128)(2,1)S(1)} collective-permute-done((bf16[128,2048]{1,0:T(8,128)(2,1)S(1)}, bf16[128,2048]{1,0:T(8,128)(2,1)S(1)}, u32[]{:S(2)}, u32[]{:S(2)}) %collective-permute-start.28) | collective-permute-done | bytes 524320 | tf_op jit(solution)/shard_map/ppermute | solution.py:418
  247.6 7.8 %collective-permute-done.27.bx = bf16[128,2048]{1,0:T(8,128)(2,1)S(1)} collective-permute-done((bf16[128,2048]{1,0:T(8,128)(2,1)S(1)}, bf16[128,2048]{1,0:T(8,128)(2,1)S(1)}, u32[]{:S(2)}, u32[]{:S(2)}) %collective-permute-start.27) | collective-permute-done | bytes 524320 | tf_op jit(solution)/shard_map/ppermute | solution.py:418
  260.0 8.5 %collective-permute-done.29.b = bf16[128,2048]{1,0:T(8,128)(2,1)S(1)} collective-permute-done((bf16[128,2048]{1,0:T(8,128)(2,1)S(1)}, bf16[128,2048]{1,0:T(8,128)(2,1)S(1)}, u32[]{:S(2)}, u32[]{:S(2)}) %collective-permute-start.29) | collective-permute-done | bytes 524320 | tf_op jit(solution)/shard_map/ppermute | solution.py:418
  282.6 17.9 %collective-permute-done.31 = bf16[256,2048]{1,0:T(8,128)(2,1)S(1)} collective-permute-done((bf16[256,2048]{1,0:T(8,128)(2,1)S(1)}, bf16[256,2048]{1,0:T(8,128)(2,1)S(1)}, u32[]{:S(2)}, u32[]{:S(2)}) %collective-permute-start.31) | collective-permute-done | bytes 1048608 | tf_op jit(solution)/shard_map/ppermute | solution.py:418
  306.1 8.1 %collective-permute-done.32 = bf16[128,2048]{1,0:T(8,128)(2,1)S(1)} collective-permute-done((bf16[128,2048]{1,0:T(8,128)(2,1)S(1)}, bf16[128,2048]{1,0:T(8,128)(2,1)S(1)}, u32[]{:S(2)}, u32[]{:S(2)}) %collective-permute-start.32) | collective-permute-done | bytes 524320 | tf_op jit(solution)/shard_map/ppermute | solution.py:418
  321.0 18.0 %fusion.199 = f32[2048,1536]{0,1:T(8,128)S(1)} fusion(bf16[2048,2048]{1,0:T(8,128)(2,1)} %constant_dynamic-update-slice_fusion.11, bf16[2048,1536]{1,0:T(8,128)(2,1)} %all-gather.9.cloned.1.call-done), kind=kOutput, calls=%fused_computation.378 | convolution fusion | flops 12884901888 | bytes 27262976 | tf_op jit(solution)/shard_map/dot_general | solution.py:40
  345.2 10.3 %convolution_convert_fusion.1 = bf16[768,2048]{1,0:T(8,128)(2,1)} fusion(bf16[2048,768]{0,1:T(8,128)(2,1)S(1)} %multiply_convert_fusion.2, bf16[2048,2048]{1,0:T(8,128)(2,1)} %constant_dynamic-update-slice_fusion.20), kind=kOutput, calls=%fused_computation.31 | convolution fusion | flops 6444023808 | bytes 14680064 | tf_op jit(solution)/shard_map/dot_general | solution.py:44
  355.6 18.4 %multiply_convert_fusion = (bf16[2048,768]{0,1:T(8,128)(2,1)S(1)}, bf16[2048,768]{0,1:T(8,128)(2,1)S(1)}) fusion(f32[2048,1536]{0,1:T(8,128)} %copy-done.27, bf16[2048,2048]{1,0:T(8,128)(2,1)} %constant_dynamic-update-slice_fusion.20, bf16[768,2048]{1,0:T(8,128)(2,1)} %all-gather.11.cloned.1.call-done), kind=kOutput, calls=%fused_computation.21 | convolution fusion | flops 6477053952 | bytes 30408704 | tf_op jit(solution)/shard_map/dot_general | solution.py:48
  374.0 6.9 convolution_convert_fusion.10
  387.1 17.7 %convolution_convert_fusion = bf16[2048,1536]{1,0:T(8,128)(2,1)} fusion(bf16[2048,2048]{1,0:T(8,128)(2,1)} %constant_dynamic-update-slice_fusion.11, bf16[2048,768]{0,1:T(8,128)(2,1)S(1)} %get-tuple-element.190, bf16[2048,768]{0,1:T(8,128)(2,1)S(1)} %get-tuple-element.191), kind=kOutput, calls=%fused_computation.18 | convolution fusion | flops 12900630528 | bytes 20971520 | tf_op jit(solution)/shard_map/dot_general | solution.py:44
  422.6 6.4 convert_add_fusion.7
  450.7 10.2 %collective-permute-done.55.b = bf16[128,2048]{1,0:T(8,128)(2,1)S(1)} collective-permute-done((bf16[128,2048]{1,0:T(8,128)(2,1)S(1)}, bf16[128,2048]{1,0:T(8,128)(2,1)S(1)}, u32[]{:S(2)}, u32[]{:S(2)}) %collective-permute-start.55) | collective-permute-done | bytes 524320 | tf_op jit(solution)/shard_map/ppermute | solution.py:418
  460.9 6.7 shard_map.275
  474.1 17.8 %collective-permute-done.62 = bf16[256,2048]{1,0:T(8,128)(2,1)S(1)} collective-permute-done((bf16[256,2048]{1,0:T(8,128)(2,1)S(1)}, bf16[256,2048]{1,0:T(8,128)(2,1)S(1)}, u32[]{:S(2)}, u32[]{:S(2)}) %collective-permute-start.62) | collective-permute-done | bytes 1048608 | tf_op jit(solution)/shard_map/ppermute | solution.py:418
  517.1 7.7 %convolution_convert_fusion.4 = bf16[2048,384]{0,1:T(8,128)(2,1)S(1)} fusion(bf16[2048,2048]{1,0:T(8,128)(2,1)} %copy-done.46, bf16[2048,384]{1,0:T(8,128)(2,1)S(1)} %copy-done.40), kind=kOutput, calls=%fused_computation.47 | convolution fusion | flops 3222011904 | bytes 11534336 | tf_op jit(solution)/shard_map/dot_general | solution.py:44
  524.8 11.5 %multiply_convert_fusion.3 = (bf16[2048,384]{1,0:T(8,128)(2,1)S(1)}, f32[2048,384]{1,0:T(8,128)}) fusion(f32[2048,384]{1,0:T(8,128)S(1)} %copy-done.29, f32[2048,384]{1,0:T(8,128)S(1)} %copy-done.25, bf16[2048,2048]{1,0:T(8,128)(2,1)} %copy-done.46, bf16[2048,768]{1,0:T(8,128)(2,1)S(1)} %copy-done.22), kind=kOutput, calls=%fused_computation.44 | convolution fusion | flops 3236167680 | bytes 20971520 | tf_op jit(solution)/shard_map/dot_general | solution.py:40
  561.7 10.0 %shard_map.277 = (f32[2048,384]{1,0:T(8,128)S(1)}, f32[2048,384]{1,0:T(8,128)}, f32[32,384]{1,0:T(8,128)S(1)}) custom-call(s32[1]{0:T(128)} %bitcast.core_ref, f32[2048,384]{1,0:T(8,128)} %get-tuple-element.119.decay_ref, f32[2048,384]{1,0:T(8,128)} %get-tuple-element.242.grad_ref, f32[2048,384]{1,0:T(8,128)} %copy-done.28), custom_call_target="tpu_custom_call" | custom-call | tf_op jit(solution)/shard_map/pallas_call | solution.py:397
  593.9 20.8 %shard_map.278 = (bf16[2048,512]{1,0:T(8,128)(2,1)S(1)}, f32[64,512]{1,0:T(8,128)S(1)}, f32[32,512]{1,0:T(8,128)S(1)}, f32[256,512]{1,0:T(8,128)S(1)}, f32[256,256]{1,0:T(8,128)S(1)}, /*index=5*/f32[8,512]{1,0:T(8,128)S(1)}) custom-call(s32[1]{0:T(128)} %bitcast.core_ref, bf16[2048,512]{1,0:T(8,128)(2,1)} %copy-done, bf16[2048,512]{1,0:T(8,128)(2,1)} %copy-done, ...), custom_call_target="tpu_custom_call" | custom-call | tf_op jit(solution)/shard_map/pallas_call | solution.py:397
  633.8 9.7 %convolution_convert_fusion.2 = bf16[2048,512]{1,0:T(8,128)(2,1)} fusion(bf16[2048,2048]{1,0:T(8,128)(2,1)} %shard_map.271, bf16[2048,512]{1,0:T(8,128)(2,1)S(1)} %bitcast.223), kind=kOutput, calls=%fused_computation.45 | convolution fusion | flops 4296015872 | bytes 12582912 | tf_op jit(solution)/shard_map/dot_general | solution.py:44
  706.0 16.3 %all-to-all-done.3 = bf16[8,80,640]{2,1,0:T(8,128)(2,1)} async-done(((bf16[8,80,640]{2,1,0:T(8,128)(2,1)}), bf16[8,80,640]{2,1,0:T(8,128)(2,1)}, u32[]{:S(2)}, u32[]{:S(2)}) %all-to-all-start.3) | async-done | bytes 819232 | tf_op jit(solution)/shard_map/all_to_all | solution.py:506
  752.2 6.3 all-to-all-done.7
  (630 shorter events, 361.6 us)
Async XLA Ops:
  7.2 151.4 %all-gather.5.cloned.1.call-start = ((), (), s32[]{:S(2)}) async-start(), calls=%async_computation.13 | async-start | bytes 2621440 | tf_op jit(solution)/shard_map/all_gather | solution.py:516
  24.7 187.4 %all-gather.7.cloned.1.call-start = ((), (), s32[]{:S(2)}) async-start(), calls=%async_computation.14 | async-start | bytes 3932160 | tf_op jit(solution)/shard_map/all_gather | solution.py:516
  67.3 253.8 %all-gather.9.cloned.1.call-start = ((), (), s32[]{:S(2)}) async-start(), calls=%async_computation.15 | async-start | bytes 7864320 | tf_op jit(solution)/shard_map/all_gather | solution.py:516
  107.6 248.0 %all-gather.11.cloned.1.call-start = ((), (), s32[]{:S(2)}) async-start(), calls=%async_computation.16 | async-start | bytes 3932160 | tf_op jit(solution)/shard_map/all_gather | solution.py:516
  109.4 37.0 %collective-permute-start.12 = (bf16[256,2048]{1,0:T(8,128)(2,1)S(1)}, bf16[256,2048]{1,0:T(8,128)(2,1)}, u32[]{:S(2)}, u32[]{:S(2)}) collective-permute-start(bf16[256,2048]{1,0:T(8,128)(2,1)S(1)} %bitcast.218), channel_id=1, source_target_pairs={{0,1},{1,0},{2,3},{3,2},{4,5},{5,4},{6,7},{7,6},{8,9},{9,8},{10,11... | collective-permute-start | bytes 3145736 | tf_op jit(solution)/shard_map/ppermute | solution.py:421
  156.9 47.0 %collective-permute-start.38 = (bf16[256,2048]{1,0:T(8,128)(2,1)}, bf16[256,2048]{1,0:T(8,128)(2,1)}, u32[]{:S(2)}, u32[]{:S(2)}) collective-permute-start(bf16[256,2048]{1,0:T(8,128)(2,1)} %bitcast.35.cot_ref), channel_id=1, source_target_pairs={{0,8},{8,0},{16,24},{24,16},{1,9},{9,1},{17,25},{25,17},{2,10},{10... | collective-permute-start | bytes 3145736 | tf_op jit(solution)/shard_map/ppermute | solution.py:418
  157.7 43.9 %collective-permute-start.39 = (bf16[256,2048]{1,0:T(8,128)(2,1)}, bf16[256,2048]{1,0:T(8,128)(2,1)}, u32[]{:S(2)}, u32[]{:S(2)}) collective-permute-start(bf16[256,2048]{1,0:T(8,128)(2,1)} %bitcast.35.cot_ref), channel_id=1, source_target_pairs={{0,16},{8,24},{16,0},{24,8},{1,17},{9,25},{17,1},{25,9},{2,18},{10... | collective-permute-start | bytes 3145736 | tf_op jit(solution)/shard_map/ppermute | solution.py:418
  173.6 246.7 %reduce-scatter.6.cloned.1.call-start = ((), (), s32[]{:S(2)}) async-start(), calls=%async_computation.17 | async-start | bytes 3932160 | tf_op jit(solution)/shard_map/reduce_scatter | solution.py:513
  187.6 32.2 %collective-permute-start.19 = (f32[4,2,384]{2,1,0:T(2,128)S(1)}, f32[4,2,384]{2,1,0:T(2,128)S(1)}, u32[]{:S(2)}, u32[]{:S(2)}) collective-permute-start(f32[4,2,384]{2,1,0:T(2,128)S(1)} %slice.785), channel_id=1, source_target_pairs={{0,6},{1,7},{8,14},{9,15},{16,22},{17,23},{24,30},{25,31}} | collective-permute-start | bytes 36872 | tf_op jit(solution)/shard_map/ppermute | solution.py:621
  219.8 55.4 %collective-permute-start.42 = (bf16[256,2048]{1,0:T(8,128)(2,1)}, bf16[256,2048]{1,0:T(8,128)(2,1)}, u32[]{:S(2)}, u32[]{:S(2)}) collective-permute-start(bf16[256,2048]{1,0:T(8,128)(2,1)} %bitcast.35.cot_ref), channel_id=1, source_target_pairs={{0,1},{1,0},{2,3},{3,2},{4,5},{5,4},{6,7},{7,6},{8,9},{9,8},{10,11... | collective-permute-start | bytes 3145736 | tf_op jit(solution)/shard_map/ppermute | solution.py:421
  247.5 31.7 %collective-permute-start.43 = (bf16[256,2048]{1,0:T(8,128)(2,1)}, bf16[256,2048]{1,0:T(8,128)(2,1)S(1)}, u32[]{:S(2)}, u32[]{:S(2)}) collective-permute-start(bf16[256,2048]{1,0:T(8,128)(2,1)} %collective-permute-done.38), channel_id=1, source_target_pairs={{0,1},{1,0},{2,3},{3,2},{4,5},{5,4},{6,7},{7,6},{8,9},{9,8},{10,11... | collective-permute-start | bytes 3145736 | tf_op jit(solution)/shard_map/ppermute | solution.py:421
  275.3 26.0 %collective-permute-start.30 = (bf16[256,2048]{1,0:T(8,128)(2,1)S(1)}, bf16[256,2048]{1,0:T(8,128)(2,1)S(1)}, u32[]{:S(2)}, u32[]{:S(2)}) collective-permute-start(bf16[256,2048]{1,0:T(8,128)(2,1)S(1)} %get-tuple-element.105), channel_id=1, source_target_pairs={{0,8},{8,0},{16,24},{24,16},{1,9},{9,1},{17,25},{25,17},{2,10},{10... | collective-permute-start | bytes 3145736 | tf_op jit(solution)/shard_map/ppermute | solution.py:418
  355.5 186.5 %reduce-scatter.8.cloned.1.call-start = ((), (), s32[]{:S(2)}) async-start(), calls=%async_computation.18 | async-start | bytes 7864320 | tf_op jit(solution)/shard_map/reduce_scatter | solution.py:513
  380.9 36.3 %collective-permute-start.50 = (bf16[256,2048]{1,0:T(8,128)(2,1)S(1)}, bf16[256,2048]{1,0:T(8,128)(2,1)}, u32[]{:S(2)}, u32[]{:S(2)}) collective-permute-start(bf16[256,2048]{1,0:T(8,128)(2,1)S(1)} %convolution_convert_fusion.10), channel_id=1, source_target_pairs={{0,1},{1,0},{2,3},{3,2},{4,5},{5,4},{6,7},{7,6},{8,9},{9,8},{10,11... | collective-permute-start | bytes 3145736 | tf_op jit(solution)/shard_map/ppermute | solution.py:421
  387.1 43.8 %collective-permute-start.47 = (bf16[256,2048]{1,0:T(8,128)(2,1)}, bf16[256,2048]{1,0:T(8,128)(2,1)}, u32[]{:S(2)}, u32[]{:S(2)}) collective-permute-start(bf16[256,2048]{1,0:T(8,128)(2,1)} %convolution_convert_fusion.12), channel_id=1, source_target_pairs={{0,1},{1,0},{2,3},{3,2},{4,5},{5,4},{6,7},{7,6},{8,9},{9,8},{10,11... | collective-permute-start | bytes 3145736 | tf_op jit(solution)/shard_map/ppermute | solution.py:421
  420.4 206.1 %reduce-scatter.10.cloned.1.call-start = ((), (), s32[]{:S(2)}) async-start(), calls=%async_computation.19 | async-start | bytes 3932160 | tf_op jit(solution)/shard_map/reduce_scatter | solution.py:513
  473.0 25.8 %collective-permute-start.56 = (bf16[256,2048]{1,0:T(8,128)(2,1)S(1)}, bf16[256,2048]{1,0:T(8,128)(2,1)S(1)}, u32[]{:S(2)}, u32[]{:S(2)}) collective-permute-start(bf16[256,2048]{1,0:T(8,128)(2,1)S(1)} %convolution_convert_fusion.17), channel_id=1, source_target_pairs={{0,1},{1,0},{2,3},{3,2},{4,5},{5,4},{6,7},{7,6},{8,9},{9,8},{10,11... | collective-permute-start | bytes 3145736 | tf_op jit(solution)/shard_map/ppermute | solution.py:421
  515.8 32.9 %collective-permute-start.72 = (bf16[128,2048]{1,0:T(8,128)(2,1)}, bf16[128,2048]{1,0:T(8,128)(2,1)}, u32[]{:S(2)}, u32[]{:S(2)}) collective-permute-start(bf16[128,2048]{1,0:T(8,128)(2,1)} %get-tuple-element.196), channel_id=1, source_target_pairs={{0,16},{8,24},{16,0},{24,8},{1,17},{9,25},{17,1},{25,9},{2,18},{10... | collective-permute-start | bytes 1572872 | tf_op jit(solution)/shard_map/ppermute | solution.py:418
  548.3 27.0 %collective-permute-start.71 = (bf16[128,2048]{1,0:T(8,128)(2,1)}, bf16[128,2048]{1,0:T(8,128)(2,1)}, u32[]{:S(2)}, u32[]{:S(2)}) collective-permute-start(bf16[128,2048]{1,0:T(8,128)(2,1)} %slice.1210), channel_id=1, source_target_pairs={{0,16},{8,24},{16,0},{24,8},{1,17},{9,25},{17,1},{25,9},{2,18},{10... | collective-permute-start | bytes 1572872 | tf_op jit(solution)/shard_map/ppermute | solution.py:418
  548.3 28.3 %collective-permute-start.58 = (bf16[128,2048]{1,0:T(8,128)(2,1)}, bf16[128,2048]{1,0:T(8,128)(2,1)}, u32[]{:S(2)}, u32[]{:S(2)}) collective-permute-start(bf16[128,2048]{1,0:T(8,128)(2,1)} %slice.1211), channel_id=1, source_target_pairs={{0,8},{8,0},{16,24},{24,16},{1,9},{9,1},{17,25},{25,17},{2,10},{10... | collective-permute-start | bytes 1572872 | tf_op jit(solution)/shard_map/ppermute | solution.py:418
  550.9 32.9 %collective-permute-start.73 = (bf16[128,2048]{1,0:T(8,128)(2,1)}, bf16[128,2048]{1,0:T(8,128)(2,1)}, u32[]{:S(2)}, u32[]{:S(2)}) collective-permute-start(bf16[128,2048]{1,0:T(8,128)(2,1)} %fusion.19), channel_id=1, source_target_pairs={{0,8},{8,0},{16,24},{24,16},{1,9},{9,1},{17,25},{25,17},{2,10},{10... | collective-permute-start | bytes 1572872 | tf_op jit(solution)/shard_map/ppermute | solution.py:418
  558.0 25.7 %collective-permute-start.70 = (bf16[128,2048]{1,0:T(8,128)(2,1)}, bf16[128,2048]{1,0:T(8,128)(2,1)}, u32[]{:S(2)}, u32[]{:S(2)}) collective-permute-start(bf16[128,2048]{1,0:T(8,128)(2,1)} %fusion.20), channel_id=1, source_target_pairs={{0,16},{8,24},{16,0},{24,8},{1,17},{9,25},{17,1},{25,9},{2,18},{10... | collective-permute-start | bytes 1572872 | tf_op jit(solution)/shard_map/ppermute | solution.py:418
  588.3 36.3 %all-to-all-start.5 = ((bf16[8,64,1536]{2,1,0:T(8,128)(2,1)}), bf16[8,64,1536]{2,1,0:T(8,128)(2,1)S(1)}, u32[]{:S(2)}, u32[]{:S(2)}) async-start(bf16[8,64,1536]{2,1,0:T(8,128)(2,1)} %bitcast.262), calls=%async_computation.9 | async-start | bytes 3145728 | tf_op jit(solution)/shard_map/all_to_all | solution.py:506
  629.0 39.7 %all-to-all-start.4 = ((bf16[8,64,768]{2,1,0:T(8,128)(2,1)}), bf16[8,64,768]{2,1,0:T(8,128)(2,1)S(1)}, u32[]{:S(2)}, u32[]{:S(2)}) async-start(bf16[8,64,768]{2,1,0:T(8,128)(2,1)} %bitcast.256), calls=%async_computation.8 | async-start | bytes 1572864 | tf_op jit(solution)/shard_map/all_to_all | solution.py:506
  633.0 40.9 %reduce-scatter.12.cloned.1.call-start = ((), (), s32[]{:S(2)}) async-start(), calls=%async_computation.20 | async-start | bytes 1024000 | tf_op jit(solution)/shard_map/reduce_scatter | solution.py:513
  633.8 111.6 %reduce-scatter.14.cloned.1.call-start = ((), (), s32[]{:S(2)}) async-start(), calls=%async_computation.21 | async-start | bytes 2621440 | tf_op jit(solution)/shard_map/reduce_scatter | solution.py:513
  653.0 30.1 %collective-permute-start.79 = (bf16[256,2048]{1,0:T(8,128)(2,1)}, bf16[256,2048]{1,0:T(8,128)(2,1)}, u32[]{:S(2)}, u32[]{:S(2)}) collective-permute-start(bf16[256,2048]{1,0:T(8,128)(2,1)} %fusion.14), channel_id=1, source_target_pairs={{0,1},{1,0},{2,3},{3,2},{4,5},{5,4},{6,7},{7,6},{8,9},{9,8},{10,11... | collective-permute-start | bytes 3145736 | tf_op jit(solution)/shard_map/ppermute | solution.py:421
  660.4 42.3 %collective-permute-start.78 = (bf16[256,2048]{1,0:T(8,128)(2,1)}, bf16[256,2048]{1,0:T(8,128)(2,1)}, u32[]{:S(2)}, u32[]{:S(2)}) collective-permute-start(bf16[256,2048]{1,0:T(8,128)(2,1)} %fusion.13), channel_id=1, source_target_pairs={{0,1},{1,0},{2,3},{3,2},{4,5},{5,4},{6,7},{7,6},{8,9},{9,8},{10,11... | collective-permute-start | bytes 3145736 | tf_op jit(solution)/shard_map/ppermute | solution.py:421
  682.5 42.2 %collective-permute-start.85 = (bf16[128,2048]{1,0:T(8,128)(2,1)}, bf16[128,2048]{1,0:T(8,128)(2,1)}, u32[]{:S(2)}, u32[]{:S(2)}) collective-permute-start(bf16[128,2048]{1,0:T(8,128)(2,1)} %slice.1208), channel_id=1, source_target_pairs={{0,16},{8,24},{16,0},{24,8},{1,17},{9,25},{17,1},{25,9},{2,18},{10... | collective-permute-start | bytes 1572872 | tf_op jit(solution)/shard_map/ppermute | solution.py:418
  686.1 38.7 %collective-permute-start.80 = (bf16[128,2048]{1,0:T(8,128)(2,1)}, bf16[128,2048]{1,0:T(8,128)(2,1)}, u32[]{:S(2)}, u32[]{:S(2)}) collective-permute-start(bf16[128,2048]{1,0:T(8,128)(2,1)} %slice.1209), channel_id=1, source_target_pairs={{0,8},{8,0},{16,24},{24,16},{1,9},{9,1},{17,25},{25,17},{2,10},{10... | collective-permute-start | bytes 1572872 | tf_op jit(solution)/shard_map/ppermute | solution.py:418
  691.1 33.7 %collective-permute-start.87 = (bf16[128,2048]{1,0:T(8,128)(2,1)}, bf16[128,2048]{1,0:T(8,128)(2,1)}, u32[]{:S(2)}, u32[]{:S(2)}) collective-permute-start(bf16[128,2048]{1,0:T(8,128)(2,1)} %fusion.17), channel_id=1, source_target_pairs={{0,8},{8,0},{16,24},{24,16},{1,9},{9,1},{17,25},{25,17},{2,10},{10... | collective-permute-start | bytes 1572872 | tf_op jit(solution)/shard_map/ppermute | solution.py:418
  694.0 30.7 %collective-permute-start.84 = (bf16[128,2048]{1,0:T(8,128)(2,1)}, bf16[128,2048]{1,0:T(8,128)(2,1)}, u32[]{:S(2)}, u32[]{:S(2)}) collective-permute-start(bf16[128,2048]{1,0:T(8,128)(2,1)} %fusion.18), channel_id=1, source_target_pairs={{0,16},{8,24},{16,0},{24,8},{1,17},{9,25},{17,1},{25,9},{2,18},{10... | collective-permute-start | bytes 1572872 | tf_op jit(solution)/shard_map/ppermute | solution.py:418
  (143 other events, 1814.7 us)
Sparse Core Ops, SparseCore 0:
  24.8 50.6 all-gather.4
  77.2 62.8 all-gather.6
  141.6 114.0 all-gather.8
  257.1 63.9 all-gather.10
  355.6 57.5 reduce-scatter.5
  420.5 107.9 reduce-scatter.7
  542.2 58.7 reduce-scatter.9
  636.2 26.0 reduce-scatter.11
  674.1 46.0 reduce-scatter.13

commit v3 on v2

--- a/solution.py
+++ b/solution.py
@@ -420,30 +420,40 @@
     def twin(self, x):
         return lax.ppermute(x, "core", [(0, 1), (1, 0)])
 
-    def pieces(self, x):
+    def pieces(self, x, late=()):
         half = x.shape[0] // 2
         x1, x2 = self.near(x, 1), self.near(x, 2)
+        if late:
+            x1, x2 = lax.optimization_barrier((x1, x2, *late))[:2]
         x3 = jnp.concatenate([self.near(x2[:half], 1), self.near(x1[half:], 2)], axis=0)
         mine = [x, x1, x2, x3]
         return mine + [self.twin(m) for m in mine]
 
-    def gather(self, x):
-        return jnp.concatenate(self.pieces(x), axis=0)
+    def gather(self, x, late=()):
+        return jnp.concatenate(self.pieces(x, late), axis=0)
 
     def terms(self, product, rows):
         n = self.n_dp
-        order = (3, 1, 2, 0)
-        other = {k: self.twin(product((n + k) * rows, (n + k + 1) * rows).astype(BF)) for k in order}
-        q = {k: product(k * rows, (k + 1) * rows) + other[k].astype(F32) for k in order}
-        return [q[k] for k in range(n)]
-
-    def add_up(self, q):
+        halves = ((n // 2, n), (0, n // 2))
+        other = [self.twin(product((n + lo) * rows, (n + hi) * rows).astype(BF)) for lo, hi in halves]
+        far, near = (product(lo * rows, hi * rows) + x.astype(F32) for (lo, hi), x in zip(halves, other))
+        far = far.astype(BF)
+        return [x[k * rows : (k + 1) * rows] for x in (near, far) for k in range(n // 2)]
+
+    def send_first(self, q):
         half = q[0].shape[0] // 2
         low = lambda x: x.astype(BF)
-        a3, b3 = self.near(low(q[3][:half]), 1), self.near(low(q[3][half:]), 2)
-        a1, b2 = self.near(low(q[1][:half]), 1), self.near(low(q[2][half:]), 2)
-        a = self.near(low(q[2][:half] + a3.astype(F32)), 2)
-        b = self.near(low(q[1][half:] + b3.astype(F32)), 1)
+        a3, b3 = self.near(q[3][:half], 1), self.near(q[3][half:], 2)
+        a1, b2 = self.near(low(q[1][:half]), 1), self.near(q[2][half:], 2)
+        return a3, b3, a1, b2
+
+    def add_up(self, q, first=None, late=()):
+        half = q[0].shape[0] // 2
+        low = lambda x: x.astype(BF)
+        a3, b3, a1, b2 = first or self.send_first(q)
+        q2, q1 = (after(q[2], *late), after(q[1], *late)) if late else (q[2], q[1])
+        self.second = (low(q2[:half].astype(F32) + a3.astype(F32)), low(q1[half:] + b3.astype(F32)))
+        a, b = self.near(self.second[0], 2), self.near(self.second[1], 1)
         return q[0], a1, a, b2, b
 
     def scatter(self, product, rows):
@@ -519,9 +529,6 @@
     cot = cotangent.reshape(rows, width)
     tok = tokens.reshape(rows, width)
     tok_pieces = plane.pieces(tok)
-    sent_in = to_members(window_columns(input_proj))
-    w_in = over_z(sent_in)
-    both = jnp.concatenate([own_columns(branch_proj), own_columns(output_proj.T)], axis=2)
     rrow = rec // devices
     small = jnp.concatenate(
         [
@@ -536,29 +543,38 @@
     small = jnp.concatenate([small, marks])
     small = jnp.pad(small, ((0, -small.shape[0] % 32), (0, 0)))
     packed = small.shape[0]
-    small = over_z(after(small, sent_in))
-    sent_both = to_members(after(both, small, tok_pieces[1], tok_pieces[2]))
-    w_both = over_z(sent_both)
-    w_branch, w_out = w_both[:, :own], w_both[:, own:]
-    small = plane.gather(small).reshape(n_core, n_dp, n_z, packed, 256)
-    keep = lax.dynamic_index_in_dim(small, zi, 2, False)[:, :, marks_at : marks_at + rows // 256]
-    keep = keep.astype(F32).reshape(total_rows, 1)
-    small = jnp.swapaxes(plane.in_order(small), 1, 2).reshape(devices, packed * 256)
-    gates_len = 2 * rrow * block
-    gates_all = small[:, :gates_len].reshape(devices, 2, rrow, block)
-    gates_all = jnp.swapaxes(gates_all, 0, 1).reshape(2, rec, block)
-    rest = small[:, gates_len:small_len].astype(F32)
-    gain = rest[:, :drow].reshape(width)
-    fgain = rest[:, drow : 2 * drow].reshape(width)
+    small = over_z(small)
+    source, small, *near = lax.optimization_barrier((input_proj, small, *tok_pieces[1:3]))
+    sent_in = to_members(window_columns(source))
+
+    def pair(a, b):
+        cut = block + part
+        return jnp.concatenate([a[..., :block], b[..., :block], a[..., block:cut], b[..., block:cut]], axis=-1)
+
+    def unpair(x, k):
+        at = 2 * block + k * part
+        return jnp.concatenate([x[..., k * block : (k + 1) * block], x[..., at : at + part]], axis=-1)
+
+    both = pair(own_columns(branch_proj), own_columns(output_proj.T))
+    sent_both = to_members(after(both, sent_in))
     ff_packed = pl.pallas_call(
         functools.partial(ff_pack_kernel, cuts=(n_dp, n_z, n_core)),
         out_shape=jax.ShapeDtypeStruct((group, drow, 2 * ff_own), BF),
         compiler_params=pltpu.CompilerParams(vmem_limit_bytes=VMEM_BYTES),
     )(ffn_gate, ffn_up)
-    sent_ff = exchange(after(ff_packed.reshape(group * drow, 2 * ff_own), tok_pieces[3], gain))
-    w_ff = over_z(sent_ff)
-    w_down = over_z(after(ffn_down, sent_ff))
-
+    w_in = over_z(sent_in)
+    w_both = over_z(sent_both)
+    w_branch, w_out = (jnp.pad(unpair(w_both, k), ((0, 0), (0, lanes - part))) for k in range(2))
+    small = plane.gather(small).reshape(n_core, n_dp, n_z, packed, 256)
+    keep = lax.dynamic_index_in_dim(small, zi, 2, False)[:, :, marks_at : marks_at + rows // 256]
+    keep = keep.astype(F32).reshape(total_rows, 1)
+    ff_packed, small = lax.optimization_barrier((ff_packed, small))
+    sent_ff = exchange(ff_packed.reshape(group * drow, 2 * ff_own))
+    gates_len = 2 * rrow * block
+    rest = small[:, :, :, gates_len // 256 : marks_at]
+    rest = jnp.swapaxes(plane.in_order(rest), 1, 2).reshape(devices, -1)[:, : small_len - gates_len].astype(F32)
+    gain = rest[:, :drow].reshape(width)
+    fgain = rest[:, drow : 2 * drow].reshape(width)
     chan = rest[:, 2 * drow :].reshape(devices, taps + 4, rrow)
     chan = jnp.swapaxes(chan, 0, 1).reshape(taps + 4, rec)
     lam = chan[taps + 3 :]
@@ -574,12 +590,6 @@
         return full, turned
 
     vec = jnp.concatenate(my_window(chan, 1), axis=1)
-    gw_full, gw_shared = my_window(gates_all, 1)
-    gw_shared = lax.dynamic_slice_in_dim(gw_shared, quarter * part, part, 2)
-    gw_shared = jnp.pad(gw_shared, ((0, 0), (0, 0), (0, lanes - part)))
-    gwf = jnp.concatenate([gw_full[0], gw_full[1]], axis=1)
-    gws = jnp.concatenate([gw_shared[0], gw_shared[1]], axis=1)
-
     mine = OwnRows(rows, width)
     normed = pl.pallas_call(
         functools.partial(norm_kernel, cuts=cuts),
@@ -589,9 +599,21 @@
         out_shape=jax.ShapeDtypeStruct((total_rows, width), BF),
         compiler_params=pltpu.CompilerParams(vmem_limit_bytes=VMEM_BYTES),
     )(gain.reshape(1, width), *tok_pieces)
-    cot_all = plane.gather(after(cot, sent_ff))
-
+
+    normed, small, sent_ff = lax.optimization_barrier((normed, small, sent_ff))
+    gates_all = small[:, :, :, : gates_len // 256].reshape(n_core, n_dp, n_z, 2, rrow * block // 256, 256)
+    gates_all = jnp.transpose(plane.in_order(gates_all), (3, 0, 2, 1, 4, 5)).reshape(2, rec, block)
+    gw_full, gw_shared = my_window(gates_all, 1)
+    gw_shared = lax.dynamic_slice_in_dim(gw_shared, quarter * part, part, 2)
+    gw_shared = jnp.pad(gw_shared, ((0, 0), (0, 0), (0, lanes - part)))
+    gwf = jnp.concatenate([gw_full[0], gw_full[1]], axis=1)
+    gws = jnp.concatenate([gw_shared[0], gw_shared[1]], axis=1)
+
+    w_ff = over_z(sent_ff)
+    w_down = over_z(after(ffn_down, sent_ff))
     inner = dot(normed, w_in).astype(BF)
+    cot_here, inner = lax.optimization_barrier((cot, inner))
+    cot_pieces = plane.pieces(cot_here)
     branch = dot(normed, w_branch)
     ends = inner.reshape(n_core, n_dp, seqs, span, window)[:, :, :, span - HALO :]
     ends = jnp.where(core == 1, ends[0], ends[1]).reshape(lines * HALO, window)
@@ -632,10 +654,13 @@
 
     hidden = (spread(local) + spread(cum) * by_line(start)).reshape(total_rows, own)
     mixed_out = (hidden * gelu_only(branch)).astype(BF)
+    mixed_out, *cot_pieces = lax.optimization_barrier((mixed_out, *cot_pieces))
     terms = plane.scatter(lambda lo, hi: dot_cols(mixed_out[lo:hi], w_out), rows)
     mid, fnormed = mine.call(functools.partial(mid_kernel, cuts=cuts), terms, [tok], fgain, [F32, BF])
 
-    fnormed = plane.gather(fnormed)
+    cot_pieces[0] = after(cot_pieces[0], fnormed)
+    cot_all = jnp.concatenate(cot_pieces, axis=0)
+    fnormed = plane.gather(fnormed, [cot_all])
     pre_lin = dot(fnormed, w_ff)
     act, slope = gelu_pair(pre_lin[:, :ff_own])
     lin = pre_lin[:, ff_own:]
@@ -645,41 +670,37 @@
     fgrad = jnp.concatenate([(hid_grad * lin * slope).astype(BF), (hid_grad * act).astype(BF)], axis=1)
     down_sum = sum_z(down_terms)
     down_out = down_sum.astype(F32)
-    ff_terms = dot_rows(fnormed, fgrad).astype(BF)
-    terms = plane.scatter(lambda lo, hi: dot_cols(fgrad[lo:hi], w_ff), rows)
+    terms = plane.terms(lambda lo, hi: dot_cols(fgrad[lo:hi], w_ff), rows)
+    ff_terms = dot_rows(fnormed, after(fgrad, down_sum, *terms)).astype(BF)
+    terms = plane.add_up(terms)
     ff_sum = sum_z(after(ff_terms, down_sum))
-    ff_part = exchange(ff_sum).reshape(group, drow, 2 * ff_own)
     terms = (after(terms[0], down_sum, ff_terms), *terms[1:])
     mid_grad, mid_low, ffn_gain_part = mine.call(
         functools.partial(mid_back_kernel, cuts=cuts), terms, [mid, cot], fgain, [F32, BF, None]
     )
-    mid_low = plane.gather(mid_low)
     later = after(fhidden, mid_grad)
     out_terms = plane.terms(lambda lo, hi: dot(later[lo:hi], w_down), rows)
-    mid_low = after(mid_low, *out_terms)
+    ffn_gain_part = jnp.sum(ffn_gain_part, axis=0)
+    mid_low = plane.gather(mid_low, [*out_terms, ffn_gain_part, down_out])
     out_terms[3] = after(out_terms[3], mid_low)
-    layer_out = mine.call(out_kernel, plane.add_up(out_terms), [mid], None, [F32])[0]
-
-    gate_out, up_out = pl.pallas_call(
-        functools.partial(ff_unpack_kernel, cuts=(n_dp, n_z, n_core)),
-        out_shape=[jax.ShapeDtypeStruct((drow, ff), F32)] * 2,
-        compiler_params=pltpu.CompilerParams(vmem_limit_bytes=VMEM_BYTES),
-    )(ff_part)
 
     mixed_grad = dot(mid_low, w_out)
     act_r, slope_r = gelu_pair(branch)
     branch_grad = (mixed_grad * hidden * slope_r).astype(BF)
     back = Blocks(n_core, n_dp, seqs, True)
+    out_first = plane.send_first(out_terms)
     adj, prod, front = back.call(
         functools.partial(reverse_kernel, own=own),
         [back.rows(span, own)] * 3,
         [back.rows(span, own)] * 2 + [back.sequence(8, own)],
         [row_f32] * 2 + [jax.ShapeDtypeStruct((lines * 8, own), F32)],
         [pltpu.VMEM((8, own), F32)],
-        core_id, after(decay, ff_sum), mixed_grad, branch,
-    )
-    both = jnp.concatenate([dot_rows(normed, branch_grad).astype(BF), dot_rows(mid_low, mixed_out).astype(BF)], axis=1)
-    suffix = carried(front, -1, [both])
+        core_id, decay, mixed_grad, branch,
+    )
+    branch_late, mixed_late, *out_first = lax.optimization_barrier((branch_grad, mixed_out, *out_first, adj))[:6]
+    out_terms = plane.add_up(out_terms, out_first)
+    both = pair(dot_rows(normed, branch_late).astype(BF), dot_rows(mid_low, mixed_late).astype(BF))
+    suffix, ff_sum, *out_terms = lax.optimization_barrier((carried(front, -1, [both]), ff_sum, *out_terms))
 
     def eight(x):
         return jnp.broadcast_to(x[:, None, :], (lines, 8, own)).reshape(lines * 8, own)
@@ -714,22 +735,35 @@
     igrad = lax.dynamic_update_slice(
         igrad.reshape(n_core, n_dp, seqs, span, window), tail, (1 - core, 0, 0, span - HALO, 0)
     ).reshape(total_rows, window)
+    ff_part = exchange(ff_sum)
     both_sum = sum_z(after(both, ff_sum))
-    igrad = after(igrad, layer_out, both_sum)
     in_terms = dot_rows(normed, igrad).astype(BF)
-    igrad = after(igrad, in_terms)
-    terms = plane.scatter(
+    both_part = exchange(both_sum)
+    igrad, in_terms, ff_part = lax.optimization_barrier((igrad, in_terms, ff_part))
+    layer_out = mine.call(out_kernel, out_terms, [mid], None, [F32])[0]
+    gate_out, up_out = pl.pallas_call(
+        functools.partial(ff_unpack_kernel, cuts=(n_dp, n_z, n_core)),
+        out_shape=[jax.ShapeDtypeStruct((drow, ff), F32)] * 2,
+        compiler_params=pltpu.CompilerParams(vmem_limit_bytes=VMEM_BYTES),
+    )(ff_part.reshape(group, drow, 2 * ff_own))
+    terms = plane.terms(
         lambda lo, hi: dot_cols(igrad[lo:hi], w_in) + dot_cols(branch_grad[lo:hi], w_branch), rows
     )
-    both_part = exchange(both_sum).reshape(group, drow, 2 * own)
+    terms = plane.add_up(terms)
+    second = plane.second
+    first_terms, layer_out, gate_out, up_out, both_part = lax.optimization_barrier(
+        (terms[0], layer_out, gate_out, up_out, both_part)
+    )
+    terms = (first_terms, *terms[1:])
+    both_part = both_part.reshape(group, drow, 2 * (block + part))
 
     def own_natural(x):
         full = jnp.swapaxes(x[:, :, :block], 0, 1).reshape(drow, group * block)
         rest = jnp.swapaxes(x[:, :, block : block + part], 0, 1).reshape(drow, group * part)
         return jnp.concatenate([full, rest], axis=1).astype(F32)
 
-    branch_proj_grad = own_natural(both_part[:, :, :own])
-    output_proj_grad = own_natural(both_part[:, :, own:]).T
+    branch_proj_grad = own_natural(unpair(both_part, 0))
+    output_proj_grad = own_natural(unpair(both_part, 1)).T
 
     def place_window(x, axis_len):
         lead = x.shape[:-1]
@@ -764,13 +798,18 @@
 
     assert lots <= n_z
     gates = jnp.concatenate([by_z(dg_full, me * block), by_z(dg_shared, shared_at)], axis=2)
-    gates = sum_z(after(gates.reshape(n_z * lot, 2 * (block + part)), both_sum))
-    in_part = exchange(sum_z(after(in_terms, gates))).reshape(group, drow, window)
+    gates = gates.reshape(n_z, lot * 2 * (block + part) // window, window)
+    joined = jnp.concatenate([in_terms.reshape(n_z, group * drow, window), gates], axis=1)
+    joined = sum_z(after(joined.reshape(-1, window), both_sum))
+    joined, first_terms = lax.optimization_barrier((joined, terms[0], *second))[:2]
+    terms = (first_terms, *terms[1:])
+    in_part = joined[: group * drow].reshape(group, drow, window)
+    gates = joined[group * drow :].reshape(lot, 2 * (block + part))
     gates = jnp.concatenate(
         [to_lines(gates[:, : 2 * block], me * block), to_lines(gates[:, 2 * block :], shared_at)], axis=2
     )
-    gates = exchange(gates.reshape(group * rrow, 2 * (block + part))).reshape(group, rrow, 2 * (block + part)).astype(F32)
-    terms = (after(terms[0], gates, both_part, gate_out, up_out), *terms[1:])
+    gates = gates.reshape(group, rrow * 2 * (block + part) // window, window)
+    joined = exchange(jnp.concatenate([in_part, gates], axis=1).reshape(-1, window))
     input_grad, gain_part = mine.call(
         functools.partial(tok_back_kernel, cuts=cuts), terms, [tok, mid_grad], gain, [F32, None]
     )
@@ -782,13 +821,17 @@
     sums = jnp.concatenate([sums[:7], sums[7:8] * (POWER * jax.nn.sigmoid(-lam))], axis=0)
     vectors = jnp.concatenate(
         [
-            jnp.sum(gain_part, axis=0).reshape(devices, drow), jnp.sum(ffn_gain_part, axis=0).reshape(devices, drow),
+            jnp.sum(gain_part, axis=0).reshape(devices, drow), ffn_gain_part.reshape(devices, drow),
             jnp.swapaxes(sums.reshape(8, devices, rrow), 0, 1).reshape(devices, 8 * rrow),
         ],
         axis=1,
     )
     vec_len = vectors.shape[1]
+    vectors, joined = lax.optimization_barrier((vectors, joined))
     vectors = lax.all_to_all(vectors, EVERY, split_axis=0, concat_axis=0, tiled=True)
+    joined = joined.reshape(group, -1, window)
+    in_part = joined[:, :drow]
+    gates = joined[:, drow:].reshape(group, rrow, 2 * (block + part)).astype(F32)
     vectors = jnp.sum(vectors.reshape(devices, vec_len), axis=0)
     gain_out = vectors[:drow]
     fgain_out = vectors[drow : 2 * drow]

time: 774 us -> 740 us (0.956)
  blocking collectives: 75.1 us -> 27.5 us
  local copies, waits for them, and re-layouts: 90.7 us -> 136 us
  matrix products: 210 us -> 178 us
  waiting for transfers between devices: 167 us -> 136 us
  starting transfers between devices: 94.5 us -> 109 us
  other arithmetic: 37.4 us -> 49.6 us
    ppermute x44, waiting for transfers between devices: 132 us -> 88.4 us  [near(): return lax.ppermute(x, 'dp', [(i, i ^ k) for i in range(self.n_dp)])]
    all_to_all x3 -> x1, blocking collectives: 55 us -> 13 us  [exchange(): return lax.all_to_all(x, GROUP, split_axis=0, concat_axis=0, tiled=True)]
    dot_general x33 -> x17, matrix products: 104 us -> 70.3 us  [dot_cols(): lax.dot_general(a, b, (((1,), (1,)), ((), ())), preferred_element_type=F32)]
    slice x14 -> x26, local copies, waits for them, and re-layouts: 10.9 us -> 27 us  [the longest x6 7.91 us: terms(): x[k * rows:(k + 1) * rows]]
    ppermute x44, starting transfers between devices: 41.2 us -> 54.1 us  [near(): return lax.ppermute(x, 'dp', [(i, i ^ k) for i in range(self.n_dp)])]
    concatenate x1 -> x6, other arithmetic: 1.92 us -> 13.9 us  [the longest x1 3.78 us: body(): jnp.concatenate([(hid_grad * lin * slope).astype(BF), (hid_grad * act).as...]
    all_to_all x4 -> x5, waiting for transfers between devices: 22.6 us -> 32.1 us  [exchange(): return lax.all_to_all(x, GROUP, split_axis=0, concat_axis=0, tiled=True)]
    unnamed x188 -> x253, local copies, waits for them, and re-layouts: 42.8 us -> 51.9 us
  transfers between devices with their start and end apart: 102 -> 94, of which waited for: 28 -> 29; matrix products, arithmetic and copies ran while one was open for 41% -> 45% of each run, Pallas kernels for 10% -> 10%
where the time goes in v3:
time: 740 us; the launch traced here: 729 us
  matrix products  178 us (24%)
  local copies, waits for them, and re-layouts  136 us (18%)
  waiting for transfers between devices  136 us (18%)
  starting transfers between devices  109 us (15%)
  Pallas kernels  76 us (10%)
  other arithmetic  49.6 us (7%)
  blocking collectives  27.5 us (4%)
  between operations  16.8 us (2%)
    ppermute x44, waiting for transfers between devices, near(): return lax.ppermute(x, 'dp', [(i, i ^ k) for i in range(self.n_dp)])  88.4 us
    dot_general x17, matrix products, dot_cols(): lax.dot_general(a, b, (((1,), (1,)), ((), ())), preferred_element_type=F32)  70.3 us
    dot_general x8, matrix products, dot(): lax.dot_general(a, b, (((1,), (0,)), ((), ())), preferred_element_type=F32)  56.6 us
    ppermute x44, starting transfers between devices, near(): return lax.ppermute(x, 'dp', [(i, i ^ k) for i in range(self.n_dp)])  54.1 us
    unnamed x253, local copies, waits for them, and re-layouts  51.9 us
    dot_general x5, matrix products, dot_rows(): lax.dot_general(a, b, (((0,), (0,)), ((), ())), preferred_element_type=F32)  51 us
    pallas_call x3, Pallas kernels, call(): pl.pallas_call(kernel, grid_spec=pltpu.PrefetchScalarGridSpec(num_scalar_...  43 us
    all_to_all x5, waiting for transfers between devices, exchange(): return lax.all_to_all(x, GROUP, split_axis=0, concat_axis=0, tiled=True)  32.1 us
  transfers between devices with their start and end apart: 94, of which 29 were waited for; matrix products, arithmetic and copies ran while one was open for 45% of the time, Pallas kernels for 10%

profile of v3, /device:TPU:0, one launch (start us, length us, event | category | flops | bytes accessed | tf_op | source)
XLA Modules:
  0.0 728.6 jit_solution(497058366041942613)
XLA Ops:
  17.8 14.5 %all_gather.15 = bf16[768,256]{1,0:T(8,128)(2,1)S(1)} all-gather(bf16[192,256]{1,0:T(8,128)(2,1)S(1)} %fusion.78), channel_id=1, replica_groups=mesh['dp'=4,'z'=4,'core'=2] {'z'}, dimensions={0}, use_global_device_ids=true | all-gather | bytes 491520 | tf_op jit(solution)/shard_map/all_gather | solution.py:526
  37.7 13.0 %all_to_all.69 = bf16[8,64,512]{2,1,0:T(8,128)(2,1)} all-to-all(bf16[8,64,512]{2,1,0:T(8,128)(2,1)S(1)} %copy.127), channel_id=1, replica_groups=mesh['dp'=4,'z'=4,'core'=2] {'dp','core'}, dimensions={0} | all-to-all | bytes 1048576 | tf_op jit(solution)/shard_map/all_to_all | solution.py:516
  111.8 9.0 %shard_map.272 = bf16[2048,2048]{1,0:T(8,128)(2,1)} custom-call(f32[1,2048]{1,0:T(1,128)S(1)} %reshape_reshape.15.gain_ref, bf16[256,2048]{1,0:T(8,128)(2,1)S(1)} %bitcast.223, bf16[256,2048]{1,0:T(8,128)(2,1)S(1)} %collective-permute-done.refs_1_, bf16[256,2048]{1,0:T(8,128)(2,1)} %collective-permute-done.1.refs_2_, ...), custom_call_target="tpu_custom_call" | custom-call | tf_op jit(solution)/shard_map/pallas_call | solution.py:594
  120.8 8.6 %all-to-all-done = bf16[8,64,1536]{2,1,0:T(8,128)(2,1)} async-done(((bf16[8,64,1536]{2,1,0:T(8,128)(2,1)}), bf16[8,64,1536]{2,1,0:T(8,128)(2,1)}, u32[]{:S(2)}, u32[]{:S(2)}) %all-to-all-start) | async-done | bytes 1572896 | tf_op jit(solution)/shard_map/all_to_all | solution.py:516
  134.7 8.7 %convolution_convert_fusion.9.inner_ref.prev_ref = bf16[2048,512]{1,0:T(8,128)(2,1)S(1)} fusion(bf16[2048,2048]{1,0:T(8,128)(2,1)} %shard_map.272, bf16[2048,512]{1,0:T(8,128)(2,1)} %all-gather.5.cloned.1.call-done), kind=kOutput, calls=%fused_computation.57 | convolution fusion | flops 4296015872 | bytes 12582912 | tf_op jit(solution)/shard_map/dot_general | solution.py:40
  151.4 12.5 %shard_map.273 = (f32[2048,384]{1,0:T(8,128)}, f32[2048,384]{1,0:T(8,128)}, f32[2048,384]{1,0:T(8,128)}, f32[32,384]{1,0:T(8,128)S(1)}) custom-call(s32[1]{0:T(128)} %bitcast.core_ref, bf16[2048,512]{1,0:T(8,128)(2,1)S(1)} %convolution_convert_fusion.9.inner_ref.prev_ref, bf16[2048,512]{1,0:T(8,128)(2,1)S(1)} %convolution_convert_fusion.9.inner_ref.prev_ref, ...), custom_call_target="tpu_custom_call" | custom-call | tf_op jit(solution)/shard_map/pallas_call | solution.py:397
  163.9 6.3 collective-permute-start.19
  190.6 7.0 fusion.110.branch_ref
  215.2 8.4 %collective-permute-done.34 = bf16[128,2048]{1,0:T(8,128)(2,1)S(1)} collective-permute-done((bf16[128,2048]{1,0:T(8,128)(2,1)S(1)}, bf16[128,2048]{1,0:T(8,128)(2,1)S(1)}, u32[]{:S(2)}, u32[]{:S(2)}) %collective-permute-start.34) | collective-permute-done | bytes 524320 | tf_op jit(solution)/shard_map/ppermute | solution.py:418
  236.6 10.4 %collective-permute-done.35.b = bf16[128,2048]{1,0:T(8,128)(2,1)} collective-permute-done((bf16[128,2048]{1,0:T(8,128)(2,1)}, bf16[128,2048]{1,0:T(8,128)(2,1)}, u32[]{:S(2)}, u32[]{:S(2)}) %collective-permute-start.35) | collective-permute-done | bytes 524320 | tf_op jit(solution)/shard_map/ppermute | solution.py:418
  255.3 20.7 %collective-permute-done.36 = bf16[256,2048]{1,0:T(8,128)(2,1)S(1)} collective-permute-done((bf16[256,2048]{1,0:T(8,128)(2,1)S(1)}, bf16[256,2048]{1,0:T(8,128)(2,1)S(1)}, u32[]{:S(2)}, u32[]{:S(2)}) %collective-permute-start.36) | collective-permute-done | bytes 1048608 | tf_op jit(solution)/shard_map/ppermute | solution.py:418
  282.4 5.9 collective-permute-done.38
  295.9 17.7 %fusion.128 = f32[2048,1536]{0,1:T(8,128)S(1)} fusion(bf16[2048,2048]{1,0:T(8,128)(2,1)} %constant_dynamic-update-slice_fusion.21, bf16[2048,1536]{1,0:T(8,128)(2,1)} %all-gather.9.cloned.1.call-done), kind=kOutput, calls=%fused_computation.299 | convolution fusion | flops 12884901888 | bytes 27262976 | tf_op jit(solution)/shard_map/dot_general | solution.py:40
  319.8 10.3 %convolution_convert_fusion.1 = bf16[768,2048]{1,0:T(8,128)(2,1)} fusion(bf16[2048,768]{0,1:T(8,128)(2,1)S(1)} %multiply_convert_fusion.2, bf16[2048,2048]{1,0:T(8,128)(2,1)} %copy-done.87), kind=kOutput, calls=%fused_computation.33 | convolution fusion | flops 6444023808 | bytes 14680064 | tf_op jit(solution)/shard_map/dot_general | solution.py:44
  331.8 17.5 %multiply_convert_fusion = (bf16[2048,768]{0,1:T(8,128)(2,1)S(1)}, bf16[2048,768]{0,1:T(8,128)(2,1)S(1)}) fusion(f32[2048,1536]{0,1:T(8,128)} %copy-done.38, bf16[2048,2048]{1,0:T(8,128)(2,1)} %copy-done.87, bf16[768,2048]{1,0:T(8,128)(2,1)} %all-gather.11.cloned.1.call-done), kind=kOutput, calls=%fused_computation.13 | convolution fusion | flops 6477053952 | bytes 30408704 | tf_op jit(solution)/shard_map/dot_general | solution.py:48
  349.3 7.6 %convolution_convert_fusion.6 = bf16[512,2048]{1,0:T(8,128)(2,1)} fusion(bf16[2048,1536]{1,0:T(8,128)(2,1)} %all-gather.9.cloned.1.call-done, bf16[2048,768]{0,1:T(8,128)(2,1)S(1)} %get-tuple-element.286, bf16[2048,768]{0,1:T(8,128)(2,1)S(1)} %get-tuple-element.285), kind=kOutput, calls=%fused_computation.54 | convolution fusion | flops 3225419776 | bytes 14680064 | tf_op jit(solution)/shard_map/dot_general | solution.py:48
  356.9 6.9 convolution_convert_fusion.5
  368.2 7.0 convert_add_fusion.2
  378.8 7.0 add_convert_fusion.4
  392.9 19.2 %convolution_convert_fusion = bf16[2048,1536]{1,0:T(8,128)(2,1)} fusion(bf16[2048,2048]{1,0:T(8,128)(2,1)} %constant_dynamic-update-slice_fusion.21, bf16[2048,1536]{0,1:T(8,128)(2,1)} %pad_maximum_fusion), kind=kOutput, calls=%fused_computation.10 | convolution fusion | flops 12888047616 | bytes 20971520 | tf_op jit(solution)/shard_map/dot_general | solution.py:44
  418.1 9.1 %collective-permute-done.51.b = bf16[128,2048]{1,0:T(8,128)(2,1)S(1)} collective-permute-done((bf16[128,2048]{1,0:T(8,128)(2,1)S(1)}, bf16[128,2048]{1,0:T(8,128)(2,1)S(1)}, u32[]{:S(2)}, u32[]{:S(2)}) %collective-permute-start.51) | collective-permute-done | bytes 524320 | tf_op jit(solution)/shard_map/ppermute | solution.py:418
  429.8 6.4 shard_map.275
  459.6 10.6 %collective-permute-done.52 = bf16[256,2048]{1,0:T(8,128)(2,1)} collective-permute-done((bf16[256,2048]{1,0:T(8,128)(2,1)}, bf16[256,2048]{1,0:T(8,128)(2,1)}, u32[]{:S(2)}, u32[]{:S(2)}) %collective-permute-start.52) | collective-permute-done | bytes 1048608 | tf_op jit(solution)/shard_map/ppermute | solution.py:418
  493.5 7.6 %multiply_convert_fusion.3 = (bf16[2048,384]{1,0:T(8,128)(2,1)}, f32[2048,384]{1,0:T(8,128)}) fusion(f32[2048,384]{1,0:T(8,128)S(1)} %copy-done.40, f32[2048,384]{1,0:T(8,128)S(1)} %copy-done.36, bf16[2048,2048]{1,0:T(8,128)(2,1)S(1)} %constant_dynamic-update-slice_fusion.30, bf16[2048,64]{1,0:T(8,128)(2,1)S(1)} %copy-done.83, ...), kind=kOutput, calls=%fused_computation.49 | convolution fusion | flops 3241672704 | bytes 20709376 | tf_op jit(solution)/shard_map/dot_general | solution.py:40
  501.1 10.1 %shard_map.276 = (f32[2048,384]{1,0:T(8,128)S(1)}, f32[2048,384]{1,0:T(8,128)}, f32[32,384]{1,0:T(8,128)S(1)}) custom-call(s32[1]{0:T(128)} %bitcast.core_ref, f32[2048,384]{1,0:T(8,128)} %get-tuple-element.151.decay_ref, f32[2048,384]{1,0:T(8,128)} %get-tuple-element.343.grad_ref, f32[2048,384]{1,0:T(8,128)} %copy-done.39), custom_call_target="tpu_custom_call" | custom-call | tf_op jit(solution)/shard_map/pallas_call | solution.py:397
  522.8 7.8 %convolution_convert_fusion.11 = bf16[2048,384]{0,1:T(8,128)(2,1)S(1)} fusion(bf16[2048,2048]{1,0:T(8,128)(2,1)} %shard_map.272, bf16[2048,384]{1,0:T(8,128)(2,1)S(1)} %copy-done.88), kind=kOutput, calls=%fused_computation.60 | convolution fusion | flops 3222011904 | bytes 11534336 | tf_op jit(solution)/shard_map/dot_general | solution.py:44
  544.3 20.4 %shard_map.277 = (bf16[2048,512]{1,0:T(8,128)(2,1)S(1)}, f32[64,512]{1,0:T(8,128)S(1)}, f32[32,512]{1,0:T(8,128)S(1)}, f32[256,512]{1,0:T(8,128)S(1)}, f32[256,256]{1,0:T(8,128)S(1)}, /*index=5*/f32[8,512]{1,0:T(8,128)S(1)}) custom-call(s32[1]{0:T(128)} %bitcast.core_ref, bf16[2048,512]{1,0:T(8,128)(2,1)} %copy-done, bf16[2048,512]{1,0:T(8,128)(2,1)} %copy-done, ...), custom_call_target="tpu_custom_call" | custom-call | tf_op jit(solution)/shard_map/pallas_call | solution.py:397
  578.9 9.9 %convolution_convert_fusion.2 = bf16[2048,512]{1,0:T(8,128)(2,1)} fusion(bf16[2048,2048]{1,0:T(8,128)(2,1)} %shard_map.272, bf16[2048,512]{1,0:T(8,128)(2,1)} %bitcast.227), kind=kOutput, calls=%fused_computation.50 | convolution fusion | flops 4296015872 | bytes 12582912 | tf_op jit(solution)/shard_map/dot_general | solution.py:44
  588.8 6.7 all-to-all-done.3
  651.1 12.2 %all-to-all-done.4 = bf16[8,64,640]{2,1,0:T(8,128)(2,1)} async-done(((bf16[8,64,640]{2,1,0:T(8,128)(2,1)}), bf16[8,64,640]{2,1,0:T(8,128)(2,1)}, u32[]{:S(2)}, u32[]{:S(2)}) %all-to-all-start.4) | async-done | bytes 655392 | tf_op jit(solution)/shard_map/all_to_all | solution.py:516
  703.3 7.9 %all-to-all-start.6 = ((f32[32,1,768]{2,1,0:T(1,128)}), f32[32,1,768]{2,1,0:T(1,128)S(1)}, u32[]{:S(2)}, u32[]{:S(2)}) async-start(f32[32,1,768]{2,1,0:T(1,128)} %copy.143), calls=%async_computation.10 | async-start | bytes 196608 | tf_op jit(solution)/shard_map/all_to_all | solution.py:831
  712.1 6.9 all-to-all-done.6
  (680 shorter events, 378.1 us)
Async XLA Ops:
  7.2 127.5 %all-gather.5.cloned.1.call-start = ((), (), s32[]{:S(2)}) async-start(), calls=%async_computation.11 | async-start | bytes 2621440 | tf_op jit(solution)/shard_map/all_gather | solution.py:526
  7.2 26.4 %collective-permute-start = (bf16[256,2048]{1,0:T(8,128)(2,1)}, bf16[256,2048]{1,0:T(8,128)(2,1)S(1)}, u32[]{:S(2)}, u32[]{:S(2)}) collective-permute-start(bf16[256,2048]{1,0:T(8,128)(2,1)} %bitcast.220), channel_id=1, source_target_pairs={{0,8},{8,0},{16,24},{24,16},{1,9},{9,1},{17,25},{25,17},{2,10},{10... | collective-permute-start | bytes 3145736 | tf_op jit(solution)/shard_map/ppermute | solution.py:418
  10.2 24.9 %collective-permute-start.1 = (bf16[256,2048]{1,0:T(8,128)(2,1)}, bf16[256,2048]{1,0:T(8,128)(2,1)}, u32[]{:S(2)}, u32[]{:S(2)}) collective-permute-start(bf16[256,2048]{1,0:T(8,128)(2,1)} %bitcast.221), channel_id=1, source_target_pairs={{0,16},{8,24},{16,0},{24,8},{1,17},{9,25},{17,1},{25,9},{2,18},{10... | collective-permute-start | bytes 3145736 | tf_op jit(solution)/shard_map/ppermute | solution.py:418
  50.7 26.4 %collective-permute-start.3 = (bf16[768,256]{1,0:T(8,128)(2,1)S(1)}, bf16[768,256]{1,0:T(8,128)(2,1)}, u32[]{:S(2)}, u32[]{:S(2)}) collective-permute-start(bf16[768,256]{1,0:T(8,128)(2,1)S(1)} %all_gather.15), channel_id=1, source_target_pairs={{0,16},{8,24},{16,0},{24,8},{1,17},{9,25},{17,1},{25,9},{2,18},{10... | collective-permute-start | bytes 1179656 | tf_op jit(solution)/shard_map/ppermute | solution.py:418
  51.3 27.7 %collective-permute-start.2 = (bf16[768,256]{1,0:T(8,128)(2,1)S(1)}, bf16[768,256]{1,0:T(8,128)(2,1)}, u32[]{:S(2)}, u32[]{:S(2)}) collective-permute-start(bf16[768,256]{1,0:T(8,128)(2,1)S(1)} %all_gather.15), channel_id=1, source_target_pairs={{0,8},{8,0},{16,24},{24,16},{1,9},{9,1},{17,25},{25,17},{2,10},{10... | collective-permute-start | bytes 1179656 | tf_op jit(solution)/shard_map/ppermute | solution.py:418
  53.8 32.1 %collective-permute-start.10 = (bf16[128,2048]{1,0:T(8,128)(2,1)}, bf16[128,2048]{1,0:T(8,128)(2,1)}, u32[]{:S(2)}, u32[]{:S(2)}) collective-permute-start(bf16[128,2048]{1,0:T(8,128)(2,1)} %slice.763), channel_id=1, source_target_pairs={{0,8},{8,0},{16,24},{24,16},{1,9},{9,1},{17,25},{25,17},{2,10},{10... | collective-permute-start | bytes 1572872 | tf_op jit(solution)/shard_map/ppermute | solution.py:418
  55.2 55.9 %collective-permute-start.12 = (bf16[256,2048]{1,0:T(8,128)(2,1)S(1)}, bf16[256,2048]{1,0:T(8,128)(2,1)}, u32[]{:S(2)}, u32[]{:S(2)}) collective-permute-start(bf16[256,2048]{1,0:T(8,128)(2,1)S(1)} %bitcast.222), channel_id=1, source_target_pairs={{0,1},{1,0},{2,3},{3,2},{4,5},{5,4},{6,7},{7,6},{8,9},{9,8},{10,11... | collective-permute-start | bytes 3145736 | tf_op jit(solution)/shard_map/ppermute | solution.py:421
  76.3 100.3 %all-gather.7.cloned.1.call-start = ((), (), s32[]{:S(2)}) async-start(), calls=%async_computation.12 | async-start | bytes 3276800 | tf_op jit(solution)/shard_map/all_gather | solution.py:526
  103.9 25.4 %all-to-all-start = ((bf16[8,64,1536]{2,1,0:T(8,128)(2,1)}), bf16[8,64,1536]{2,1,0:T(8,128)(2,1)}, u32[]{:S(2)}, u32[]{:S(2)}) async-start(bf16[8,64,1536]{2,1,0:T(8,128)(2,1)} %copy-done.4), calls=%async_computation | async-start | bytes 3145728 | tf_op jit(solution)/shard_map/all_to_all | solution.py:516
  108.3 187.6 %all-gather.9.cloned.1.call-start = ((), (), s32[]{:S(2)}) async-start(), calls=%async_computation.13 | async-start | bytes 7864320 | tf_op jit(solution)/shard_map/all_gather | solution.py:526
  134.4 197.4 %all-gather.11.cloned.1.call-start = ((), (), s32[]{:S(2)}) async-start(), calls=%async_computation.14 | async-start | bytes 3932160 | tf_op jit(solution)/shard_map/all_gather | solution.py:526
  143.4 28.1 %collective-permute-start.21 = (bf16[256,2048]{1,0:T(8,128)(2,1)S(1)}, bf16[256,2048]{1,0:T(8,128)(2,1)S(1)}, u32[]{:S(2)}, u32[]{:S(2)}) collective-permute-start(bf16[256,2048]{1,0:T(8,128)(2,1)S(1)} %bitcast.232), channel_id=1, source_target_pairs={{0,16},{8,24},{16,0},{24,8},{1,17},{9,25},{17,1},{25,9},{2,18},{10... | collective-permute-start | bytes 3145736 | tf_op jit(solution)/shard_map/ppermute | solution.py:418
  144.1 29.9 %collective-permute-start.20 = (bf16[256,2048]{1,0:T(8,128)(2,1)S(1)}, bf16[256,2048]{1,0:T(8,128)(2,1)S(1)}, u32[]{:S(2)}, u32[]{:S(2)}) collective-permute-start(bf16[256,2048]{1,0:T(8,128)(2,1)S(1)} %bitcast.233), channel_id=1, source_target_pairs={{0,8},{8,0},{16,24},{24,16},{1,9},{9,1},{17,25},{25,17},{2,10},{10... | collective-permute-start | bytes 3145736 | tf_op jit(solution)/shard_map/ppermute | solution.py:418
  149.6 51.1 %collective-permute-start.24 = (bf16[256,2048]{1,0:T(8,128)(2,1)S(1)}, bf16[256,2048]{1,0:T(8,128)(2,1)}, u32[]{:S(2)}, u32[]{:S(2)}) collective-permute-start(bf16[256,2048]{1,0:T(8,128)(2,1)S(1)} %bitcast.234), channel_id=1, source_target_pairs={{0,1},{1,0},{2,3},{3,2},{4,5},{5,4},{6,7},{7,6},{8,9},{9,8},{10,11... | collective-permute-start | bytes 3145736 | tf_op jit(solution)/shard_map/ppermute | solution.py:421
  163.9 26.0 %collective-permute-start.19 = (f32[4,2,384]{2,1,0:T(2,128)S(1)}, f32[4,2,384]{2,1,0:T(2,128)S(1)}, u32[]{:S(2)}, u32[]{:S(2)}) collective-permute-start(f32[4,2,384]{2,1,0:T(2,128)S(1)} %slice.777), channel_id=1, source_target_pairs={{0,6},{1,7},{8,14},{9,15},{16,22},{17,23},{24,30},{25,31}} | collective-permute-start | bytes 36872 | tf_op jit(solution)/shard_map/ppermute | solution.py:643
  227.7 165.1 %reduce-scatter.5.cloned.1.call-start = ((), (), s32[]{:S(2)}) async-start(), calls=%async_computation.15 | async-start | bytes 3932160 | tf_op jit(solution)/shard_map/reduce_scatter | solution.py:523
  330.1 209.2 %reduce-scatter.7.cloned.1.call-start = ((), (), s32[]{:S(2)}) async-start(), calls=%async_computation.16 | async-start | bytes 7864320 | tf_op jit(solution)/shard_map/reduce_scatter | solution.py:523
  389.5 25.6 %collective-permute-start.47 = (bf16[128,2048]{1,0:T(8,128)(2,1)}, bf16[128,2048]{1,0:T(8,128)(2,1)}, u32[]{:S(2)}, u32[]{:S(2)}) collective-permute-start(bf16[128,2048]{1,0:T(8,128)(2,1)} %get-tuple-element.298), channel_id=1, source_target_pairs={{0,8},{8,0},{16,24},{24,16},{1,9},{9,1},{17,25},{25,17},{2,10},{10... | collective-permute-start | bytes 1572872 | tf_op jit(solution)/shard_map/ppermute | solution.py:418
  391.0 27.1 %collective-permute-start.49 = (bf16[128,2048]{1,0:T(8,128)(2,1)}, bf16[128,2048]{1,0:T(8,128)(2,1)}, u32[]{:S(2)}, u32[]{:S(2)}) collective-permute-start(bf16[128,2048]{1,0:T(8,128)(2,1)} %get-tuple-element.297), channel_id=1, source_target_pairs={{0,16},{8,24},{16,0},{24,8},{1,17},{9,25},{17,1},{25,9},{2,18},{10... | collective-permute-start | bytes 1572872 | tf_op jit(solution)/shard_map/ppermute | solution.py:418
  391.6 26.5 %collective-permute-start.45 = (bf16[128,2048]{1,0:T(8,128)(2,1)}, bf16[128,2048]{1,0:T(8,128)(2,1)}, u32[]{:S(2)}, u32[]{:S(2)}) collective-permute-start(bf16[128,2048]{1,0:T(8,128)(2,1)} %slice.1056), channel_id=1, source_target_pairs={{0,8},{8,0},{16,24},{24,16},{1,9},{9,1},{17,25},{25,17},{2,10},{10... | collective-permute-start | bytes 1572872 | tf_op jit(solution)/shard_map/ppermute | solution.py:418
  412.1 186.9 %reduce-scatter.9.cloned.1.call-start = ((), (), s32[]{:S(2)}) async-start(), calls=%async_computation.17 | async-start | bytes 3276800 | tf_op jit(solution)/shard_map/reduce_scatter | solution.py:523
  444.9 25.4 %collective-permute-start.52 = (bf16[256,2048]{1,0:T(8,128)(2,1)}, bf16[256,2048]{1,0:T(8,128)(2,1)}, u32[]{:S(2)}, u32[]{:S(2)}) collective-permute-start(bf16[256,2048]{1,0:T(8,128)(2,1)} %copy-done.13), channel_id=1, source_target_pairs={{0,8},{8,0},{16,24},{24,16},{1,9},{9,1},{17,25},{25,17},{2,10},{10... | collective-permute-start | bytes 3145736 | tf_op jit(solution)/shard_map/ppermute | solution.py:418
  445.5 25.1 %collective-permute-start.53 = (bf16[256,2048]{1,0:T(8,128)(2,1)}, bf16[256,2048]{1,0:T(8,128)(2,1)}, u32[]{:S(2)}, u32[]{:S(2)}) collective-permute-start(bf16[256,2048]{1,0:T(8,128)(2,1)} %copy-done.13), channel_id=1, source_target_pairs={{0,16},{8,24},{16,0},{24,8},{1,17},{9,25},{17,1},{25,9},{2,18},{10... | collective-permute-start | bytes 3145736 | tf_op jit(solution)/shard_map/ppermute | solution.py:418
  484.4 28.9 %collective-permute-start.66 = (bf16[128,2048]{1,0:T(8,128)(2,1)}, bf16[128,2048]{1,0:T(8,128)(2,1)S(1)}, u32[]{:S(2)}, u32[]{:S(2)}) collective-permute-start(bf16[128,2048]{1,0:T(8,128)(2,1)} %slice.815), channel_id=1, source_target_pairs={{0,16},{8,24},{16,0},{24,8},{1,17},{9,25},{17,1},{25,9},{2,18},{10... | collective-permute-start | bytes 1572872 | tf_op jit(solution)/shard_map/ppermute | solution.py:418
  488.3 26.4 %collective-permute-start.65 = (bf16[128,2048]{1,0:T(8,128)(2,1)}, bf16[128,2048]{1,0:T(8,128)(2,1)S(1)}, u32[]{:S(2)}, u32[]{:S(2)}) collective-permute-start(bf16[128,2048]{1,0:T(8,128)(2,1)} %slice.1055), channel_id=1, source_target_pairs={{0,8},{8,0},{16,24},{24,16},{1,9},{9,1},{17,25},{25,17},{2,10},{10... | collective-permute-start | bytes 1572872 | tf_op jit(solution)/shard_map/ppermute | solution.py:418
  511.8 26.0 %collective-permute-start.68 = (f32[4,2,384]{2,1,0:T(2,128)}, f32[4,2,384]{2,1,0:T(2,128)}, u32[]{:S(2)}, u32[]{:S(2)}) collective-permute-start(f32[4,2,384]{2,1,0:T(2,128)} %slice.813), channel_id=1, source_target_pairs={{6,0},{7,1},{14,8},{15,9},{22,16},{23,17},{30,24},{31,25}} | collective-permute-start | bytes 36872 | tf_op jit(solution)/shard_map/ppermute | solution.py:643
  570.1 25.4 %all-to-all-start.3 = ((bf16[8,64,1536]{2,1,0:T(8,128)(2,1)}), bf16[8,64,1536]{2,1,0:T(8,128)(2,1)}, u32[]{:S(2)}, u32[]{:S(2)}) async-start(bf16[8,64,1536]{2,1,0:T(8,128)(2,1)} %bitcast.254), calls=%async_computation.5 | async-start | bytes 3145728 | tf_op jit(solution)/shard_map/all_to_all | solution.py:516
  574.4 88.9 %reduce-scatter.11.cloned.1.call-start = ((), (), s32[]{:S(2)}) async-start(), calls=%async_computation.18 | async-start | bytes 3645440 | tf_op jit(solution)/shard_map/reduce_scatter | solution.py:523
  635.3 51.6 %collective-permute-start.78 = (bf16[128,2048]{1,0:T(8,128)(2,1)}, bf16[128,2048]{1,0:T(8,128)(2,1)S(1)}, u32[]{:S(2)}, u32[]{:S(2)}) collective-permute-start(bf16[128,2048]{1,0:T(8,128)(2,1)} %get-tuple-element.293), channel_id=1, source_target_pairs={{0,16},{8,24},{16,0},{24,8},{1,17},{9,25},{17,1},{25,9},{2,18},{10... | collective-permute-start | bytes 1572872 | tf_op jit(solution)/shard_map/ppermute | solution.py:418
  636.6 50.3 %collective-permute-start.76 = (bf16[128,2048]{1,0:T(8,128)(2,1)}, bf16[128,2048]{1,0:T(8,128)(2,1)S(1)}, u32[]{:S(2)}, u32[]{:S(2)}) collective-permute-start(bf16[128,2048]{1,0:T(8,128)(2,1)} %slice.1054), channel_id=1, source_target_pairs={{0,8},{8,0},{16,24},{24,16},{1,9},{9,1},{17,25},{25,17},{2,10},{10... | collective-permute-start | bytes 1572872 | tf_op jit(solution)/shard_map/ppermute | solution.py:418
  645.8 41.1 %collective-permute-start.79 = (bf16[128,2048]{1,0:T(8,128)(2,1)}, bf16[128,2048]{1,0:T(8,128)(2,1)S(1)}, u32[]{:S(2)}, u32[]{:S(2)}) collective-permute-start(bf16[128,2048]{1,0:T(8,128)(2,1)} %fusion.33), channel_id=1, source_target_pairs={{0,8},{8,0},{16,24},{24,16},{1,9},{9,1},{17,25},{25,17},{2,10},{10... | collective-permute-start | bytes 1572872 | tf_op jit(solution)/shard_map/ppermute | solution.py:418
  649.6 37.3 %collective-permute-start.77 = (bf16[128,2048]{1,0:T(8,128)(2,1)}, bf16[128,2048]{1,0:T(8,128)(2,1)S(1)}, u32[]{:S(2)}, u32[]{:S(2)}) collective-permute-start(bf16[128,2048]{1,0:T(8,128)(2,1)} %add_convert_fusion.6), channel_id=1, source_target_pairs={{0,16},{8,24},{16,0},{24,8},{1,17},{9,25},{17,1},{25,9},{2,18},{10... | collective-permute-start | bytes 1572872 | tf_op jit(solution)/shard_map/ppermute | solution.py:418
  (172 other events, 1804.6 us)
Sparse Core Ops, SparseCore 0:
  50.8 45.2 all-gather.4
  98.3 53.5 all-gather.6
  153.5 114.1 all-gather.8
  269.1 62.6 all-gather.10
  333.9 58.8 reduce-scatter.4
  412.2 111.5 reduce-scatter.6
  539.4 55.2 reduce-scatter.8
  599.2 59.3 reduce-scatter.10

commit v4 on v3

--- a/solution.py
+++ b/solution.py
@@ -543,9 +543,8 @@
     small = jnp.concatenate([small, marks])
     small = jnp.pad(small, ((0, -small.shape[0] % 32), (0, 0)))
     packed = small.shape[0]
-    small = over_z(small)
-    source, small, *near = lax.optimization_barrier((input_proj, small, *tok_pieces[1:3]))
-    sent_in = to_members(window_columns(source))
+    sent_in = to_members(window_columns(input_proj))
+    small = over_z(after(small, sent_in))
 
     def pair(a, b):
         cut = block + part
@@ -556,7 +555,7 @@
         return jnp.concatenate([x[..., k * block : (k + 1) * block], x[..., at : at + part]], axis=-1)
 
     both = pair(own_columns(branch_proj), own_columns(output_proj.T))
-    sent_both = to_members(after(both, sent_in))
+    sent_both = to_members(after(both, small, *tok_pieces[1:3]))
     ff_packed = pl.pallas_call(
         functools.partial(ff_pack_kernel, cuts=(n_dp, n_z, n_core)),
         out_shape=jax.ShapeDtypeStruct((group, drow, 2 * ff_own), BF),
@@ -600,7 +599,7 @@
         compiler_params=pltpu.CompilerParams(vmem_limit_bytes=VMEM_BYTES),
     )(gain.reshape(1, width), *tok_pieces)
 
-    normed, small, sent_ff = lax.optimization_barrier((normed, small, sent_ff))
+    normed, small = lax.optimization_barrier((normed, small))
     gates_all = small[:, :, :, : gates_len // 256].reshape(n_core, n_dp, n_z, 2, rrow * block // 256, 256)
     gates_all = jnp.transpose(plane.in_order(gates_all), (3, 0, 2, 1, 4, 5)).reshape(2, rec, block)
     gw_full, gw_shared = my_window(gates_all, 1)
@@ -609,11 +608,10 @@
     gwf = jnp.concatenate([gw_full[0], gw_full[1]], axis=1)
     gws = jnp.concatenate([gw_shared[0], gw_shared[1]], axis=1)
 
+    inner = dot(normed, w_in).astype(BF)
+    cot_here, inner, sent_ff = lax.optimization_barrier((cot, inner, sent_ff))
     w_ff = over_z(sent_ff)
     w_down = over_z(after(ffn_down, sent_ff))
-    inner = dot(normed, w_in).astype(BF)
-    cot_here, inner = lax.optimization_barrier((cot, inner))
-    cot_pieces = plane.pieces(cot_here)
     branch = dot(normed, w_branch)
     ends = inner.reshape(n_core, n_dp, seqs, span, window)[:, :, :, span - HALO :]
     ends = jnp.where(core == 1, ends[0], ends[1]).reshape(lines * HALO, window)
@@ -634,6 +632,8 @@
         [pltpu.VMEM((span + HALO, window), F32), pltpu.VMEM((span, own), F32), pltpu.VMEM((8, own), F32)],
         core_id, inner, inner, halo, keep, vec, gwf, gws,
     )
+
+    cot_pieces = plane.pieces(cot_here, [last])
 
     def carried(x, way, beside):
         x = x.reshape(lines, 8, own)[:, :2]
@@ -698,9 +698,10 @@
         core_id, decay, mixed_grad, branch,
     )
     branch_late, mixed_late, *out_first = lax.optimization_barrier((branch_grad, mixed_out, *out_first, adj))[:6]
-    out_terms = plane.add_up(out_terms, out_first)
     both = pair(dot_rows(normed, branch_late).astype(BF), dot_rows(mid_low, mixed_late).astype(BF))
-    suffix, ff_sum, *out_terms = lax.optimization_barrier((carried(front, -1, [both]), ff_sum, *out_terms))
+    both, ff_sum = lax.optimization_barrier((both, ff_sum))
+    out_terms = plane.add_up(out_terms, out_first, [both])
+    suffix, *out_terms = lax.optimization_barrier((carried(front, -1, [both]), *out_terms))
 
     def eight(x):
         return jnp.broadcast_to(x[:, None, :], (lines, 8, own)).reshape(lines * 8, own)
@@ -737,18 +738,20 @@
     ).reshape(total_rows, window)
     ff_part = exchange(ff_sum)
     both_sum = sum_z(after(both, ff_sum))
+    igrad = after(igrad, both_sum)
     in_terms = dot_rows(normed, igrad).astype(BF)
-    both_part = exchange(both_sum)
     igrad, in_terms, ff_part = lax.optimization_barrier((igrad, in_terms, ff_part))
-    layer_out = mine.call(out_kernel, out_terms, [mid], None, [F32])[0]
+    terms = plane.terms(
+        lambda lo, hi: dot_cols(igrad[lo:hi], w_in) + dot_cols(branch_grad[lo:hi], w_branch), rows
+    )
+    both_late, ff_part, mid_late = lax.optimization_barrier((both_sum, ff_part, mid, *terms))[:3]
+    both_part = exchange(both_late)
+    layer_out = mine.call(out_kernel, out_terms, [mid_late], None, [F32])[0]
     gate_out, up_out = pl.pallas_call(
         functools.partial(ff_unpack_kernel, cuts=(n_dp, n_z, n_core)),
         out_shape=[jax.ShapeDtypeStruct((drow, ff), F32)] * 2,
         compiler_params=pltpu.CompilerParams(vmem_limit_bytes=VMEM_BYTES),
     )(ff_part.reshape(group, drow, 2 * ff_own))
-    terms = plane.terms(
-        lambda lo, hi: dot_cols(igrad[lo:hi], w_in) + dot_cols(branch_grad[lo:hi], w_branch), rows
-    )
     terms = plane.add_up(terms)
     second = plane.second
     first_terms, layer_out, gate_out, up_out, both_part = lax.optimization_barrier(
@@ -801,18 +804,27 @@
     gates = gates.reshape(n_z, lot * 2 * (block + part) // window, window)
     joined = jnp.concatenate([in_terms.reshape(n_z, group * drow, window), gates], axis=1)
     joined = sum_z(after(joined.reshape(-1, window), both_sum))
-    joined, first_terms = lax.optimization_barrier((joined, terms[0], *second))[:2]
-    terms = (first_terms, *terms[1:])
+    joined = after(joined, *second)
+    input_grad, gain_part = mine.call(
+        functools.partial(tok_back_kernel, cuts=cuts), terms, [tok, mid_grad], gain, [F32, None]
+    )
+    blocks_z = jnp.swapaxes(jnp.sum(gain_part, axis=0).reshape(n_dp, n_z, n_core * drow), 0, 1).reshape(n_z, group * drow)
+    blocks_z = lax.dynamic_slice_in_dim(jnp.concatenate([blocks_z, blocks_z]), zi, n_z, 0)
+    gain_sum = blocks_z[0]
+    for k in range(1, n_z):
+        gain_sum = gain_sum + lax.ppermute(blocks_z[k], "z", [(i, (i + k) % n_z) for i in range(n_z)])
+    gain_high = gain_sum.astype(BF)
+    gain_low = (gain_sum - gain_high.astype(F32)).astype(BF)
+    gain_rows = jnp.concatenate([gain_high.reshape(group, drow), gain_low.reshape(group, drow)], axis=1)
+    gain_rows = jnp.pad(gain_rows[:, None, :], ((0, 0), (0, 3), (0, window - 2 * drow)))
     in_part = joined[: group * drow].reshape(group, drow, window)
     gates = joined[group * drow :].reshape(lot, 2 * (block + part))
     gates = jnp.concatenate(
         [to_lines(gates[:, : 2 * block], me * block), to_lines(gates[:, 2 * block :], shared_at)], axis=2
     )
     gates = gates.reshape(group, rrow * 2 * (block + part) // window, window)
-    joined = exchange(jnp.concatenate([in_part, gates], axis=1).reshape(-1, window))
-    input_grad, gain_part = mine.call(
-        functools.partial(tok_back_kernel, cuts=cuts), terms, [tok, mid_grad], gain, [F32, None]
-    )
+    gates_end = drow + gates.shape[1]
+    joined = exchange(jnp.concatenate([in_part, gates, gain_rows], axis=1).reshape(-1, window))
 
     lane = jnp.arange(window)
     mine = lane < block + part
@@ -821,21 +833,21 @@
     sums = jnp.concatenate([sums[:7], sums[7:8] * (POWER * jax.nn.sigmoid(-lam))], axis=0)
     vectors = jnp.concatenate(
         [
-            jnp.sum(gain_part, axis=0).reshape(devices, drow), ffn_gain_part.reshape(devices, drow),
+            ffn_gain_part.reshape(devices, drow),
             jnp.swapaxes(sums.reshape(8, devices, rrow), 0, 1).reshape(devices, 8 * rrow),
         ],
         axis=1,
     )
     vec_len = vectors.shape[1]
-    vectors, joined = lax.optimization_barrier((vectors, joined))
     vectors = lax.all_to_all(vectors, EVERY, split_axis=0, concat_axis=0, tiled=True)
     joined = joined.reshape(group, -1, window)
     in_part = joined[:, :drow]
-    gates = joined[:, drow:].reshape(group, rrow, 2 * (block + part)).astype(F32)
+    gates = joined[:, drow:gates_end].reshape(group, rrow, 2 * (block + part)).astype(F32)
+    gain_out = jnp.sum(joined[:, gates_end].astype(F32), axis=0)
+    gain_out = gain_out[:drow] + gain_out[drow : 2 * drow]
     vectors = jnp.sum(vectors.reshape(devices, vec_len), axis=0)
-    gain_out = vectors[:drow]
-    fgain_out = vectors[drow : 2 * drow]
-    chan_out = vectors[2 * drow :].reshape(8, rrow)
+    fgain_out = vectors[:drow]
+    chan_out = vectors[drow:].reshape(8, rrow)
 
     gates_out = jnp.sum(gates[:, :, : 2 * block], axis=0).reshape(rrow, 2, block)
     rest = jnp.sum(gates[:, :, 2 * block :].reshape(shared, sharers, rrow, 2, part), axis=0)

time: 740 us -> 725 us (0.980)
  waiting for transfers between devices: 136 us -> 117 us
  local copies, waits for them, and re-layouts: 136 us -> 126 us
  starting transfers between devices: 109 us -> 117 us
    all_to_all x5, waiting for transfers between devices: 32.1 us -> 11.9 us  [exchange(): return lax.all_to_all(x, GROUP, split_axis=0, concat_axis=0, tiled=True)]
    ppermute x0 -> x3, starting transfers between devices: none -> 9.33 us  [body(): lax.ppermute(blocks_z[k], 'z', [(i, (i + k) % n_z) for i in range(n_z)])]
    unnamed x253 -> x241, local copies, waits for them, and re-layouts: 51.9 us -> 57.1 us
  transfers between devices with their start and end apart: 94 -> 97, of which waited for: 29 -> 30; matrix products, arithmetic and copies ran while one was open for 45% -> 44% of each run, Pallas kernels for 10% -> 11%
where the time goes in v4:
time: 725 us; the launch traced here: 716 us
  matrix products  175 us (24%)
  local copies, waits for them, and re-layouts  126 us (17%)
  starting transfers between devices  117 us (16%)
  waiting for transfers between devices  117 us (16%)
  Pallas kernels  77.1 us (11%)
  other arithmetic  53.1 us (7%)
  blocking collectives  33.4 us (5%)
  between operations  17.3 us (2%)
    ppermute x44, waiting for transfers between devices, near(): return lax.ppermute(x, 'dp', [(i, i ^ k) for i in range(self.n_dp)])  81.6 us
    dot_general x17, matrix products, dot_cols(): lax.dot_general(a, b, (((1,), (1,)), ((), ())), preferred_element_type=F32)  68.8 us
    unnamed x241, local copies, waits for them, and re-layouts  57.1 us
    dot_general x8, matrix products, dot(): lax.dot_general(a, b, (((1,), (0,)), ((), ())), preferred_element_type=F32)  55.8 us
    dot_general x5, matrix products, dot_rows(): lax.dot_general(a, b, (((0,), (0,)), ((), ())), preferred_element_type=F32)  50.3 us
    ppermute x44, starting transfers between devices, near(): return lax.ppermute(x, 'dp', [(i, i ^ k) for i in range(self.n_dp)])  50 us
    pallas_call x3, Pallas kernels, call(): pl.pallas_call(kernel, grid_spec=pltpu.PrefetchScalarGridSpec(num_scalar_...  43.4 us
    all_to_all x5, starting transfers between devices, exchange(): return lax.all_to_all(x, GROUP, split_axis=0, concat_axis=0, tiled=True)  20.1 us
  transfers between devices with their start and end apart: 97, of which 30 were waited for; matrix products, arithmetic and copies ran while one was open for 44% of the time, Pallas kernels for 11%

profile of v4, /device:TPU:0, one launch (start us, length us, event | category | flops | bytes accessed | tf_op | source)
XLA Modules:
  0.0 716.4 jit_solution(3026284755973744986)
XLA Ops:
  9.9 14.9 %all_to_all.66 = bf16[8,64,512]{2,1,0:T(8,128)(2,1)} all-to-all(bf16[8,64,512]{2,1,0:T(8,128)(2,1)S(1)} %copy.127), channel_id=1, replica_groups=mesh['dp'=4,'z'=4,'core'=2] {'dp','core'}, dimensions={0} | all-to-all | bytes 1048576 | tf_op jit(solution)/shard_map/all_to_all | solution.py:516
  26.5 18.4 %all_gather.15 = bf16[768,256]{1,0:T(8,128)(2,1)S(1)} all-gather(bf16[192,256]{1,0:T(8,128)(2,1)S(1)} %fusion.79), channel_id=1, replica_groups=mesh['dp'=4,'z'=4,'core'=2] {'z'}, dimensions={0}, use_global_device_ids=true | all-gather | bytes 491520 | tf_op jit(solution)/shard_map/all_gather | solution.py:526
  108.0 8.9 %shard_map.272 = bf16[2048,2048]{1,0:T(8,128)(2,1)} custom-call(f32[1,2048]{1,0:T(1,128)S(1)} %reshape_reshape.15.gain_ref, bf16[256,2048]{1,0:T(8,128)(2,1)S(1)} %bitcast.235, bf16[256,2048]{1,0:T(8,128)(2,1)} %collective-permute-done.8.refs_1_, bf16[256,2048]{1,0:T(8,128)(2,1)S(1)} %collective-permute-done.9.refs_2_, ...), custom_call_target="tpu_custom_call" | custom-call | tf_op jit(solution)/shard_map/pallas_call | solution.py:593
  120.3 8.6 %convolution_convert_fusion.9.inner_ref.prev_ref = bf16[2048,512]{1,0:T(8,128)(2,1)S(1)} fusion(bf16[2048,2048]{1,0:T(8,128)(2,1)} %shard_map.272, bf16[2048,512]{1,0:T(8,128)(2,1)} %all-gather.5.cloned.1.call-done), kind=kOutput, calls=%fused_computation.57 | convolution fusion | flops 4296015872 | bytes 12582912 | tf_op jit(solution)/shard_map/dot_general | solution.py:40
  132.3 5.0 reverse_select_fusion
  145.8 12.4 %shard_map.273 = (f32[2048,384]{1,0:T(8,128)}, f32[2048,384]{1,0:T(8,128)}, f32[2048,384]{1,0:T(8,128)}, f32[32,384]{1,0:T(8,128)S(1)}) custom-call(s32[1]{0:T(128)} %bitcast.core_ref, bf16[2048,512]{1,0:T(8,128)(2,1)S(1)} %convolution_convert_fusion.9.inner_ref.prev_ref, bf16[2048,512]{1,0:T(8,128)(2,1)S(1)} %convolution_convert_fusion.9.inner_ref.prev_ref, ...), custom_call_target="tpu_custom_call" | custom-call | tf_op jit(solution)/shard_map/pallas_call | solution.py:397
  161.6 7.3 %collective-permute-start.19 = (f32[4,2,384]{2,1,0:T(2,128)S(1)}, f32[4,2,384]{2,1,0:T(2,128)S(1)}, u32[]{:S(2)}, u32[]{:S(2)}) collective-permute-start(f32[4,2,384]{2,1,0:T(2,128)S(1)} %slice.805), channel_id=1, source_target_pairs={{0,6},{1,7},{8,14},{9,15},{16,22},{17,23},{24,30},{25,31}} | collective-permute-start | bytes 36872 | tf_op jit(solution)/shard_map/ppermute | solution.py:643
  182.1 7.1 fusion.113.branch_ref
  206.6 8.4 %collective-permute-done.34 = bf16[128,2048]{1,0:T(8,128)(2,1)S(1)} collective-permute-done((bf16[128,2048]{1,0:T(8,128)(2,1)S(1)}, bf16[128,2048]{1,0:T(8,128)(2,1)S(1)}, u32[]{:S(2)}, u32[]{:S(2)}) %collective-permute-start.34) | collective-permute-done | bytes 524320 | tf_op jit(solution)/shard_map/ppermute | solution.py:418
  226.4 10.5 %collective-permute-done.35.b = bf16[128,2048]{1,0:T(8,128)(2,1)} collective-permute-done((bf16[128,2048]{1,0:T(8,128)(2,1)}, bf16[128,2048]{1,0:T(8,128)(2,1)}, u32[]{:S(2)}, u32[]{:S(2)}) %collective-permute-start.35) | collective-permute-done | bytes 524320 | tf_op jit(solution)/shard_map/ppermute | solution.py:418
  250.6 15.4 %collective-permute-done.36 = bf16[256,2048]{1,0:T(8,128)(2,1)S(1)} collective-permute-done((bf16[256,2048]{1,0:T(8,128)(2,1)S(1)}, bf16[256,2048]{1,0:T(8,128)(2,1)S(1)}, u32[]{:S(2)}, u32[]{:S(2)}) %collective-permute-start.36) | collective-permute-done | bytes 1048608 | tf_op jit(solution)/shard_map/ppermute | solution.py:418
  273.2 5.5 collective-permute-done.38
  286.2 17.7 %fusion.133 = f32[2048,1536]{0,1:T(8,128)S(1)} fusion(bf16[2048,2048]{1,0:T(8,128)(2,1)} %constant_dynamic-update-slice_fusion.21, bf16[2048,1536]{1,0:T(8,128)(2,1)} %all-gather.9.cloned.1.call-done), kind=kOutput, calls=%fused_computation.311 | convolution fusion | flops 12884901888 | bytes 27262976 | tf_op jit(solution)/shard_map/dot_general | solution.py:40
  312.3 10.3 %convolution_convert_fusion.1 = bf16[768,2048]{1,0:T(8,128)(2,1)} fusion(bf16[2048,768]{0,1:T(8,128)(2,1)S(1)} %multiply_convert_fusion.2, bf16[2048,2048]{1,0:T(8,128)(2,1)} %copy-done.75), kind=kOutput, calls=%fused_computation.33 | convolution fusion | flops 6444023808 | bytes 14680064 | tf_op jit(solution)/shard_map/dot_general | solution.py:44
  322.8 7.5 %all-gather.11.cloned.1.call-done = bf16[768,2048]{1,0:T(8,128)(2,1)} async-done(((bf16[192,2048]{1,0:T(8,128)(2,1)}), bf16[768,2048]{1,0:T(8,128)(2,1)}) %all-gather.11.cloned.1.call-update) | async-done | bytes 3145744 | tf_op jit(solution)/shard_map/all_gather | solution.py:526
  330.3 17.5 %multiply_convert_fusion = (bf16[2048,768]{0,1:T(8,128)(2,1)S(1)}, bf16[2048,768]{0,1:T(8,128)(2,1)S(1)}) fusion(f32[2048,1536]{0,1:T(8,128)} %copy-done.33, bf16[2048,2048]{1,0:T(8,128)(2,1)} %copy-done.75, bf16[768,2048]{1,0:T(8,128)(2,1)} %all-gather.11.cloned.1.call-done), kind=kOutput, calls=%fused_computation.13 | convolution fusion | flops 6477053952 | bytes 30408704 | tf_op jit(solution)/shard_map/dot_general | solution.py:48
  347.8 7.6 %convolution_convert_fusion.6 = bf16[512,2048]{1,0:T(8,128)(2,1)} fusion(bf16[2048,1536]{1,0:T(8,128)(2,1)} %all-gather.9.cloned.1.call-done, bf16[2048,768]{0,1:T(8,128)(2,1)S(1)} %get-tuple-element.297, bf16[2048,768]{0,1:T(8,128)(2,1)S(1)} %get-tuple-element.296), kind=kOutput, calls=%fused_computation.54 | convolution fusion | flops 3225419776 | bytes 14680064 | tf_op jit(solution)/shard_map/dot_general | solution.py:48
  355.4 6.7 convolution_convert_fusion.5
  366.5 7.0 convert_add_fusion.2
  377.0 7.0 add_convert_fusion.4
  391.4 19.2 %convolution_convert_fusion = bf16[2048,1536]{1,0:T(8,128)(2,1)} fusion(bf16[2048,2048]{1,0:T(8,128)(2,1)} %constant_dynamic-update-slice_fusion.21, bf16[2048,1536]{0,1:T(8,128)(2,1)} %pad_maximum_fusion), kind=kOutput, calls=%fused_computation.10 | convolution fusion | flops 12888047616 | bytes 20971520 | tf_op jit(solution)/shard_map/dot_general | solution.py:44
  418.6 7.5 %collective-permute-done.51.b = bf16[128,2048]{1,0:T(8,128)(2,1)S(1)} collective-permute-done((bf16[128,2048]{1,0:T(8,128)(2,1)S(1)}, bf16[128,2048]{1,0:T(8,128)(2,1)S(1)}, u32[]{:S(2)}, u32[]{:S(2)}) %collective-permute-start.51) | collective-permute-done | bytes 524320 | tf_op jit(solution)/shard_map/ppermute | solution.py:418
  430.8 6.3 shard_map.275
  460.5 8.7 %collective-permute-done.52 = bf16[256,2048]{1,0:T(8,128)(2,1)} collective-permute-done((bf16[256,2048]{1,0:T(8,128)(2,1)S(1)}, bf16[256,2048]{1,0:T(8,128)(2,1)}, u32[]{:S(2)}, u32[]{:S(2)}) %collective-permute-start.52) | collective-permute-done | bytes 1048608 | tf_op jit(solution)/shard_map/ppermute | solution.py:418
  492.4 7.6 %multiply_convert_fusion.3 = (bf16[2048,384]{1,0:T(8,128)(2,1)}, f32[2048,384]{1,0:T(8,128)}) fusion(f32[2048,384]{1,0:T(8,128)S(1)} %copy-done.35, f32[2048,384]{1,0:T(8,128)S(1)} %copy-done.31, bf16[2048,2048]{1,0:T(8,128)(2,1)S(1)} %constant_dynamic-update-slice_fusion.30, bf16[2048,64]{1,0:T(8,128)(2,1)S(1)} %copy-done.70, ...), kind=kOutput, calls=%fused_computation.49 | convolution fusion | flops 3241672704 | bytes 20709376 | tf_op jit(solution)/shard_map/dot_general | solution.py:40
  500.0 10.1 %shard_map.276 = (f32[2048,384]{1,0:T(8,128)S(1)}, f32[2048,384]{1,0:T(8,128)}, f32[32,384]{1,0:T(8,128)S(1)}) custom-call(s32[1]{0:T(128)} %bitcast.core_ref, f32[2048,384]{1,0:T(8,128)} %get-tuple-element.155.decay_ref, f32[2048,384]{1,0:T(8,128)} %get-tuple-element.360.grad_ref, f32[2048,384]{1,0:T(8,128)} %copy-done.34), custom_call_target="tpu_custom_call" | custom-call | tf_op jit(solution)/shard_map/pallas_call | solution.py:397
  513.1 7.3 %convolution_convert_fusion.11 = bf16[2048,384]{0,1:T(8,128)(2,1)S(1)} fusion(bf16[2048,2048]{1,0:T(8,128)(2,1)} %shard_map.272, bf16[2048,384]{1,0:T(8,128)(2,1)S(1)} %copy-done.76), kind=kOutput, calls=%fused_computation.60 | convolution fusion | flops 3222011904 | bytes 11534336 | tf_op jit(solution)/shard_map/dot_general | solution.py:44
  549.2 20.9 %shard_map.277 = (bf16[2048,512]{1,0:T(8,128)(2,1)S(1)}, f32[64,512]{1,0:T(8,128)S(1)}, f32[32,512]{1,0:T(8,128)S(1)}, f32[256,512]{1,0:T(8,128)S(1)}, f32[256,256]{1,0:T(8,128)S(1)}, /*index=5*/f32[8,512]{1,0:T(8,128)S(1)}) custom-call(s32[1]{0:T(128)} %bitcast.core_ref, bf16[2048,512]{1,0:T(8,128)(2,1)} %copy-done, bf16[2048,512]{1,0:T(8,128)(2,1)} %copy-done, ...), custom_call_target="tpu_custom_call" | custom-call | tf_op jit(solution)/shard_map/pallas_call | solution.py:397
  582.0 9.7 %convolution_convert_fusion.2 = bf16[2048,512]{1,0:T(8,128)(2,1)} fusion(bf16[2048,2048]{1,0:T(8,128)(2,1)} %shard_map.272, bf16[2048,512]{1,0:T(8,128)(2,1)S(1)} %bitcast.239), kind=kOutput, calls=%fused_computation.50 | convolution fusion | flops 4296015872 | bytes 12582912 | tf_op jit(solution)/shard_map/dot_general | solution.py:44
  648.3 8.8 %all-to-all-start.6 = ((f32[32,1,704]{2,1,0:T(1,128)}), f32[32,1,704]{2,1,0:T(1,128)S(1)}, u32[]{:S(2)}, u32[]{:S(2)}) async-start(f32[32,1,704]{2,1,0:T(1,128)} %copy.153), calls=%async_computation.10 | async-start | bytes 196608 | tf_op jit(solution)/shard_map/all_to_all | solution.py:842
  659.1 5.2 shard_map.280
  690.3 11.8 %all-to-all-done.5 = bf16[8,168,512]{2,1,0:T(8,128)(2,1)S(1)} async-done(((bf16[8,168,512]{2,1,0:T(8,128)(2,1)}), bf16[8,168,512]{2,1,0:T(8,128)(2,1)S(1)}, u32[]{:S(2)}, u32[]{:S(2)}) %all-to-all-start.5) | async-done | bytes 1376288 | tf_op jit(solution)/shard_map/all_to_all | solution.py:516
  (677 shorter events, 372.3 us)
Async XLA Ops:
  7.2 113.1 %all-gather.5.cloned.1.call-start = ((), (), s32[]{:S(2)}) async-start(), calls=%async_computation.11 | async-start | bytes 2621440 | tf_op jit(solution)/shard_map/all_gather | solution.py:526
  24.9 47.4 %collective-permute-start.9 = (bf16[256,2048]{1,0:T(8,128)(2,1)S(1)}, bf16[256,2048]{1,0:T(8,128)(2,1)S(1)}, u32[]{:S(2)}, u32[]{:S(2)}) collective-permute-start(bf16[256,2048]{1,0:T(8,128)(2,1)S(1)} %bitcast.232), channel_id=1, source_target_pairs={{0,16},{8,24},{16,0},{24,8},{1,17},{9,25},{17,1},{25,9},{2,18},{10... | collective-permute-start | bytes 3145736 | tf_op jit(solution)/shard_map/ppermute | solution.py:418
  25.5 47.3 %collective-permute-start.8 = (bf16[256,2048]{1,0:T(8,128)(2,1)S(1)}, bf16[256,2048]{1,0:T(8,128)(2,1)}, u32[]{:S(2)}, u32[]{:S(2)}) collective-permute-start(bf16[256,2048]{1,0:T(8,128)(2,1)S(1)} %bitcast.233), channel_id=1, source_target_pairs={{0,8},{8,0},{16,24},{24,16},{1,9},{9,1},{17,25},{25,17},{2,10},{10... | collective-permute-start | bytes 3145736 | tf_op jit(solution)/shard_map/ppermute | solution.py:418
  69.2 37.8 %collective-permute-start.12 = (bf16[256,2048]{1,0:T(8,128)(2,1)S(1)}, bf16[256,2048]{1,0:T(8,128)(2,1)}, u32[]{:S(2)}, u32[]{:S(2)}) collective-permute-start(bf16[256,2048]{1,0:T(8,128)(2,1)S(1)} %bitcast.234), channel_id=1, source_target_pairs={{0,1},{1,0},{2,3},{3,2},{4,5},{5,4},{6,7},{7,6},{8,9},{9,8},{10,11... | collective-permute-start | bytes 3145736 | tf_op jit(solution)/shard_map/ppermute | solution.py:421
  77.3 99.8 %all-gather.7.cloned.1.call-start = ((), (), s32[]{:S(2)}) async-start(), calls=%async_computation.12 | async-start | bytes 3276800 | tf_op jit(solution)/shard_map/all_gather | solution.py:526
  96.6 32.3 %all-to-all-start.1 = ((bf16[8,64,1536]{2,1,0:T(8,128)(2,1)}), bf16[8,64,1536]{2,1,0:T(8,128)(2,1)}, u32[]{:S(2)}, u32[]{:S(2)}) async-start(bf16[8,64,1536]{2,1,0:T(8,128)(2,1)} %shard_map.271), calls=%async_computation.1 | async-start | bytes 3145728 | tf_op jit(solution)/shard_map/all_to_all | solution.py:516
  100.9 185.3 %all-gather.9.cloned.1.call-start = ((), (), s32[]{:S(2)}) async-start(), calls=%async_computation.13 | async-start | bytes 7864320 | tf_op jit(solution)/shard_map/all_gather | solution.py:526
  128.9 29.4 %collective-permute-start.20 = (bf16[256,2048]{1,0:T(8,128)(2,1)}, bf16[256,2048]{1,0:T(8,128)(2,1)}, u32[]{:S(2)}, u32[]{:S(2)}) collective-permute-start(bf16[256,2048]{1,0:T(8,128)(2,1)} %bitcast.1.cot_ref), channel_id=1, source_target_pairs={{0,8},{8,0},{16,24},{24,16},{1,9},{9,1},{17,25},{25,17},{2,10},{10... | collective-permute-start | bytes 3145736 | tf_op jit(solution)/shard_map/ppermute | solution.py:418
  130.8 27.5 %collective-permute-start.21 = (bf16[256,2048]{1,0:T(8,128)(2,1)}, bf16[256,2048]{1,0:T(8,128)(2,1)}, u32[]{:S(2)}, u32[]{:S(2)}) collective-permute-start(bf16[256,2048]{1,0:T(8,128)(2,1)} %bitcast.1.cot_ref), channel_id=1, source_target_pairs={{0,16},{8,24},{16,0},{24,8},{1,17},{9,25},{17,1},{25,9},{2,18},{10... | collective-permute-start | bytes 3145736 | tf_op jit(solution)/shard_map/ppermute | solution.py:418
  137.3 193.0 %all-gather.11.cloned.1.call-start = ((), (), s32[]{:S(2)}) async-start(), calls=%async_computation.14 | async-start | bytes 3932160 | tf_op jit(solution)/shard_map/all_gather | solution.py:526
  161.6 30.6 %collective-permute-start.24 = (bf16[256,2048]{1,0:T(8,128)(2,1)}, bf16[256,2048]{1,0:T(8,128)(2,1)}, u32[]{:S(2)}, u32[]{:S(2)}) collective-permute-start(bf16[256,2048]{1,0:T(8,128)(2,1)} %bitcast.1.cot_ref), channel_id=1, source_target_pairs={{0,1},{1,0},{2,3},{3,2},{4,5},{5,4},{6,7},{7,6},{8,9},{9,8},{10,11... | collective-permute-start | bytes 3145736 | tf_op jit(solution)/shard_map/ppermute | solution.py:421
  201.2 25.0 %collective-permute-start.33 = (bf16[128,2048]{1,0:T(8,128)(2,1)}, bf16[128,2048]{1,0:T(8,128)(2,1)S(1)}, u32[]{:S(2)}, u32[]{:S(2)}) collective-permute-start(bf16[128,2048]{1,0:T(8,128)(2,1)} %get-tuple-element.315), channel_id=1, source_target_pairs={{0,16},{8,24},{16,0},{24,8},{1,17},{9,25},{17,1},{25,9},{2,18},{10... | collective-permute-start | bytes 1572872 | tf_op jit(solution)/shard_map/ppermute | solution.py:418
  218.0 173.4 %reduce-scatter.5.cloned.1.call-start = ((), (), s32[]{:S(2)}) async-start(), calls=%async_computation.15 | async-start | bytes 3932160 | tf_op jit(solution)/shard_map/reduce_scatter | solution.py:523
  241.4 24.6 %collective-permute-start.36 = (bf16[256,2048]{1,0:T(8,128)(2,1)S(1)}, bf16[256,2048]{1,0:T(8,128)(2,1)S(1)}, u32[]{:S(2)}, u32[]{:S(2)}) collective-permute-start(bf16[256,2048]{1,0:T(8,128)(2,1)S(1)} %get-tuple-element.161), channel_id=1, source_target_pairs={{0,8},{8,0},{16,24},{24,16},{1,9},{9,1},{17,25},{25,17},{2,10},{10... | collective-permute-start | bytes 3145736 | tf_op jit(solution)/shard_map/ppermute | solution.py:418
  242.1 24.0 %collective-permute-start.37 = (bf16[256,2048]{1,0:T(8,128)(2,1)S(1)}, bf16[256,2048]{1,0:T(8,128)(2,1)S(1)}, u32[]{:S(2)}, u32[]{:S(2)}) collective-permute-start(bf16[256,2048]{1,0:T(8,128)(2,1)S(1)} %get-tuple-element.161), channel_id=1, source_target_pairs={{0,16},{8,24},{16,0},{24,8},{1,17},{9,25},{17,1},{25,9},{2,18},{10... | collective-permute-start | bytes 3145736 | tf_op jit(solution)/shard_map/ppermute | solution.py:418
  322.6 203.7 %reduce-scatter.7.cloned.1.call-start = ((), (), s32[]{:S(2)}) async-start(), calls=%async_computation.16 | async-start | bytes 7864320 | tf_op jit(solution)/shard_map/reduce_scatter | solution.py:523
  385.2 25.9 %collective-permute-start.50 = (bf16[128,2048]{1,0:T(8,128)(2,1)}, bf16[128,2048]{1,0:T(8,128)(2,1)}, u32[]{:S(2)}, u32[]{:S(2)}) collective-permute-start(bf16[128,2048]{1,0:T(8,128)(2,1)} %get-tuple-element.311), channel_id=1, source_target_pairs={{0,16},{8,24},{16,0},{24,8},{1,17},{9,25},{17,1},{25,9},{2,18},{10... | collective-permute-start | bytes 1572872 | tf_op jit(solution)/shard_map/ppermute | solution.py:418
  386.5 27.6 %collective-permute-start.47 = (bf16[128,2048]{1,0:T(8,128)(2,1)}, bf16[128,2048]{1,0:T(8,128)(2,1)}, u32[]{:S(2)}, u32[]{:S(2)}) collective-permute-start(bf16[128,2048]{1,0:T(8,128)(2,1)} %get-tuple-element.313), channel_id=1, source_target_pairs={{0,8},{8,0},{16,24},{24,16},{1,9},{9,1},{17,25},{25,17},{2,10},{10... | collective-permute-start | bytes 1572872 | tf_op jit(solution)/shard_map/ppermute | solution.py:418
  388.0 29.0 %collective-permute-start.49 = (bf16[128,2048]{1,0:T(8,128)(2,1)}, bf16[128,2048]{1,0:T(8,128)(2,1)S(1)}, u32[]{:S(2)}, u32[]{:S(2)}) collective-permute-start(bf16[128,2048]{1,0:T(8,128)(2,1)} %get-tuple-element.312), channel_id=1, source_target_pairs={{0,16},{8,24},{16,0},{24,8},{1,17},{9,25},{17,1},{25,9},{2,18},{10... | collective-permute-start | bytes 1572872 | tf_op jit(solution)/shard_map/ppermute | solution.py:418
  388.6 29.2 %collective-permute-start.45 = (bf16[128,2048]{1,0:T(8,128)(2,1)}, bf16[128,2048]{1,0:T(8,128)(2,1)S(1)}, u32[]{:S(2)}, u32[]{:S(2)}) collective-permute-start(bf16[128,2048]{1,0:T(8,128)(2,1)} %slice.1090), channel_id=1, source_target_pairs={{0,8},{8,0},{16,24},{24,16},{1,9},{9,1},{17,25},{25,17},{2,10},{10... | collective-permute-start | bytes 1572872 | tf_op jit(solution)/shard_map/ppermute | solution.py:418
  410.6 171.4 %reduce-scatter.9.cloned.1.call-start = ((), (), s32[]{:S(2)}) async-start(), calls=%async_computation.17 | async-start | bytes 3276800 | tf_op jit(solution)/shard_map/reduce_scatter | solution.py:523
  444.0 25.2 %collective-permute-start.52 = (bf16[256,2048]{1,0:T(8,128)(2,1)S(1)}, bf16[256,2048]{1,0:T(8,128)(2,1)}, u32[]{:S(2)}, u32[]{:S(2)}) collective-permute-start(bf16[256,2048]{1,0:T(8,128)(2,1)S(1)} %get-tuple-element.178), channel_id=1, source_target_pairs={{0,8},{8,0},{16,24},{24,16},{1,9},{9,1},{17,25},{25,17},{2,10},{10... | collective-permute-start | bytes 3145736 | tf_op jit(solution)/shard_map/ppermute | solution.py:418
  444.5 24.9 %collective-permute-start.53 = (bf16[256,2048]{1,0:T(8,128)(2,1)S(1)}, bf16[256,2048]{1,0:T(8,128)(2,1)}, u32[]{:S(2)}, u32[]{:S(2)}) collective-permute-start(bf16[256,2048]{1,0:T(8,128)(2,1)S(1)} %get-tuple-element.178), channel_id=1, source_target_pairs={{0,16},{8,24},{16,0},{24,8},{1,17},{9,25},{17,1},{25,9},{2,18},{10... | collective-permute-start | bytes 3145736 | tf_op jit(solution)/shard_map/ppermute | solution.py:418
  483.3 26.8 %collective-permute-start.66 = (bf16[128,2048]{1,0:T(8,128)(2,1)}, bf16[128,2048]{1,0:T(8,128)(2,1)S(1)}, u32[]{:S(2)}, u32[]{:S(2)}) collective-permute-start(bf16[128,2048]{1,0:T(8,128)(2,1)} %slice.843), channel_id=1, source_target_pairs={{0,16},{8,24},{16,0},{24,8},{1,17},{9,25},{17,1},{25,9},{2,18},{10... | collective-permute-start | bytes 1572872 | tf_op jit(solution)/shard_map/ppermute | solution.py:418
  544.8 47.0 %all-to-all-start.3 = ((bf16[8,64,1536]{2,1,0:T(8,128)(2,1)}), bf16[8,64,1536]{2,1,0:T(8,128)(2,1)}, u32[]{:S(2)}, u32[]{:S(2)}) async-start(bf16[8,64,1536]{2,1,0:T(8,128)(2,1)} %bitcast.264), calls=%async_computation.6 | async-start | bytes 3145728 | tf_op jit(solution)/shard_map/all_to_all | solution.py:516
  549.1 127.2 %reduce-scatter.11.cloned.1.call-start = ((), (), s32[]{:S(2)}) async-start(), calls=%async_computation.18 | async-start | bytes 3645440 | tf_op jit(solution)/shard_map/reduce_scatter | solution.py:523
  622.1 26.2 %all-to-all-start.4 = ((bf16[8,64,640]{2,1,0:T(8,128)(2,1)}), bf16[8,64,640]{2,1,0:T(8,128)(2,1)}, u32[]{:S(2)}, u32[]{:S(2)}) async-start(bf16[8,64,640]{2,1,0:T(8,128)(2,1)} %bitcast.256), calls=%async_computation.7 | async-start | bytes 1310720 | tf_op jit(solution)/shard_map/all_to_all | solution.py:516
  626.4 30.7 %collective-permute-start.77 = (bf16[128,2048]{1,0:T(8,128)(2,1)}, bf16[128,2048]{1,0:T(8,128)(2,1)}, u32[]{:S(2)}, u32[]{:S(2)}) collective-permute-start(bf16[128,2048]{1,0:T(8,128)(2,1)} %get-tuple-element.307), channel_id=1, source_target_pairs={{0,16},{8,24},{16,0},{24,8},{1,17},{9,25},{17,1},{25,9},{2,18},{10... | collective-permute-start | bytes 1572872 | tf_op jit(solution)/shard_map/ppermute | solution.py:418
  628.3 28.8 %collective-permute-start.73 = (bf16[128,2048]{1,0:T(8,128)(2,1)}, bf16[128,2048]{1,0:T(8,128)(2,1)}, u32[]{:S(2)}, u32[]{:S(2)}) collective-permute-start(bf16[128,2048]{1,0:T(8,128)(2,1)} %slice.1088), channel_id=1, source_target_pairs={{0,8},{8,0},{16,24},{24,16},{1,9},{9,1},{17,25},{25,17},{2,10},{10... | collective-permute-start | bytes 1572872 | tf_op jit(solution)/shard_map/ppermute | solution.py:418
  632.1 27.1 %collective-permute-start.79 = (bf16[128,2048]{1,0:T(8,128)(2,1)}, bf16[128,2048]{1,0:T(8,128)(2,1)}, u32[]{:S(2)}, u32[]{:S(2)}) collective-permute-start(bf16[128,2048]{1,0:T(8,128)(2,1)} %fusion.35), channel_id=1, source_target_pairs={{0,8},{8,0},{16,24},{24,16},{1,9},{9,1},{17,25},{25,17},{2,10},{10... | collective-permute-start | bytes 1572872 | tf_op jit(solution)/shard_map/ppermute | solution.py:418
  634.8 24.4 %collective-permute-start.76 = (bf16[128,2048]{1,0:T(8,128)(2,1)}, bf16[128,2048]{1,0:T(8,128)(2,1)}, u32[]{:S(2)}, u32[]{:S(2)}) collective-permute-start(bf16[128,2048]{1,0:T(8,128)(2,1)} %add_convert_fusion.6), channel_id=1, source_target_pairs={{0,16},{8,24},{16,0},{24,8},{1,17},{9,25},{17,1},{25,9},{2,18},{10... | collective-permute-start | bytes 1572872 | tf_op jit(solution)/shard_map/ppermute | solution.py:418
  648.3 25.5 %all-to-all-start.6 = ((f32[32,1,704]{2,1,0:T(1,128)}), f32[32,1,704]{2,1,0:T(1,128)S(1)}, u32[]{:S(2)}, u32[]{:S(2)}) async-start(f32[32,1,704]{2,1,0:T(1,128)} %copy.153), calls=%async_computation.10 | async-start | bytes 196608 | tf_op jit(solution)/shard_map/all_to_all | solution.py:842
  (167 other events, 1765.0 us)
Sparse Core Ops, SparseCore 0:
  25.0 48.4 all-gather.4
  95.8 53.4 all-gather.6
  150.8 115.3 all-gather.8
  267.6 62.6 all-gather.10
  332.4 58.8 reduce-scatter.4
  410.7 110.7 reduce-scatter.6
  526.4 53.8 reduce-scatter.8
  601.0 60.6 reduce-scatter.10

commit v5 on v4

--- a/solution.py
+++ b/solution.py
@@ -339,6 +339,16 @@
             ],
             compiler_params=pltpu.CompilerParams(vmem_limit_bytes=VMEM_BYTES),
         )(*pieces, *arrays, *gains)
+
+
+def pair_pack_kernel(a_ref, b_ref, out_ref, *, block, part):
+    group = out_ref.shape[0]
+    for n in range(group):
+        at = group * block + n * part
+        out_ref[n, :, :block] = a_ref[:, n * block : (n + 1) * block]
+        out_ref[n, :, block : 2 * block] = b_ref[:, n * block : (n + 1) * block]
+        parts = [ref[:, at : at + part].astype(F32) for ref in (a_ref, b_ref)]
+        out_ref[n, :, 2 * block :] = jnp.concatenate(parts, axis=1).astype(BF)
 
 
 def ff_pack_kernel(gate_ref, up_ref, out_ref, *, cuts):
@@ -499,12 +509,6 @@
     core = plane.core
     core_id = core.astype(jnp.int32).reshape(1)
 
-    def own_columns(w):
-        lead = w.shape[0]
-        full = w[:, : group * block].reshape(lead, group, block)
-        rest = w[:, group * block :].reshape(lead, group, part)
-        return jnp.concatenate([full, rest, jnp.zeros((lead, group, lanes - part), w.dtype)], axis=2)
-
     def window_columns(w):
         lead = w.shape[0]
         full = w[:, : group * block].reshape(lead, group, block)
@@ -530,17 +534,15 @@
     tok = tokens.reshape(rows, width)
     tok_pieces = plane.pieces(tok)
     rrow = rec // devices
-    small = jnp.concatenate(
-        [
-            gate_weight.reshape(-1), norm_gain, ffn_gain, conv_kernel.reshape(-1), conv_bias, gate_bias.reshape(-1),
-            decay_param,
-        ]
-    )
-    small_len = small.shape[0]
+    vectors = jnp.concatenate(
+        [norm_gain, ffn_gain, conv_kernel.reshape(-1), conv_bias, gate_bias.reshape(-1), decay_param]
+    )
+    small_len = vectors.shape[0]
+    vectors = jnp.pad(vectors, (0, -small_len % 256)).reshape(-1, 256)
+    gates_rows = 2 * rrow * block // 256
+    marks_at = gates_rows + vectors.shape[0]
     marks = (1 - doc_reset).astype(BF).reshape(-1, 256)
-    small = jnp.pad(small, (0, -small_len % 256)).reshape(-1, 256)
-    marks_at = small.shape[0]
-    small = jnp.concatenate([small, marks])
+    small = jnp.concatenate([gate_weight.reshape(gates_rows, 256), vectors, marks], axis=0)
     small = jnp.pad(small, ((0, -small.shape[0] % 32), (0, 0)))
     packed = small.shape[0]
     sent_in = to_members(window_columns(input_proj))
@@ -554,8 +556,12 @@
         at = 2 * block + k * part
         return jnp.concatenate([x[..., k * block : (k + 1) * block], x[..., at : at + part]], axis=-1)
 
-    both = pair(own_columns(branch_proj), own_columns(output_proj.T))
-    sent_both = to_members(after(both, small, *tok_pieces[1:3]))
+    both = pl.pallas_call(
+        functools.partial(pair_pack_kernel, block=block, part=part),
+        out_shape=jax.ShapeDtypeStruct((group, drow, 2 * (block + part)), BF),
+        compiler_params=pltpu.CompilerParams(vmem_limit_bytes=VMEM_BYTES),
+    )(branch_proj, output_proj.T)
+    sent_both = exchange(after(both, small).reshape(group * drow, 2 * (block + part)))
     ff_packed = pl.pallas_call(
         functools.partial(ff_pack_kernel, cuts=(n_dp, n_z, n_core)),
         out_shape=jax.ShapeDtypeStruct((group, drow, 2 * ff_own), BF),
@@ -564,14 +570,13 @@
     w_in = over_z(sent_in)
     w_both = over_z(sent_both)
     w_branch, w_out = (jnp.pad(unpair(w_both, k), ((0, 0), (0, lanes - part))) for k in range(2))
-    small = plane.gather(small).reshape(n_core, n_dp, n_z, packed, 256)
+    small = plane.gather(small, [sent_both]).reshape(n_core, n_dp, n_z, packed, 256)
     keep = lax.dynamic_index_in_dim(small, zi, 2, False)[:, :, marks_at : marks_at + rows // 256]
     keep = keep.astype(F32).reshape(total_rows, 1)
     ff_packed, small = lax.optimization_barrier((ff_packed, small))
     sent_ff = exchange(ff_packed.reshape(group * drow, 2 * ff_own))
-    gates_len = 2 * rrow * block
-    rest = small[:, :, :, gates_len // 256 : marks_at]
-    rest = jnp.swapaxes(plane.in_order(rest), 1, 2).reshape(devices, -1)[:, : small_len - gates_len].astype(F32)
+    rest = small[:, :, :, gates_rows:marks_at]
+    rest = jnp.swapaxes(plane.in_order(rest), 1, 2).reshape(devices, -1)[:, :small_len].astype(F32)
     gain = rest[:, :drow].reshape(width)
     fgain = rest[:, drow : 2 * drow].reshape(width)
     chan = rest[:, 2 * drow :].reshape(devices, taps + 4, rrow)
@@ -600,7 +605,7 @@
     )(gain.reshape(1, width), *tok_pieces)
 
     normed, small = lax.optimization_barrier((normed, small))
-    gates_all = small[:, :, :, : gates_len // 256].reshape(n_core, n_dp, n_z, 2, rrow * block // 256, 256)
+    gates_all = small[:, :, :, :gates_rows].reshape(n_core, n_dp, n_z, 2, rrow * block // 256, 256)
     gates_all = jnp.transpose(plane.in_order(gates_all), (3, 0, 2, 1, 4, 5)).reshape(2, rec, block)
     gw_full, gw_shared = my_window(gates_all, 1)
     gw_shared = lax.dynamic_slice_in_dim(gw_shared, quarter * part, part, 2)

time: 725 us -> 718 us (level)
  local copies, waits for them, and re-layouts: 126 us -> 114 us
  waiting for transfers between devices: 117 us -> 125 us
    ppermute x44, waiting for transfers between devices: 81.6 us -> 102 us  [near(): return lax.ppermute(x, 'dp', [(i, i ^ k) for i in range(self.n_dp)])]
    all_gather x4, waiting for transfers between devices: 7.55 us -> 0.04 us  [over_z(): return lax.all_gather(x, 'z', axis=0, tiled=True)]
    unnamed x241 -> x243, local copies, waits for them, and re-layouts: 57.1 us -> 52.6 us
  transfers between devices with their start and end apart: 97 -> 97, of which waited for: 30 -> 27; matrix products, arithmetic and copies ran while one was open for 44% -> 42% of each run, Pallas kernels for 11% -> 11%
where the time goes in v5:
time: 718 us; the launch traced here: 711 us
  matrix products  177 us (25%)
  waiting for transfers between devices  125 us (17%)
  local copies, waits for them, and re-layouts  114 us (16%)
  starting transfers between devices  113 us (16%)
  Pallas kernels  78.4 us (11%)
  other arithmetic  51.2 us (7%)
  blocking collectives  35.3 us (5%)
  between operations  17.4 us (2%)
    ppermute x44, waiting for transfers between devices, near(): return lax.ppermute(x, 'dp', [(i, i ^ k) for i in range(self.n_dp)])  102 us
    dot_general x17, matrix products, dot_cols(): lax.dot_general(a, b, (((1,), (1,)), ((), ())), preferred_element_type=F32)  69.2 us
    dot_general x8, matrix products, dot(): lax.dot_general(a, b, (((1,), (0,)), ((), ())), preferred_element_type=F32)  55.8 us
    unnamed x243, local copies, waits for them, and re-layouts  52.6 us
    dot_general x5, matrix products, dot_rows(): lax.dot_general(a, b, (((0,), (0,)), ((), ())), preferred_element_type=F32)  51.7 us
    ppermute x44, starting transfers between devices, near(): return lax.ppermute(x, 'dp', [(i, i ^ k) for i in range(self.n_dp)])  48.1 us
    pallas_call x3, Pallas kernels, call(): pl.pallas_call(kernel, grid_spec=pltpu.PrefetchScalarGridSpec(num_scalar_...  43.4 us
    all_gather x1, blocking collectives, over_z(): return lax.all_gather(x, 'z', axis=0, tiled=True)  20.3 us
  transfers between devices with their start and end apart: 97, of which 27 were waited for; matrix products, arithmetic and copies ran while one was open for 42% of the time, Pallas kernels for 11%

profile of v5, /device:TPU:0, one launch (start us, length us, event | category | flops | bytes accessed | tf_op | source)
XLA Modules:
  0.0 710.9 jit_solution(10454340568876538874)
XLA Ops:
  9.8 14.9 %all_to_all.66 = bf16[8,64,512]{2,1,0:T(8,128)(2,1)} all-to-all(bf16[8,64,512]{2,1,0:T(8,128)(2,1)S(1)} %copy.95), channel_id=1, replica_groups=mesh['dp'=4,'z'=4,'core'=2] {'dp','core'}, dimensions={0} | all-to-all | bytes 1048576 | tf_op jit(solution)/shard_map/all_to_all | solution.py:520
  32.0 20.3 %all_gather.15 = bf16[768,256]{1,0:T(8,128)(2,1)} all-gather(bf16[192,256]{1,0:T(8,128)(2,1)S(1)} %fusion.81), channel_id=1, replica_groups=mesh['dp'=4,'z'=4,'core'=2] {'z'}, dimensions={0}, use_global_device_ids=true | all-gather | bytes 491520 | tf_op jit(solution)/shard_map/all_gather | solution.py:530
  63.9 10.8 %collective-permute-done = bf16[768,256]{1,0:T(8,128)(2,1)} collective-permute-done((bf16[768,256]{1,0:T(8,128)(2,1)}, bf16[768,256]{1,0:T(8,128)(2,1)}, u32[]{:S(2)}, u32[]{:S(2)}) %collective-permute-start) | collective-permute-done | bytes 393248 | tf_op jit(solution)/shard_map/ppermute | solution.py:428
  92.0 8.7 %collective-permute-done.10 = bf16[128,2048]{1,0:T(8,128)(2,1)S(1)} collective-permute-done((bf16[128,2048]{1,0:T(8,128)(2,1)S(1)}, bf16[128,2048]{1,0:T(8,128)(2,1)S(1)}, u32[]{:S(2)}, u32[]{:S(2)}) %collective-permute-start.10) | collective-permute-done | bytes 524320 | tf_op jit(solution)/shard_map/ppermute | solution.py:428
  114.7 9.3 %shard_map.273 = bf16[2048,2048]{1,0:T(8,128)(2,1)} custom-call(f32[1,2048]{1,0:T(1,128)S(1)} %reshape_reshape.15.gain_ref, bf16[256,2048]{1,0:T(8,128)(2,1)S(1)} %bitcast.231, bf16[256,2048]{1,0:T(8,128)(2,1)} %collective-permute-done.8.refs_1_, bf16[256,2048]{1,0:T(8,128)(2,1)S(1)} %collective-permute-done.9.refs_2_, ...), custom_call_target="tpu_custom_call" | custom-call | tf_op jit(solution)/shard_map/pallas_call | solution.py:598
  127.0 8.5 %convolution_convert_fusion.9.inner_ref.prev_ref = bf16[2048,512]{1,0:T(8,128)(2,1)S(1)} fusion(bf16[2048,2048]{1,0:T(8,128)(2,1)} %shard_map.273, bf16[2048,512]{1,0:T(8,128)(2,1)} %all-gather.5.cloned.1.call-done), kind=kOutput, calls=%fused_computation.57 | convolution fusion | flops 4296015872 | bytes 12582912 | tf_op jit(solution)/shard_map/dot_general | solution.py:40
  150.4 12.4 %shard_map.274 = (f32[2048,384]{1,0:T(8,128)}, f32[2048,384]{1,0:T(8,128)}, f32[2048,384]{1,0:T(8,128)}, f32[32,384]{1,0:T(8,128)S(1)}) custom-call(s32[1]{0:T(128)} %bitcast.core_ref, bf16[2048,512]{1,0:T(8,128)(2,1)S(1)} %convolution_convert_fusion.9.inner_ref.prev_ref, bf16[2048,512]{1,0:T(8,128)(2,1)S(1)} %convolution_convert_fusion.9.inner_ref.prev_ref, ...), custom_call_target="tpu_custom_call" | custom-call | tf_op jit(solution)/shard_map/pallas_call | solution.py:407
  162.9 6.0 collective-permute-start.19
  187.7 7.1 fusion.115.branch_ref
  212.4 8.4 %collective-permute-done.34 = bf16[128,2048]{1,0:T(8,128)(2,1)S(1)} collective-permute-done((bf16[128,2048]{1,0:T(8,128)(2,1)S(1)}, bf16[128,2048]{1,0:T(8,128)(2,1)S(1)}, u32[]{:S(2)}, u32[]{:S(2)}) %collective-permute-start.34) | collective-permute-done | bytes 524320 | tf_op jit(solution)/shard_map/ppermute | solution.py:428
  232.9 10.5 %collective-permute-done.35.b = bf16[128,2048]{1,0:T(8,128)(2,1)} collective-permute-done((bf16[128,2048]{1,0:T(8,128)(2,1)}, bf16[128,2048]{1,0:T(8,128)(2,1)}, u32[]{:S(2)}, u32[]{:S(2)}) %collective-permute-start.35) | collective-permute-done | bytes 524320 | tf_op jit(solution)/shard_map/ppermute | solution.py:428
  253.2 18.8 %collective-permute-done.36 = bf16[256,2048]{1,0:T(8,128)(2,1)S(1)} collective-permute-done((bf16[256,2048]{1,0:T(8,128)(2,1)S(1)}, bf16[256,2048]{1,0:T(8,128)(2,1)S(1)}, u32[]{:S(2)}, u32[]{:S(2)}) %collective-permute-start.36) | collective-permute-done | bytes 1048608 | tf_op jit(solution)/shard_map/ppermute | solution.py:428
  279.0 5.4 collective-permute-done.38
  291.9 17.8 %fusion.135 = f32[2048,1536]{0,1:T(8,128)S(1)} fusion(bf16[2048,2048]{1,0:T(8,128)(2,1)} %constant_dynamic-update-slice_fusion.21, bf16[2048,1536]{1,0:T(8,128)(2,1)} %all-gather.9.cloned.1.call-done), kind=kOutput, calls=%fused_computation.315 | convolution fusion | flops 12884901888 | bytes 27262976 | tf_op jit(solution)/shard_map/dot_general | solution.py:40
  318.0 10.3 %convolution_convert_fusion.1 = bf16[768,2048]{1,0:T(8,128)(2,1)} fusion(bf16[2048,768]{0,1:T(8,128)(2,1)S(1)} %multiply_convert_fusion.2, bf16[2048,2048]{1,0:T(8,128)(2,1)} %copy-done.82), kind=kOutput, calls=%fused_computation.33 | convolution fusion | flops 6444023808 | bytes 14680064 | tf_op jit(solution)/shard_map/dot_general | solution.py:44
  328.6 18.0 %multiply_convert_fusion = (bf16[2048,768]{0,1:T(8,128)(2,1)S(1)}, bf16[2048,768]{0,1:T(8,128)(2,1)S(1)}) fusion(f32[2048,1536]{0,1:T(8,128)} %copy-done.35, bf16[2048,2048]{1,0:T(8,128)(2,1)} %copy-done.82, bf16[768,2048]{1,0:T(8,128)(2,1)} %all-gather.11.cloned.1.call-done), kind=kOutput, calls=%fused_computation.13 | convolution fusion | flops 6477053952 | bytes 30408704 | tf_op jit(solution)/shard_map/dot_general | solution.py:48
  346.5 7.6 %convolution_convert_fusion.6 = bf16[512,2048]{1,0:T(8,128)(2,1)} fusion(bf16[2048,1536]{1,0:T(8,128)(2,1)} %all-gather.9.cloned.1.call-done, bf16[2048,768]{0,1:T(8,128)(2,1)S(1)} %get-tuple-element.286, bf16[2048,768]{0,1:T(8,128)(2,1)S(1)} %get-tuple-element.285), kind=kOutput, calls=%fused_computation.54 | convolution fusion | flops 3225419776 | bytes 14680064 | tf_op jit(solution)/shard_map/dot_general | solution.py:48
  354.6 6.8 convolution_convert_fusion.5
  365.2 7.0 convert_add_fusion.2
  375.7 6.9 add_convert_fusion.4
  388.0 19.2 %convolution_convert_fusion = bf16[2048,1536]{1,0:T(8,128)(2,1)} fusion(bf16[2048,2048]{1,0:T(8,128)(2,1)} %constant_dynamic-update-slice_fusion.21, bf16[2048,1536]{0,1:T(8,128)(2,1)} %pad_maximum_fusion), kind=kOutput, calls=%fused_computation.10 | convolution fusion | flops 12888047616 | bytes 20971520 | tf_op jit(solution)/shard_map/dot_general | solution.py:44
  413.9 8.5 %collective-permute-done.51.b = bf16[128,2048]{1,0:T(8,128)(2,1)S(1)} collective-permute-done((bf16[128,2048]{1,0:T(8,128)(2,1)S(1)}, bf16[128,2048]{1,0:T(8,128)(2,1)S(1)}, u32[]{:S(2)}, u32[]{:S(2)}) %collective-permute-start.51) | collective-permute-done | bytes 524320 | tf_op jit(solution)/shard_map/ppermute | solution.py:428
  426.3 6.3 shard_map.276
  456.6 8.0 %collective-permute-done.52 = bf16[256,2048]{1,0:T(8,128)(2,1)} collective-permute-done((bf16[256,2048]{1,0:T(8,128)(2,1)S(1)}, bf16[256,2048]{1,0:T(8,128)(2,1)}, u32[]{:S(2)}, u32[]{:S(2)}) %collective-permute-start.52) | collective-permute-done | bytes 1048608 | tf_op jit(solution)/shard_map/ppermute | solution.py:428
  491.0 7.6 %multiply_convert_fusion.3 = (bf16[2048,384]{1,0:T(8,128)(2,1)}, f32[2048,384]{1,0:T(8,128)}) fusion(f32[2048,384]{1,0:T(8,128)S(1)} %copy-done.37, f32[2048,384]{1,0:T(8,128)S(1)} %copy-done.33, bf16[2048,2048]{1,0:T(8,128)(2,1)S(1)} %constant_dynamic-update-slice_fusion.30, bf16[2048,64]{1,0:T(8,128)(2,1)S(1)} %copy-done.77, ...), kind=kOutput, calls=%fused_computation.49 | convolution fusion | flops 3241672704 | bytes 20709376 | tf_op jit(solution)/shard_map/dot_general | solution.py:40
  498.5 10.1 %shard_map.277 = (f32[2048,384]{1,0:T(8,128)S(1)}, f32[2048,384]{1,0:T(8,128)}, f32[32,384]{1,0:T(8,128)S(1)}) custom-call(s32[1]{0:T(128)} %bitcast.core_ref, f32[2048,384]{1,0:T(8,128)} %get-tuple-element.159.decay_ref, f32[2048,384]{1,0:T(8,128)} %get-tuple-element.349.grad_ref, f32[2048,384]{1,0:T(8,128)} %copy-done.36), custom_call_target="tpu_custom_call" | custom-call | tf_op jit(solution)/shard_map/pallas_call | solution.py:407
  508.7 8.7 %convolution_convert_fusion.11 = bf16[2048,384]{0,1:T(8,128)(2,1)S(1)} fusion(bf16[2048,2048]{1,0:T(8,128)(2,1)} %shard_map.273, bf16[2048,384]{1,0:T(8,128)(2,1)S(1)} %copy-done.83), kind=kOutput, calls=%fused_computation.60 | convolution fusion | flops 3222011904 | bytes 11534336 | tf_op jit(solution)/shard_map/dot_general | solution.py:44
  543.8 20.9 %shard_map.278 = (bf16[2048,512]{1,0:T(8,128)(2,1)S(1)}, f32[64,512]{1,0:T(8,128)S(1)}, f32[32,512]{1,0:T(8,128)S(1)}, f32[256,512]{1,0:T(8,128)S(1)}, f32[256,256]{1,0:T(8,128)S(1)}, /*index=5*/f32[8,512]{1,0:T(8,128)S(1)}) custom-call(s32[1]{0:T(128)} %bitcast.core_ref, bf16[2048,512]{1,0:T(8,128)(2,1)} %copy-done, bf16[2048,512]{1,0:T(8,128)(2,1)} %copy-done, ...), custom_call_target="tpu_custom_call" | custom-call | tf_op jit(solution)/shard_map/pallas_call | solution.py:407
  576.6 9.7 %convolution_convert_fusion.2 = bf16[2048,512]{1,0:T(8,128)(2,1)} fusion(bf16[2048,2048]{1,0:T(8,128)(2,1)} %shard_map.273, bf16[2048,512]{1,0:T(8,128)(2,1)S(1)} %bitcast.235), kind=kOutput, calls=%fused_computation.50 | convolution fusion | flops 4296015872 | bytes 12582912 | tf_op jit(solution)/shard_map/dot_general | solution.py:44
  642.8 8.7 %all-to-all-start.6 = ((f32[32,1,704]{2,1,0:T(1,128)}), f32[32,1,704]{2,1,0:T(1,128)S(1)}, u32[]{:S(2)}, u32[]{:S(2)}) async-start(f32[32,1,704]{2,1,0:T(1,128)} %copy.120), calls=%async_computation.10 | async-start | bytes 196608 | tf_op jit(solution)/shard_map/all_to_all | solution.py:847
  653.7 5.2 shard_map.281
  684.8 11.8 %all-to-all-done.5 = bf16[8,168,512]{2,1,0:T(8,128)(2,1)S(1)} async-done(((bf16[8,168,512]{2,1,0:T(8,128)(2,1)}), bf16[8,168,512]{2,1,0:T(8,128)(2,1)S(1)}, u32[]{:S(2)}, u32[]{:S(2)}) %all-to-all-start.5) | async-done | bytes 1376288 | tf_op jit(solution)/shard_map/all_to_all | solution.py:520
  (671 shorter events, 353.3 us)
Async XLA Ops:
  7.2 119.8 %all-gather.5.cloned.1.call-start = ((), (), s32[]{:S(2)}) async-start(), calls=%async_computation.11 | async-start | bytes 2621440 | tf_op jit(solution)/shard_map/all_gather | solution.py:530
  24.8 59.0 %collective-permute-start.9 = (bf16[256,2048]{1,0:T(8,128)(2,1)S(1)}, bf16[256,2048]{1,0:T(8,128)(2,1)S(1)}, u32[]{:S(2)}, u32[]{:S(2)}) collective-permute-start(bf16[256,2048]{1,0:T(8,128)(2,1)S(1)} %bitcast.228), channel_id=1, source_target_pairs={{0,16},{8,24},{16,0},{24,8},{1,17},{9,25},{17,1},{25,9},{2,18},{10... | collective-permute-start | bytes 3145736 | tf_op jit(solution)/shard_map/ppermute | solution.py:428
  25.5 58.5 %collective-permute-start.8 = (bf16[256,2048]{1,0:T(8,128)(2,1)S(1)}, bf16[256,2048]{1,0:T(8,128)(2,1)}, u32[]{:S(2)}, u32[]{:S(2)}) collective-permute-start(bf16[256,2048]{1,0:T(8,128)(2,1)S(1)} %bitcast.229), channel_id=1, source_target_pairs={{0,8},{8,0},{16,24},{24,16},{1,9},{9,1},{17,25},{25,17},{2,10},{10... | collective-permute-start | bytes 3145736 | tf_op jit(solution)/shard_map/ppermute | solution.py:428
  56.0 117.3 %all-gather.7.cloned.1.call-start = ((), (), s32[]{:S(2)}) async-start(), calls=%async_computation.12 | async-start | bytes 3276800 | tf_op jit(solution)/shard_map/all_gather | solution.py:530
  62.1 26.4 %collective-permute-start.4 = (bf16[768,256]{1,0:T(8,128)(2,1)}, bf16[768,256]{1,0:T(8,128)(2,1)S(1)}, u32[]{:S(2)}, u32[]{:S(2)}) collective-permute-start(bf16[768,256]{1,0:T(8,128)(2,1)} %all_gather.15), channel_id=1, source_target_pairs={{0,1},{1,0},{2,3},{3,2},{4,5},{5,4},{6,7},{7,6},{8,9},{9,8},{10,11... | collective-permute-start | bytes 1179656 | tf_op jit(solution)/shard_map/ppermute | solution.py:431
  83.8 30.3 %collective-permute-start.12 = (bf16[256,2048]{1,0:T(8,128)(2,1)S(1)}, bf16[256,2048]{1,0:T(8,128)(2,1)}, u32[]{:S(2)}, u32[]{:S(2)}) collective-permute-start(bf16[256,2048]{1,0:T(8,128)(2,1)S(1)} %bitcast.230), channel_id=1, source_target_pairs={{0,1},{1,0},{2,3},{3,2},{4,5},{5,4},{6,7},{7,6},{8,9},{9,8},{10,11... | collective-permute-start | bytes 3145736 | tf_op jit(solution)/shard_map/ppermute | solution.py:431
  106.6 28.9 %all-to-all-start.2 = ((bf16[8,64,1536]{2,1,0:T(8,128)(2,1)}), bf16[8,64,1536]{2,1,0:T(8,128)(2,1)}, u32[]{:S(2)}, u32[]{:S(2)}) async-start(bf16[8,64,1536]{2,1,0:T(8,128)(2,1)} %shard_map.271), calls=%async_computation.2 | async-start | bytes 3145728 | tf_op jit(solution)/shard_map/all_to_all | solution.py:520
  110.9 181.0 %all-gather.9.cloned.1.call-start = ((), (), s32[]{:S(2)}) async-start(), calls=%async_computation.13 | async-start | bytes 7864320 | tf_op jit(solution)/shard_map/all_gather | solution.py:530
  135.5 193.0 %all-gather.11.cloned.1.call-start = ((), (), s32[]{:S(2)}) async-start(), calls=%async_computation.14 | async-start | bytes 3932160 | tf_op jit(solution)/shard_map/all_gather | solution.py:530
  139.7 31.5 %collective-permute-start.20 = (bf16[256,2048]{1,0:T(8,128)(2,1)}, bf16[256,2048]{1,0:T(8,128)(2,1)S(1)}, u32[]{:S(2)}, u32[]{:S(2)}) collective-permute-start(bf16[256,2048]{1,0:T(8,128)(2,1)} %bitcast.1.cot_ref), channel_id=1, source_target_pairs={{0,8},{8,0},{16,24},{24,16},{1,9},{9,1},{17,25},{25,17},{2,10},{10... | collective-permute-start | bytes 3145736 | tf_op jit(solution)/shard_map/ppermute | solution.py:428
  141.6 29.6 %collective-permute-start.21 = (bf16[256,2048]{1,0:T(8,128)(2,1)}, bf16[256,2048]{1,0:T(8,128)(2,1)S(1)}, u32[]{:S(2)}, u32[]{:S(2)}) collective-permute-start(bf16[256,2048]{1,0:T(8,128)(2,1)} %bitcast.1.cot_ref), channel_id=1, source_target_pairs={{0,16},{8,24},{16,0},{24,8},{1,17},{9,25},{17,1},{25,9},{2,18},{10... | collective-permute-start | bytes 3145736 | tf_op jit(solution)/shard_map/ppermute | solution.py:428
  147.5 50.3 %collective-permute-start.24 = (bf16[256,2048]{1,0:T(8,128)(2,1)}, bf16[256,2048]{1,0:T(8,128)(2,1)}, u32[]{:S(2)}, u32[]{:S(2)}) collective-permute-start(bf16[256,2048]{1,0:T(8,128)(2,1)} %bitcast.1.cot_ref), channel_id=1, source_target_pairs={{0,1},{1,0},{2,3},{3,2},{4,5},{5,4},{6,7},{7,6},{8,9},{9,8},{10,11... | collective-permute-start | bytes 3145736 | tf_op jit(solution)/shard_map/ppermute | solution.py:431
  207.3 24.7 %collective-permute-start.33 = (bf16[128,2048]{1,0:T(8,128)(2,1)}, bf16[128,2048]{1,0:T(8,128)(2,1)S(1)}, u32[]{:S(2)}, u32[]{:S(2)}) collective-permute-start(bf16[128,2048]{1,0:T(8,128)(2,1)} %get-tuple-element.304), channel_id=1, source_target_pairs={{0,16},{8,24},{16,0},{24,8},{1,17},{9,25},{17,1},{25,9},{2,18},{10... | collective-permute-start | bytes 1572872 | tf_op jit(solution)/shard_map/ppermute | solution.py:428
  224.0 163.9 %reduce-scatter.5.cloned.1.call-start = ((), (), s32[]{:S(2)}) async-start(), calls=%async_computation.15 | async-start | bytes 3932160 | tf_op jit(solution)/shard_map/reduce_scatter | solution.py:527
  247.7 24.3 %collective-permute-start.36 = (bf16[256,2048]{1,0:T(8,128)(2,1)S(1)}, bf16[256,2048]{1,0:T(8,128)(2,1)S(1)}, u32[]{:S(2)}, u32[]{:S(2)}) collective-permute-start(bf16[256,2048]{1,0:T(8,128)(2,1)S(1)} %get-tuple-element.165), channel_id=1, source_target_pairs={{0,8},{8,0},{16,24},{24,16},{1,9},{9,1},{17,25},{25,17},{2,10},{10... | collective-permute-start | bytes 3145736 | tf_op jit(solution)/shard_map/ppermute | solution.py:428
  328.3 195.0 %reduce-scatter.7.cloned.1.call-start = ((), (), s32[]{:S(2)}) async-start(), calls=%async_computation.16 | async-start | bytes 7864320 | tf_op jit(solution)/shard_map/reduce_scatter | solution.py:527
  385.1 24.6 %collective-permute-start.47 = (bf16[128,2048]{1,0:T(8,128)(2,1)}, bf16[128,2048]{1,0:T(8,128)(2,1)}, u32[]{:S(2)}, u32[]{:S(2)}) collective-permute-start(bf16[128,2048]{1,0:T(8,128)(2,1)} %get-tuple-element.302), channel_id=1, source_target_pairs={{0,8},{8,0},{16,24},{24,16},{1,9},{9,1},{17,25},{25,17},{2,10},{10... | collective-permute-start | bytes 1572872 | tf_op jit(solution)/shard_map/ppermute | solution.py:428
  385.6 26.7 %collective-permute-start.49 = (bf16[128,2048]{1,0:T(8,128)(2,1)}, bf16[128,2048]{1,0:T(8,128)(2,1)S(1)}, u32[]{:S(2)}, u32[]{:S(2)}) collective-permute-start(bf16[128,2048]{1,0:T(8,128)(2,1)} %get-tuple-element.301), channel_id=1, source_target_pairs={{0,16},{8,24},{16,0},{24,8},{1,17},{9,25},{17,1},{25,9},{2,18},{10... | collective-permute-start | bytes 1572872 | tf_op jit(solution)/shard_map/ppermute | solution.py:428
  386.5 26.6 %collective-permute-start.45 = (bf16[128,2048]{1,0:T(8,128)(2,1)}, bf16[128,2048]{1,0:T(8,128)(2,1)S(1)}, u32[]{:S(2)}, u32[]{:S(2)}) collective-permute-start(bf16[128,2048]{1,0:T(8,128)(2,1)} %slice.1071), channel_id=1, source_target_pairs={{0,8},{8,0},{16,24},{24,16},{1,9},{9,1},{17,25},{25,17},{2,10},{10... | collective-permute-start | bytes 1572872 | tf_op jit(solution)/shard_map/ppermute | solution.py:428
  407.2 169.3 %reduce-scatter.9.cloned.1.call-start = ((), (), s32[]{:S(2)}) async-start(), calls=%async_computation.17 | async-start | bytes 3276800 | tf_op jit(solution)/shard_map/reduce_scatter | solution.py:527
  439.4 25.2 %collective-permute-start.52 = (bf16[256,2048]{1,0:T(8,128)(2,1)S(1)}, bf16[256,2048]{1,0:T(8,128)(2,1)}, u32[]{:S(2)}, u32[]{:S(2)}) collective-permute-start(bf16[256,2048]{1,0:T(8,128)(2,1)S(1)} %get-tuple-element.182), channel_id=1, source_target_pairs={{0,8},{8,0},{16,24},{24,16},{1,9},{9,1},{17,25},{25,17},{2,10},{10... | collective-permute-start | bytes 3145736 | tf_op jit(solution)/shard_map/ppermute | solution.py:428
  440.8 24.9 %collective-permute-start.53 = (bf16[256,2048]{1,0:T(8,128)(2,1)S(1)}, bf16[256,2048]{1,0:T(8,128)(2,1)}, u32[]{:S(2)}, u32[]{:S(2)}) collective-permute-start(bf16[256,2048]{1,0:T(8,128)(2,1)S(1)} %get-tuple-element.182), channel_id=1, source_target_pairs={{0,16},{8,24},{16,0},{24,8},{1,17},{9,25},{17,1},{25,9},{2,18},{10... | collective-permute-start | bytes 3145736 | tf_op jit(solution)/shard_map/ppermute | solution.py:428
  479.5 29.1 %collective-permute-start.66 = (bf16[128,2048]{1,0:T(8,128)(2,1)}, bf16[128,2048]{1,0:T(8,128)(2,1)S(1)}, u32[]{:S(2)}, u32[]{:S(2)}) collective-permute-start(bf16[128,2048]{1,0:T(8,128)(2,1)} %slice.823), channel_id=1, source_target_pairs={{0,16},{8,24},{16,0},{24,8},{1,17},{9,25},{17,1},{25,9},{2,18},{10... | collective-permute-start | bytes 1572872 | tf_op jit(solution)/shard_map/ppermute | solution.py:428
  481.9 26.7 %collective-permute-start.65 = (bf16[128,2048]{1,0:T(8,128)(2,1)}, bf16[128,2048]{1,0:T(8,128)(2,1)S(1)}, u32[]{:S(2)}, u32[]{:S(2)}) collective-permute-start(bf16[128,2048]{1,0:T(8,128)(2,1)} %slice.1070), channel_id=1, source_target_pairs={{0,8},{8,0},{16,24},{24,16},{1,9},{9,1},{17,25},{25,17},{2,10},{10... | collective-permute-start | bytes 1572872 | tf_op jit(solution)/shard_map/ppermute | solution.py:428
  539.3 47.0 %all-to-all-start.3 = ((bf16[8,64,1536]{2,1,0:T(8,128)(2,1)}), bf16[8,64,1536]{2,1,0:T(8,128)(2,1)}, u32[]{:S(2)}, u32[]{:S(2)}) async-start(bf16[8,64,1536]{2,1,0:T(8,128)(2,1)} %bitcast.260), calls=%async_computation.6 | async-start | bytes 3145728 | tf_op jit(solution)/shard_map/all_to_all | solution.py:520
  543.6 127.1 %reduce-scatter.11.cloned.1.call-start = ((), (), s32[]{:S(2)}) async-start(), calls=%async_computation.18 | async-start | bytes 3645440 | tf_op jit(solution)/shard_map/reduce_scatter | solution.py:527
  616.6 26.2 %all-to-all-start.4 = ((bf16[8,64,640]{2,1,0:T(8,128)(2,1)}), bf16[8,64,640]{2,1,0:T(8,128)(2,1)}, u32[]{:S(2)}, u32[]{:S(2)}) async-start(bf16[8,64,640]{2,1,0:T(8,128)(2,1)} %bitcast.253), calls=%async_computation.7 | async-start | bytes 1310720 | tf_op jit(solution)/shard_map/all_to_all | solution.py:520
  620.9 30.6 %collective-permute-start.77 = (bf16[128,2048]{1,0:T(8,128)(2,1)}, bf16[128,2048]{1,0:T(8,128)(2,1)}, u32[]{:S(2)}, u32[]{:S(2)}) collective-permute-start(bf16[128,2048]{1,0:T(8,128)(2,1)} %get-tuple-element.296), channel_id=1, source_target_pairs={{0,16},{8,24},{16,0},{24,8},{1,17},{9,25},{17,1},{25,9},{2,18},{10... | collective-permute-start | bytes 1572872 | tf_op jit(solution)/shard_map/ppermute | solution.py:428
  622.9 28.7 %collective-permute-start.73 = (bf16[128,2048]{1,0:T(8,128)(2,1)}, bf16[128,2048]{1,0:T(8,128)(2,1)}, u32[]{:S(2)}, u32[]{:S(2)}) collective-permute-start(bf16[128,2048]{1,0:T(8,128)(2,1)} %slice.1069), channel_id=1, source_target_pairs={{0,8},{8,0},{16,24},{24,16},{1,9},{9,1},{17,25},{25,17},{2,10},{10... | collective-permute-start | bytes 1572872 | tf_op jit(solution)/shard_map/ppermute | solution.py:428
  626.6 27.1 %collective-permute-start.79 = (bf16[128,2048]{1,0:T(8,128)(2,1)}, bf16[128,2048]{1,0:T(8,128)(2,1)}, u32[]{:S(2)}, u32[]{:S(2)}) collective-permute-start(bf16[128,2048]{1,0:T(8,128)(2,1)} %fusion.35), channel_id=1, source_target_pairs={{0,8},{8,0},{16,24},{24,16},{1,9},{9,1},{17,25},{25,17},{2,10},{10... | collective-permute-start | bytes 1572872 | tf_op jit(solution)/shard_map/ppermute | solution.py:428
  629.3 24.4 %collective-permute-start.76 = (bf16[128,2048]{1,0:T(8,128)(2,1)}, bf16[128,2048]{1,0:T(8,128)(2,1)}, u32[]{:S(2)}, u32[]{:S(2)}) collective-permute-start(bf16[128,2048]{1,0:T(8,128)(2,1)} %add_convert_fusion.6), channel_id=1, source_target_pairs={{0,16},{8,24},{16,0},{24,8},{1,17},{9,25},{17,1},{25,9},{2,18},{10... | collective-permute-start | bytes 1572872 | tf_op jit(solution)/shard_map/ppermute | solution.py:428
  642.8 25.8 %all-to-all-start.6 = ((f32[32,1,704]{2,1,0:T(1,128)}), f32[32,1,704]{2,1,0:T(1,128)S(1)}, u32[]{:S(2)}, u32[]{:S(2)}) async-start(f32[32,1,704]{2,1,0:T(1,128)} %copy.120), calls=%async_computation.10 | async-start | bytes 196608 | tf_op jit(solution)/shard_map/all_to_all | solution.py:847
  (168 other events, 1783.3 us)
Sparse Core Ops, SparseCore 0:
  24.9 51.6 all-gather.4
  83.9 53.8 all-gather.6
  139.4 114.1 all-gather.8
  255.0 62.5 all-gather.10
  328.4 58.2 reduce-scatter.4
  407.3 109.5 reduce-scatter.6
  523.5 52.1 reduce-scatter.8
  595.5 60.5 reduce-scatter.10

commit v6 on v5

--- a/solution.py
+++ b/solution.py
@@ -676,7 +676,7 @@
     down_sum = sum_z(down_terms)
     down_out = down_sum.astype(F32)
     terms = plane.terms(lambda lo, hi: dot_cols(fgrad[lo:hi], w_ff), rows)
-    ff_terms = dot_rows(fnormed, after(fgrad, down_sum, *terms)).astype(BF)
+    ff_terms = dot_rows(fnormed, after(fgrad, *terms)).astype(BF)
     terms = plane.add_up(terms)
     ff_sum = sum_z(after(ff_terms, down_sum))
     terms = (after(terms[0], down_sum, ff_terms), *terms[1:])

time: 718 us -> 735 us (1.024)
  waiting for transfers between devices: 125 us -> 141 us
    reduce_scatter x4, waiting for transfers between devices: 0.04 us -> 9.35 us  [sum_z(): return lax.psum_scatter(x, 'z', scatter_dimension=0, tiled=True)]
    unnamed x243 -> x251, local copies, waits for them, and re-layouts: 52.6 us -> 53.9 us
  transfers between devices with their start and end apart: 97 -> 97, of which waited for: 27 -> 30; matrix products, arithmetic and copies ran while one was open for 42% -> 37% of each run, Pallas kernels for 11% -> 11%
where the time goes in v6:
time: 735 us; the launch traced here: 728 us
  matrix products  177 us (24%)
  waiting for transfers between devices  141 us (19%)
  local copies, waits for them, and re-layouts  116 us (16%)
  starting transfers between devices  111 us (15%)
  Pallas kernels  78.5 us (11%)
  other arithmetic  51.6 us (7%)
  blocking collectives  35.3 us (5%)
  between operations  17.4 us (2%)
    ppermute x44, waiting for transfers between devices, near(): return lax.ppermute(x, 'dp', [(i, i ^ k) for i in range(self.n_dp)])  106 us
    dot_general x17, matrix products, dot_cols(): lax.dot_general(a, b, (((1,), (1,)), ((), ())), preferred_element_type=F32)  72.1 us
    dot_general x8, matrix products, dot(): lax.dot_general(a, b, (((1,), (0,)), ((), ())), preferred_element_type=F32)  55.8 us
    unnamed x251, local copies, waits for them, and re-layouts  53.9 us
    dot_general x5, matrix products, dot_rows(): lax.dot_general(a, b, (((0,), (0,)), ((), ())), preferred_element_type=F32)  48.6 us
    ppermute x44, starting transfers between devices, near(): return lax.ppermute(x, 'dp', [(i, i ^ k) for i in range(self.n_dp)])  48.5 us
    pallas_call x3, Pallas kernels, call(): pl.pallas_call(kernel, grid_spec=pltpu.PrefetchScalarGridSpec(num_scalar_...  43.4 us
    all_gather x1, blocking collectives, over_z(): return lax.all_gather(x, 'z', axis=0, tiled=True)  20.3 us
  transfers between devices with their start and end apart: 97, of which 30 were waited for; matrix products, arithmetic and copies ran while one was open for 37% of the time, Pallas kernels for 11%

profile of v6, /device:TPU:0, one launch (start us, length us, event | category | flops | bytes accessed | tf_op | source)
XLA Modules:
  0.0 727.7 jit_solution(5055607801225989379)
XLA Ops:
  9.8 14.9 %all_to_all.66 = bf16[8,64,512]{2,1,0:T(8,128)(2,1)} all-to-all(bf16[8,64,512]{2,1,0:T(8,128)(2,1)S(1)} %copy.95), channel_id=1, replica_groups=mesh['dp'=4,'z'=4,'core'=2] {'dp','core'}, dimensions={0} | all-to-all | bytes 1048576 | tf_op jit(solution)/shard_map/all_to_all | solution.py:520
  32.0 20.3 %all_gather.15 = bf16[768,256]{1,0:T(8,128)(2,1)} all-gather(bf16[192,256]{1,0:T(8,128)(2,1)S(1)} %fusion.81), channel_id=1, replica_groups=mesh['dp'=4,'z'=4,'core'=2] {'z'}, dimensions={0}, use_global_device_ids=true | all-gather | bytes 491520 | tf_op jit(solution)/shard_map/all_gather | solution.py:530
  63.9 10.8 %collective-permute-done = bf16[768,256]{1,0:T(8,128)(2,1)} collective-permute-done((bf16[768,256]{1,0:T(8,128)(2,1)}, bf16[768,256]{1,0:T(8,128)(2,1)}, u32[]{:S(2)}, u32[]{:S(2)}) %collective-permute-start) | collective-permute-done | bytes 393248 | tf_op jit(solution)/shard_map/ppermute | solution.py:428
  92.1 8.6 %collective-permute-done.10 = bf16[128,2048]{1,0:T(8,128)(2,1)S(1)} collective-permute-done((bf16[128,2048]{1,0:T(8,128)(2,1)S(1)}, bf16[128,2048]{1,0:T(8,128)(2,1)S(1)}, u32[]{:S(2)}, u32[]{:S(2)}) %collective-permute-start.10) | collective-permute-done | bytes 524320 | tf_op jit(solution)/shard_map/ppermute | solution.py:428
  114.7 9.3 %shard_map.273 = bf16[2048,2048]{1,0:T(8,128)(2,1)} custom-call(f32[1,2048]{1,0:T(1,128)S(1)} %reshape_reshape.15.gain_ref, bf16[256,2048]{1,0:T(8,128)(2,1)S(1)} %bitcast.231, bf16[256,2048]{1,0:T(8,128)(2,1)} %collective-permute-done.8.refs_1_, bf16[256,2048]{1,0:T(8,128)(2,1)S(1)} %collective-permute-done.9.refs_2_, ...), custom_call_target="tpu_custom_call" | custom-call | tf_op jit(solution)/shard_map/pallas_call | solution.py:598
  127.0 8.5 %convolution_convert_fusion.9.inner_ref.prev_ref = bf16[2048,512]{1,0:T(8,128)(2,1)S(1)} fusion(bf16[2048,2048]{1,0:T(8,128)(2,1)} %shard_map.273, bf16[2048,512]{1,0:T(8,128)(2,1)} %all-gather.5.cloned.1.call-done), kind=kOutput, calls=%fused_computation.57 | convolution fusion | flops 4296015872 | bytes 12582912 | tf_op jit(solution)/shard_map/dot_general | solution.py:40
  150.4 12.4 %shard_map.274 = (f32[2048,384]{1,0:T(8,128)}, f32[2048,384]{1,0:T(8,128)}, f32[2048,384]{1,0:T(8,128)}, f32[32,384]{1,0:T(8,128)S(1)}) custom-call(s32[1]{0:T(128)} %bitcast.core_ref, bf16[2048,512]{1,0:T(8,128)(2,1)S(1)} %convolution_convert_fusion.9.inner_ref.prev_ref, bf16[2048,512]{1,0:T(8,128)(2,1)S(1)} %convolution_convert_fusion.9.inner_ref.prev_ref, ...), custom_call_target="tpu_custom_call" | custom-call | tf_op jit(solution)/shard_map/pallas_call | solution.py:407
  162.8 6.1 collective-permute-start.19
  176.3 6.0 collective-permute-done.22
  187.7 7.1 fusion.115.branch_ref
  212.3 8.4 %collective-permute-done.34 = bf16[128,2048]{1,0:T(8,128)(2,1)S(1)} collective-permute-done((bf16[128,2048]{1,0:T(8,128)(2,1)S(1)}, bf16[128,2048]{1,0:T(8,128)(2,1)S(1)}, u32[]{:S(2)}, u32[]{:S(2)}) %collective-permute-start.34) | collective-permute-done | bytes 524320 | tf_op jit(solution)/shard_map/ppermute | solution.py:428
  232.8 10.5 %collective-permute-done.35.b = bf16[128,2048]{1,0:T(8,128)(2,1)} collective-permute-done((bf16[128,2048]{1,0:T(8,128)(2,1)}, bf16[128,2048]{1,0:T(8,128)(2,1)}, u32[]{:S(2)}, u32[]{:S(2)}) %collective-permute-start.35) | collective-permute-done | bytes 524320 | tf_op jit(solution)/shard_map/ppermute | solution.py:428
  253.2 18.8 %collective-permute-done.36 = bf16[256,2048]{1,0:T(8,128)(2,1)S(1)} collective-permute-done((bf16[256,2048]{1,0:T(8,128)(2,1)S(1)}, bf16[256,2048]{1,0:T(8,128)(2,1)S(1)}, u32[]{:S(2)}, u32[]{:S(2)}) %collective-permute-start.36) | collective-permute-done | bytes 1048608 | tf_op jit(solution)/shard_map/ppermute | solution.py:428
  291.9 17.8 %fusion.135 = f32[2048,1536]{0,1:T(8,128)S(1)} fusion(bf16[2048,2048]{1,0:T(8,128)(2,1)} %constant_dynamic-update-slice_fusion.21, bf16[2048,1536]{1,0:T(8,128)(2,1)} %all-gather.9.cloned.1.call-done), kind=kOutput, calls=%fused_computation.315 | convolution fusion | flops 12884901888 | bytes 27262976 | tf_op jit(solution)/shard_map/dot_general | solution.py:40
  318.0 10.3 %convolution_convert_fusion.1 = bf16[768,2048]{1,0:T(8,128)(2,1)} fusion(bf16[2048,768]{0,1:T(8,128)(2,1)S(1)} %multiply_convert_fusion.2, bf16[2048,2048]{1,0:T(8,128)(2,1)} %copy-done.86), kind=kOutput, calls=%fused_computation.33 | convolution fusion | flops 6444023808 | bytes 14680064 | tf_op jit(solution)/shard_map/dot_general | solution.py:44
  328.3 17.5 %multiply_convert_fusion = (bf16[2048,768]{0,1:T(8,128)(2,1)S(1)}, bf16[2048,768]{0,1:T(8,128)(2,1)S(1)}) fusion(f32[2048,1536]{0,1:T(8,128)} %copy-done.35, bf16[2048,2048]{1,0:T(8,128)(2,1)} %copy-done.86, bf16[768,2048]{1,0:T(8,128)(2,1)} %all-gather.11.cloned.1.call-done), kind=kOutput, calls=%fused_computation.13 | convolution fusion | flops 6477053952 | bytes 30408704 | tf_op jit(solution)/shard_map/dot_general | solution.py:48
  345.9 9.8 %convolution_convert_fusion.6 = bf16[512,2048]{1,0:T(8,128)(2,1)} fusion(bf16[2048,1536]{1,0:T(8,128)(2,1)} %all-gather.9.cloned.1.call-done, bf16[2048,768]{0,1:T(8,128)(2,1)S(1)} %get-tuple-element.286, bf16[2048,768]{0,1:T(8,128)(2,1)S(1)} %get-tuple-element.285), kind=kOutput, calls=%fused_computation.54 | convolution fusion | flops 3225419776 | bytes 14680064 | tf_op jit(solution)/shard_map/dot_general | solution.py:48
  356.1 7.5 %convolution_convert_fusion.5 = bf16[512,2048]{1,0:T(8,128)(2,1)} fusion(bf16[2048,1536]{1,0:T(8,128)(2,1)} %all-gather.9.cloned.1.call-done, bf16[2048,768]{0,1:T(8,128)(2,1)S(1)} %get-tuple-element.286, bf16[2048,768]{0,1:T(8,128)(2,1)S(1)} %get-tuple-element.285), kind=kOutput, calls=%fused_computation.53 | convolution fusion | flops 3225419776 | bytes 14680064 | tf_op jit(solution)/shard_map/dot_general | solution.py:48
  367.9 7.2 convert_add_fusion.2
  379.7 7.1 add_convert_fusion.4
  391.6 17.3 %convolution_convert_fusion = bf16[2048,1536]{1,0:T(8,128)(2,1)} fusion(bf16[2048,2048]{1,0:T(8,128)(2,1)} %constant_dynamic-update-slice_fusion.21, bf16[2048,1536]{0,1:T(8,128)(2,1)S(1)} %pad_maximum_fusion), kind=kOutput, calls=%fused_computation.10 | convolution fusion | flops 12888047616 | bytes 20971520 | tf_op jit(solution)/shard_map/dot_general | solution.py:44
  412.7 9.3 %reduce-scatter.5.cloned.1.call-done = bf16[192,2048]{1,0:T(8,128)(2,1)} async-done(((bf16[768,2048]{1,0:T(8,128)(2,1)}), bf16[192,2048]{1,0:T(8,128)(2,1)}) %reduce-scatter.5.cloned.1.call-update) | async-done | bytes 786448 | tf_op jit(solution)/shard_map/reduce_scatter | solution.py:527
  429.6 7.6 %collective-permute-done.51.b = bf16[128,2048]{1,0:T(8,128)(2,1)S(1)} collective-permute-done((bf16[128,2048]{1,0:T(8,128)(2,1)S(1)}, bf16[128,2048]{1,0:T(8,128)(2,1)S(1)}, u32[]{:S(2)}, u32[]{:S(2)}) %collective-permute-start.51) | collective-permute-done | bytes 524320 | tf_op jit(solution)/shard_map/ppermute | solution.py:428
  441.9 6.3 shard_map.276
  471.7 8.6 %collective-permute-done.52 = bf16[256,2048]{1,0:T(8,128)(2,1)} collective-permute-done((bf16[256,2048]{1,0:T(8,128)(2,1)S(1)}, bf16[256,2048]{1,0:T(8,128)(2,1)}, u32[]{:S(2)}, u32[]{:S(2)}) %collective-permute-start.52) | collective-permute-done | bytes 1048608 | tf_op jit(solution)/shard_map/ppermute | solution.py:428
  503.6 7.6 %multiply_convert_fusion.3 = (bf16[2048,384]{1,0:T(8,128)(2,1)}, f32[2048,384]{1,0:T(8,128)}) fusion(f32[2048,384]{1,0:T(8,128)S(1)} %copy-done.37, f32[2048,384]{1,0:T(8,128)S(1)} %copy-done.33, bf16[2048,2048]{1,0:T(8,128)(2,1)S(1)} %constant_dynamic-update-slice_fusion.30, bf16[2048,64]{1,0:T(8,128)(2,1)S(1)} %copy-done.81, ...), kind=kOutput, calls=%fused_computation.49 | convolution fusion | flops 3241672704 | bytes 20709376 | tf_op jit(solution)/shard_map/dot_general | solution.py:40
  511.2 10.1 %shard_map.277 = (f32[2048,384]{1,0:T(8,128)S(1)}, f32[2048,384]{1,0:T(8,128)}, f32[32,384]{1,0:T(8,128)S(1)}) custom-call(s32[1]{0:T(128)} %bitcast.core_ref, f32[2048,384]{1,0:T(8,128)} %get-tuple-element.159.decay_ref, f32[2048,384]{1,0:T(8,128)} %get-tuple-element.349.grad_ref, f32[2048,384]{1,0:T(8,128)} %copy-done.36), custom_call_target="tpu_custom_call" | custom-call | tf_op jit(solution)/shard_map/pallas_call | solution.py:407
  524.3 7.5 %convolution_convert_fusion.11 = bf16[2048,384]{0,1:T(8,128)(2,1)S(1)} fusion(bf16[2048,2048]{1,0:T(8,128)(2,1)} %shard_map.273, bf16[2048,384]{1,0:T(8,128)(2,1)S(1)} %copy-done.87), kind=kOutput, calls=%fused_computation.60 | convolution fusion | flops 3222011904 | bytes 11534336 | tf_op jit(solution)/shard_map/dot_general | solution.py:44
  560.5 20.9 %shard_map.278 = (bf16[2048,512]{1,0:T(8,128)(2,1)S(1)}, f32[64,512]{1,0:T(8,128)S(1)}, f32[32,512]{1,0:T(8,128)S(1)}, f32[256,512]{1,0:T(8,128)S(1)}, f32[256,256]{1,0:T(8,128)S(1)}, /*index=5*/f32[8,512]{1,0:T(8,128)S(1)}) custom-call(s32[1]{0:T(128)} %bitcast.core_ref, bf16[2048,512]{1,0:T(8,128)(2,1)} %copy-done, bf16[2048,512]{1,0:T(8,128)(2,1)} %copy-done, ...), custom_call_target="tpu_custom_call" | custom-call | tf_op jit(solution)/shard_map/pallas_call | solution.py:407
  593.3 9.7 %convolution_convert_fusion.2 = bf16[2048,512]{1,0:T(8,128)(2,1)} fusion(bf16[2048,2048]{1,0:T(8,128)(2,1)} %shard_map.273, bf16[2048,512]{1,0:T(8,128)(2,1)S(1)} %bitcast.235), kind=kOutput, calls=%fused_computation.50 | convolution fusion | flops 4296015872 | bytes 12582912 | tf_op jit(solution)/shard_map/dot_general | solution.py:44
  659.6 8.8 %all-to-all-start.6 = ((f32[32,1,704]{2,1,0:T(1,128)}), f32[32,1,704]{2,1,0:T(1,128)S(1)}, u32[]{:S(2)}, u32[]{:S(2)}) async-start(f32[32,1,704]{2,1,0:T(1,128)} %copy.120), calls=%async_computation.10 | async-start | bytes 196608 | tf_op jit(solution)/shard_map/all_to_all | solution.py:847
  701.6 11.8 %all-to-all-done.5 = bf16[8,168,512]{2,1,0:T(8,128)(2,1)S(1)} async-done(((bf16[8,168,512]{2,1,0:T(8,128)(2,1)}), bf16[8,168,512]{2,1,0:T(8,128)(2,1)S(1)}, u32[]{:S(2)}, u32[]{:S(2)}) %all-to-all-start.5) | async-done | bytes 1376288 | tf_op jit(solution)/shard_map/all_to_all | solution.py:520
  (679 shorter events, 365.9 us)
Async XLA Ops:
  7.2 119.8 %all-gather.5.cloned.1.call-start = ((), (), s32[]{:S(2)}) async-start(), calls=%async_computation.11 | async-start | bytes 2621440 | tf_op jit(solution)/shard_map/all_gather | solution.py:530
  24.8 59.0 %collective-permute-start.9 = (bf16[256,2048]{1,0:T(8,128)(2,1)S(1)}, bf16[256,2048]{1,0:T(8,128)(2,1)S(1)}, u32[]{:S(2)}, u32[]{:S(2)}) collective-permute-start(bf16[256,2048]{1,0:T(8,128)(2,1)S(1)} %bitcast.228), channel_id=1, source_target_pairs={{0,16},{8,24},{16,0},{24,8},{1,17},{9,25},{17,1},{25,9},{2,18},{10... | collective-permute-start | bytes 3145736 | tf_op jit(solution)/shard_map/ppermute | solution.py:428
  25.5 58.5 %collective-permute-start.8 = (bf16[256,2048]{1,0:T(8,128)(2,1)S(1)}, bf16[256,2048]{1,0:T(8,128)(2,1)}, u32[]{:S(2)}, u32[]{:S(2)}) collective-permute-start(bf16[256,2048]{1,0:T(8,128)(2,1)S(1)} %bitcast.229), channel_id=1, source_target_pairs={{0,8},{8,0},{16,24},{24,16},{1,9},{9,1},{17,25},{25,17},{2,10},{10... | collective-permute-start | bytes 3145736 | tf_op jit(solution)/shard_map/ppermute | solution.py:428
  56.0 116.2 %all-gather.7.cloned.1.call-start = ((), (), s32[]{:S(2)}) async-start(), calls=%async_computation.12 | async-start | bytes 3276800 | tf_op jit(solution)/shard_map/all_gather | solution.py:530
  62.1 26.4 %collective-permute-start.4 = (bf16[768,256]{1,0:T(8,128)(2,1)}, bf16[768,256]{1,0:T(8,128)(2,1)S(1)}, u32[]{:S(2)}, u32[]{:S(2)}) collective-permute-start(bf16[768,256]{1,0:T(8,128)(2,1)} %all_gather.15), channel_id=1, source_target_pairs={{0,1},{1,0},{2,3},{3,2},{4,5},{5,4},{6,7},{7,6},{8,9},{9,8},{10,11... | collective-permute-start | bytes 1179656 | tf_op jit(solution)/shard_map/ppermute | solution.py:431
  83.8 30.3 %collective-permute-start.12 = (bf16[256,2048]{1,0:T(8,128)(2,1)S(1)}, bf16[256,2048]{1,0:T(8,128)(2,1)}, u32[]{:S(2)}, u32[]{:S(2)}) collective-permute-start(bf16[256,2048]{1,0:T(8,128)(2,1)S(1)} %bitcast.230), channel_id=1, source_target_pairs={{0,1},{1,0},{2,3},{3,2},{4,5},{5,4},{6,7},{7,6},{8,9},{9,8},{10,11... | collective-permute-start | bytes 3145736 | tf_op jit(solution)/shard_map/ppermute | solution.py:431
  90.0 24.1 %collective-permute-start.13 = (bf16[256,2048]{1,0:T(8,128)(2,1)}, bf16[256,2048]{1,0:T(8,128)(2,1)}, u32[]{:S(2)}, u32[]{:S(2)}) collective-permute-start(bf16[256,2048]{1,0:T(8,128)(2,1)} %collective-permute-done.8.refs_1_), channel_id=1, source_target_pairs={{0,1},{1,0},{2,3},{3,2},{4,5},{5,4},{6,7},{7,6},{8,9},{9,8},{10,11... | collective-permute-start | bytes 3145736 | tf_op jit(solution)/shard_map/ppermute | solution.py:431
  106.6 28.9 %all-to-all-start.2 = ((bf16[8,64,1536]{2,1,0:T(8,128)(2,1)}), bf16[8,64,1536]{2,1,0:T(8,128)(2,1)}, u32[]{:S(2)}, u32[]{:S(2)}) async-start(bf16[8,64,1536]{2,1,0:T(8,128)(2,1)} %shard_map.271), calls=%async_computation.2 | async-start | bytes 3145728 | tf_op jit(solution)/shard_map/all_to_all | solution.py:520
  110.9 181.0 %all-gather.9.cloned.1.call-start = ((), (), s32[]{:S(2)}) async-start(), calls=%async_computation.13 | async-start | bytes 7864320 | tf_op jit(solution)/shard_map/all_gather | solution.py:530
  135.5 192.8 %all-gather.11.cloned.1.call-start = ((), (), s32[]{:S(2)}) async-start(), calls=%async_computation.14 | async-start | bytes 3932160 | tf_op jit(solution)/shard_map/all_gather | solution.py:530
  139.7 30.5 %collective-permute-start.20 = (bf16[256,2048]{1,0:T(8,128)(2,1)}, bf16[256,2048]{1,0:T(8,128)(2,1)S(1)}, u32[]{:S(2)}, u32[]{:S(2)}) collective-permute-start(bf16[256,2048]{1,0:T(8,128)(2,1)} %bitcast.1.cot_ref), channel_id=1, source_target_pairs={{0,8},{8,0},{16,24},{24,16},{1,9},{9,1},{17,25},{25,17},{2,10},{10... | collective-permute-start | bytes 3145736 | tf_op jit(solution)/shard_map/ppermute | solution.py:428
  141.6 28.6 %collective-permute-start.21 = (bf16[256,2048]{1,0:T(8,128)(2,1)}, bf16[256,2048]{1,0:T(8,128)(2,1)S(1)}, u32[]{:S(2)}, u32[]{:S(2)}) collective-permute-start(bf16[256,2048]{1,0:T(8,128)(2,1)} %bitcast.1.cot_ref), channel_id=1, source_target_pairs={{0,16},{8,24},{16,0},{24,8},{1,17},{9,25},{17,1},{25,9},{2,18},{10... | collective-permute-start | bytes 3145736 | tf_op jit(solution)/shard_map/ppermute | solution.py:428
  147.5 50.4 %collective-permute-start.24 = (bf16[256,2048]{1,0:T(8,128)(2,1)}, bf16[256,2048]{1,0:T(8,128)(2,1)}, u32[]{:S(2)}, u32[]{:S(2)}) collective-permute-start(bf16[256,2048]{1,0:T(8,128)(2,1)} %bitcast.1.cot_ref), channel_id=1, source_target_pairs={{0,1},{1,0},{2,3},{3,2},{4,5},{5,4},{6,7},{7,6},{8,9},{9,8},{10,11... | collective-permute-start | bytes 3145736 | tf_op jit(solution)/shard_map/ppermute | solution.py:431
  162.8 24.2 %collective-permute-start.19 = (f32[4,2,384]{2,1,0:T(2,128)S(1)}, f32[4,2,384]{2,1,0:T(2,128)S(1)}, u32[]{:S(2)}, u32[]{:S(2)}) collective-permute-start(f32[4,2,384]{2,1,0:T(2,128)S(1)} %slice.787), channel_id=1, source_target_pairs={{0,6},{1,7},{8,14},{9,15},{16,22},{17,23},{24,30},{25,31}} | collective-permute-start | bytes 36872 | tf_op jit(solution)/shard_map/ppermute | solution.py:648
  207.3 24.7 %collective-permute-start.33 = (bf16[128,2048]{1,0:T(8,128)(2,1)}, bf16[128,2048]{1,0:T(8,128)(2,1)S(1)}, u32[]{:S(2)}, u32[]{:S(2)}) collective-permute-start(bf16[128,2048]{1,0:T(8,128)(2,1)} %get-tuple-element.304), channel_id=1, source_target_pairs={{0,16},{8,24},{16,0},{24,8},{1,17},{9,25},{17,1},{25,9},{2,18},{10... | collective-permute-start | bytes 1572872 | tf_op jit(solution)/shard_map/ppermute | solution.py:428
  224.0 198.1 %reduce-scatter.5.cloned.1.call-start = ((), (), s32[]{:S(2)}) async-start(), calls=%async_computation.15 | async-start | bytes 3932160 | tf_op jit(solution)/shard_map/reduce_scatter | solution.py:527
  247.7 24.3 %collective-permute-start.36 = (bf16[256,2048]{1,0:T(8,128)(2,1)S(1)}, bf16[256,2048]{1,0:T(8,128)(2,1)S(1)}, u32[]{:S(2)}, u32[]{:S(2)}) collective-permute-start(bf16[256,2048]{1,0:T(8,128)(2,1)S(1)} %get-tuple-element.165), channel_id=1, source_target_pairs={{0,8},{8,0},{16,24},{24,16},{1,9},{9,1},{17,25},{25,17},{2,10},{10... | collective-permute-start | bytes 3145736 | tf_op jit(solution)/shard_map/ppermute | solution.py:428
  363.7 173.9 %reduce-scatter.7.cloned.1.call-start = ((), (), s32[]{:S(2)}) async-start(), calls=%async_computation.16 | async-start | bytes 7864320 | tf_op jit(solution)/shard_map/reduce_scatter | solution.py:527
  389.3 32.9 %collective-permute-start.50 = (bf16[128,2048]{1,0:T(8,128)(2,1)}, bf16[128,2048]{1,0:T(8,128)(2,1)}, u32[]{:S(2)}, u32[]{:S(2)}) collective-permute-start(bf16[128,2048]{1,0:T(8,128)(2,1)} %get-tuple-element.300), channel_id=1, source_target_pairs={{0,16},{8,24},{16,0},{24,8},{1,17},{9,25},{17,1},{25,9},{2,18},{10... | collective-permute-start | bytes 1572872 | tf_op jit(solution)/shard_map/ppermute | solution.py:428
  390.8 34.4 %collective-permute-start.47 = (bf16[128,2048]{1,0:T(8,128)(2,1)}, bf16[128,2048]{1,0:T(8,128)(2,1)}, u32[]{:S(2)}, u32[]{:S(2)}) collective-permute-start(bf16[128,2048]{1,0:T(8,128)(2,1)} %get-tuple-element.302), channel_id=1, source_target_pairs={{0,8},{8,0},{16,24},{24,16},{1,9},{9,1},{17,25},{25,17},{2,10},{10... | collective-permute-start | bytes 1572872 | tf_op jit(solution)/shard_map/ppermute | solution.py:428
  422.1 171.2 %reduce-scatter.9.cloned.1.call-start = ((), (), s32[]{:S(2)}) async-start(), calls=%async_computation.17 | async-start | bytes 3276800 | tf_op jit(solution)/shard_map/reduce_scatter | solution.py:527
  455.1 25.2 %collective-permute-start.52 = (bf16[256,2048]{1,0:T(8,128)(2,1)S(1)}, bf16[256,2048]{1,0:T(8,128)(2,1)}, u32[]{:S(2)}, u32[]{:S(2)}) collective-permute-start(bf16[256,2048]{1,0:T(8,128)(2,1)S(1)} %get-tuple-element.182), channel_id=1, source_target_pairs={{0,8},{8,0},{16,24},{24,16},{1,9},{9,1},{17,25},{25,17},{2,10},{10... | collective-permute-start | bytes 3145736 | tf_op jit(solution)/shard_map/ppermute | solution.py:428
  455.7 24.9 %collective-permute-start.53 = (bf16[256,2048]{1,0:T(8,128)(2,1)S(1)}, bf16[256,2048]{1,0:T(8,128)(2,1)}, u32[]{:S(2)}, u32[]{:S(2)}) collective-permute-start(bf16[256,2048]{1,0:T(8,128)(2,1)S(1)} %get-tuple-element.182), channel_id=1, source_target_pairs={{0,16},{8,24},{16,0},{24,8},{1,17},{9,25},{17,1},{25,9},{2,18},{10... | collective-permute-start | bytes 3145736 | tf_op jit(solution)/shard_map/ppermute | solution.py:428
  494.4 26.9 %collective-permute-start.66 = (bf16[128,2048]{1,0:T(8,128)(2,1)}, bf16[128,2048]{1,0:T(8,128)(2,1)S(1)}, u32[]{:S(2)}, u32[]{:S(2)}) collective-permute-start(bf16[128,2048]{1,0:T(8,128)(2,1)} %slice.823), channel_id=1, source_target_pairs={{0,16},{8,24},{16,0},{24,8},{1,17},{9,25},{17,1},{25,9},{2,18},{10... | collective-permute-start | bytes 1572872 | tf_op jit(solution)/shard_map/ppermute | solution.py:428
  556.1 47.0 %all-to-all-start.3 = ((bf16[8,64,1536]{2,1,0:T(8,128)(2,1)}), bf16[8,64,1536]{2,1,0:T(8,128)(2,1)}, u32[]{:S(2)}, u32[]{:S(2)}) async-start(bf16[8,64,1536]{2,1,0:T(8,128)(2,1)} %bitcast.260), calls=%async_computation.6 | async-start | bytes 3145728 | tf_op jit(solution)/shard_map/all_to_all | solution.py:520
  560.4 127.1 %reduce-scatter.11.cloned.1.call-start = ((), (), s32[]{:S(2)}) async-start(), calls=%async_computation.18 | async-start | bytes 3645440 | tf_op jit(solution)/shard_map/reduce_scatter | solution.py:527
  633.4 26.3 %all-to-all-start.4 = ((bf16[8,64,640]{2,1,0:T(8,128)(2,1)}), bf16[8,64,640]{2,1,0:T(8,128)(2,1)}, u32[]{:S(2)}, u32[]{:S(2)}) async-start(bf16[8,64,640]{2,1,0:T(8,128)(2,1)} %bitcast.253), calls=%async_computation.7 | async-start | bytes 1310720 | tf_op jit(solution)/shard_map/all_to_all | solution.py:520
  637.7 30.7 %collective-permute-start.77 = (bf16[128,2048]{1,0:T(8,128)(2,1)}, bf16[128,2048]{1,0:T(8,128)(2,1)}, u32[]{:S(2)}, u32[]{:S(2)}) collective-permute-start(bf16[128,2048]{1,0:T(8,128)(2,1)} %get-tuple-element.296), channel_id=1, source_target_pairs={{0,16},{8,24},{16,0},{24,8},{1,17},{9,25},{17,1},{25,9},{2,18},{10... | collective-permute-start | bytes 1572872 | tf_op jit(solution)/shard_map/ppermute | solution.py:428
  639.6 28.8 %collective-permute-start.73 = (bf16[128,2048]{1,0:T(8,128)(2,1)}, bf16[128,2048]{1,0:T(8,128)(2,1)}, u32[]{:S(2)}, u32[]{:S(2)}) collective-permute-start(bf16[128,2048]{1,0:T(8,128)(2,1)} %slice.1069), channel_id=1, source_target_pairs={{0,8},{8,0},{16,24},{24,16},{1,9},{9,1},{17,25},{25,17},{2,10},{10... | collective-permute-start | bytes 1572872 | tf_op jit(solution)/shard_map/ppermute | solution.py:428
  643.4 27.0 %collective-permute-start.79 = (bf16[128,2048]{1,0:T(8,128)(2,1)}, bf16[128,2048]{1,0:T(8,128)(2,1)}, u32[]{:S(2)}, u32[]{:S(2)}) collective-permute-start(bf16[128,2048]{1,0:T(8,128)(2,1)} %fusion.35), channel_id=1, source_target_pairs={{0,8},{8,0},{16,24},{24,16},{1,9},{9,1},{17,25},{25,17},{2,10},{10... | collective-permute-start | bytes 1572872 | tf_op jit(solution)/shard_map/ppermute | solution.py:428
  646.1 24.3 %collective-permute-start.76 = (bf16[128,2048]{1,0:T(8,128)(2,1)}, bf16[128,2048]{1,0:T(8,128)(2,1)}, u32[]{:S(2)}, u32[]{:S(2)}) collective-permute-start(bf16[128,2048]{1,0:T(8,128)(2,1)} %add_convert_fusion.6), channel_id=1, source_target_pairs={{0,16},{8,24},{16,0},{24,8},{1,17},{9,25},{17,1},{25,9},{2,18},{10... | collective-permute-start | bytes 1572872 | tf_op jit(solution)/shard_map/ppermute | solution.py:428
  659.6 25.4 %all-to-all-start.6 = ((f32[32,1,704]{2,1,0:T(1,128)}), f32[32,1,704]{2,1,0:T(1,128)S(1)}, u32[]{:S(2)}, u32[]{:S(2)}) async-start(f32[32,1,704]{2,1,0:T(1,128)} %copy.120), calls=%async_computation.10 | async-start | bytes 196608 | tf_op jit(solution)/shard_map/all_to_all | solution.py:847
  (172 other events, 1813.2 us)
Sparse Core Ops, SparseCore 0:
  24.9 51.6 all-gather.4
  83.9 53.8 all-gather.6
  139.4 114.1 all-gather.8
  255.0 62.5 all-gather.10
  363.8 58.2 reduce-scatter.4
  424.2 110.7 reduce-scatter.6
  537.7 53.7 reduce-scatter.8
  612.3 60.5 reduce-scatter.10

commit v7 on v5

--- a/solution.py
+++ b/solution.py
@@ -88,7 +88,7 @@
         out_c[at, :] = a
         return b[7:8, :], a[7:8, :]
 
-    return lax.fori_loop(0, rows // 8, one, (h, c), unroll=4)
+    return lax.fori_loop(0, rows // 8, one, (h, c), unroll=8)
 
 
 def forward_kernel(
@@ -148,7 +148,7 @@
         prod_ref[at, :] = jnp.where(last, p, pltpu.roll(a, 7, 0))
         return b[0:1, :], a[0:1, :]
 
-    s, p = lax.fori_loop(0, rows // 8, one, (carry[0:1, :], carry[1:2, :]), unroll=4)
+    s, p = lax.fori_loop(0, rows // 8, one, (carry[0:1, :], carry[1:2, :]), unroll=8)
     carry[0:1, :] = s
     carry[1:2, :] = p
     first_ref[...] = carry[...]
@@ -191,14 +191,14 @@
     factor = vec[7:8, :own]
     log_decay = factor * rate
     e = jnp.exp(log_decay)
-    root = jnp.sqrt(minus_expm1(2.0 * log_decay))
-    scale = keep * root + (1.0 - keep)
+    left = minus_expm1(2.0 * log_decay)
+    scale = keep * jnp.sqrt(left) + (1.0 - keep)
 
     adj = adj_ref[...] + prod_ref[...] * suffix_ref[0:1, :]
     hext[0:8, :] = jnp.where(at_start, jnp.broadcast_to(start_ref[0:1, :], (8, own)), before_ref[...])
     hext[8 : 8 + rows, :] = hidden_ref[...]
     before = hext[7 : 7 + rows, :]
-    d_log = keep * (adj * before * e - adj * opening * conv * (e * e) / root)
+    d_log = keep * (adj * before * e - adj * opening * conv * (e * e) * lax.rsqrt(left))
     direct = adj * scale * opening
     g_rate = (d_log * factor * rate * (1.0 - rate)).astype(BF)
     g_open = (adj * scale * conv * opening * (1.0 - opening)).astype(BF)

time: 718 us -> 718 us (level)
  transfers between devices with their start and end apart: 97 -> 97, of which waited for: 27 -> 28; matrix products, arithmetic and copies ran while one was open for 42% -> 42% of each run, Pallas kernels for 11% -> 11%
where the time goes in v7:
time: 718 us; the launch traced here: 710 us
  matrix products  177 us (25%)
  waiting for transfers between devices  127 us (18%)
  local copies, waits for them, and re-layouts  114 us (16%)
  starting transfers between devices  111 us (15%)
  Pallas kernels  77.8 us (11%)
  other arithmetic  51.2 us (7%)
  blocking collectives  35.3 us (5%)
  between operations  17.4 us (2%)
    ppermute x44, waiting for transfers between devices, near(): return lax.ppermute(x, 'dp', [(i, i ^ k) for i in range(self.n_dp)])  103 us
    dot_general x17, matrix products, dot_cols(): lax.dot_general(a, b, (((1,), (1,)), ((), ())), preferred_element_type=F32)  69.2 us
    dot_general x8, matrix products, dot(): lax.dot_general(a, b, (((1,), (0,)), ((), ())), preferred_element_type=F32)  55.8 us
    unnamed x243, local copies, waits for them, and re-layouts  52.8 us
    dot_general x5, matrix products, dot_rows(): lax.dot_general(a, b, (((0,), (0,)), ((), ())), preferred_element_type=F32)  51.7 us
    ppermute x44, starting transfers between devices, near(): return lax.ppermute(x, 'dp', [(i, i ^ k) for i in range(self.n_dp)])  47.6 us
    pallas_call x3, Pallas kernels, call(): pl.pallas_call(kernel, grid_spec=pltpu.PrefetchScalarGridSpec(num_scalar_...  42.8 us
    all_gather x1, blocking collectives, over_z(): return lax.all_gather(x, 'z', axis=0, tiled=True)  20.3 us
  transfers between devices with their start and end apart: 97, of which 28 were waited for; matrix products, arithmetic and copies ran while one was open for 42% of the time, Pallas kernels for 11%

profile of v7, /device:TPU:0, one launch (start us, length us, event | category | flops | bytes accessed | tf_op | source)
XLA Modules:
  0.0 710.2 jit_solution(4527028103393989085)
XLA Ops:
  9.8 14.9 %all_to_all.66 = bf16[8,64,512]{2,1,0:T(8,128)(2,1)} all-to-all(bf16[8,64,512]{2,1,0:T(8,128)(2,1)S(1)} %copy.95), channel_id=1, replica_groups=mesh['dp'=4,'z'=4,'core'=2] {'dp','core'}, dimensions={0} | all-to-all | bytes 1048576 | tf_op jit(solution)/shard_map/all_to_all | solution.py:520
  32.0 20.3 %all_gather.15 = bf16[768,256]{1,0:T(8,128)(2,1)} all-gather(bf16[192,256]{1,0:T(8,128)(2,1)S(1)} %fusion.81), channel_id=1, replica_groups=mesh['dp'=4,'z'=4,'core'=2] {'z'}, dimensions={0}, use_global_device_ids=true | all-gather | bytes 491520 | tf_op jit(solution)/shard_map/all_gather | solution.py:530
  63.9 10.8 %collective-permute-done = bf16[768,256]{1,0:T(8,128)(2,1)} collective-permute-done((bf16[768,256]{1,0:T(8,128)(2,1)}, bf16[768,256]{1,0:T(8,128)(2,1)}, u32[]{:S(2)}, u32[]{:S(2)}) %collective-permute-start) | collective-permute-done | bytes 393248 | tf_op jit(solution)/shard_map/ppermute | solution.py:428
  92.0 8.7 %collective-permute-done.10 = bf16[128,2048]{1,0:T(8,128)(2,1)S(1)} collective-permute-done((bf16[128,2048]{1,0:T(8,128)(2,1)S(1)}, bf16[128,2048]{1,0:T(8,128)(2,1)S(1)}, u32[]{:S(2)}, u32[]{:S(2)}) %collective-permute-start.10) | collective-permute-done | bytes 524320 | tf_op jit(solution)/shard_map/ppermute | solution.py:428
  114.7 9.3 %shard_map.273 = bf16[2048,2048]{1,0:T(8,128)(2,1)} custom-call(f32[1,2048]{1,0:T(1,128)S(1)} %reshape_reshape.15.gain_ref, bf16[256,2048]{1,0:T(8,128)(2,1)S(1)} %bitcast.231, bf16[256,2048]{1,0:T(8,128)(2,1)} %collective-permute-done.8.refs_1_, bf16[256,2048]{1,0:T(8,128)(2,1)S(1)} %collective-permute-done.9.refs_2_, ...), custom_call_target="tpu_custom_call" | custom-call | tf_op jit(solution)/shard_map/pallas_call | solution.py:598
  127.0 8.5 %convolution_convert_fusion.9.inner_ref.prev_ref = bf16[2048,512]{1,0:T(8,128)(2,1)S(1)} fusion(bf16[2048,2048]{1,0:T(8,128)(2,1)} %shard_map.273, bf16[2048,512]{1,0:T(8,128)(2,1)} %all-gather.5.cloned.1.call-done), kind=kOutput, calls=%fused_computation.57 | convolution fusion | flops 4296015872 | bytes 12582912 | tf_op jit(solution)/shard_map/dot_general | solution.py:40
  150.4 12.2 %shard_map.274 = (f32[2048,384]{1,0:T(8,128)}, f32[2048,384]{1,0:T(8,128)}, f32[2048,384]{1,0:T(8,128)}, f32[32,384]{1,0:T(8,128)S(1)}) custom-call(s32[1]{0:T(128)} %bitcast.core_ref, bf16[2048,512]{1,0:T(8,128)(2,1)S(1)} %convolution_convert_fusion.9.inner_ref.prev_ref, bf16[2048,512]{1,0:T(8,128)(2,1)S(1)} %convolution_convert_fusion.9.inner_ref.prev_ref, ...), custom_call_target="tpu_custom_call" | custom-call | tf_op jit(solution)/shard_map/pallas_call | solution.py:407
  162.7 6.0 collective-permute-start.19
  187.5 7.1 fusion.115.branch_ref
  212.2 8.4 %collective-permute-done.34 = bf16[128,2048]{1,0:T(8,128)(2,1)S(1)} collective-permute-done((bf16[128,2048]{1,0:T(8,128)(2,1)S(1)}, bf16[128,2048]{1,0:T(8,128)(2,1)S(1)}, u32[]{:S(2)}, u32[]{:S(2)}) %collective-permute-start.34) | collective-permute-done | bytes 524320 | tf_op jit(solution)/shard_map/ppermute | solution.py:428
  232.8 10.5 %collective-permute-done.35.b = bf16[128,2048]{1,0:T(8,128)(2,1)} collective-permute-done((bf16[128,2048]{1,0:T(8,128)(2,1)}, bf16[128,2048]{1,0:T(8,128)(2,1)}, u32[]{:S(2)}, u32[]{:S(2)}) %collective-permute-start.35) | collective-permute-done | bytes 524320 | tf_op jit(solution)/shard_map/ppermute | solution.py:428
  253.0 18.9 %collective-permute-done.36 = bf16[256,2048]{1,0:T(8,128)(2,1)S(1)} collective-permute-done((bf16[256,2048]{1,0:T(8,128)(2,1)S(1)}, bf16[256,2048]{1,0:T(8,128)(2,1)S(1)}, u32[]{:S(2)}, u32[]{:S(2)}) %collective-permute-start.36) | collective-permute-done | bytes 1048608 | tf_op jit(solution)/shard_map/ppermute | solution.py:428
  278.8 5.5 collective-permute-done.38
  291.8 17.8 %fusion.135 = f32[2048,1536]{0,1:T(8,128)S(1)} fusion(bf16[2048,2048]{1,0:T(8,128)(2,1)} %constant_dynamic-update-slice_fusion.21, bf16[2048,1536]{1,0:T(8,128)(2,1)} %all-gather.9.cloned.1.call-done), kind=kOutput, calls=%fused_computation.315 | convolution fusion | flops 12884901888 | bytes 27262976 | tf_op jit(solution)/shard_map/dot_general | solution.py:40
  317.9 10.3 %convolution_convert_fusion.1 = bf16[768,2048]{1,0:T(8,128)(2,1)} fusion(bf16[2048,768]{0,1:T(8,128)(2,1)S(1)} %multiply_convert_fusion.2, bf16[2048,2048]{1,0:T(8,128)(2,1)} %copy-done.82), kind=kOutput, calls=%fused_computation.33 | convolution fusion | flops 6444023808 | bytes 14680064 | tf_op jit(solution)/shard_map/dot_general | solution.py:44
  328.4 17.9 %multiply_convert_fusion = (bf16[2048,768]{0,1:T(8,128)(2,1)S(1)}, bf16[2048,768]{0,1:T(8,128)(2,1)S(1)}) fusion(f32[2048,1536]{0,1:T(8,128)} %copy-done.35, bf16[2048,2048]{1,0:T(8,128)(2,1)} %copy-done.82, bf16[768,2048]{1,0:T(8,128)(2,1)} %all-gather.11.cloned.1.call-done), kind=kOutput, calls=%fused_computation.13 | convolution fusion | flops 6477053952 | bytes 30408704 | tf_op jit(solution)/shard_map/dot_general | solution.py:48
  346.4 7.6 %convolution_convert_fusion.6 = bf16[512,2048]{1,0:T(8,128)(2,1)} fusion(bf16[2048,1536]{1,0:T(8,128)(2,1)} %all-gather.9.cloned.1.call-done, bf16[2048,768]{0,1:T(8,128)(2,1)S(1)} %get-tuple-element.286, bf16[2048,768]{0,1:T(8,128)(2,1)S(1)} %get-tuple-element.285), kind=kOutput, calls=%fused_computation.54 | convolution fusion | flops 3225419776 | bytes 14680064 | tf_op jit(solution)/shard_map/dot_general | solution.py:48
  354.5 6.8 convolution_convert_fusion.5
  365.1 7.0 convert_add_fusion.2
  375.6 6.9 add_convert_fusion.4
  387.9 19.2 %convolution_convert_fusion = bf16[2048,1536]{1,0:T(8,128)(2,1)} fusion(bf16[2048,2048]{1,0:T(8,128)(2,1)} %constant_dynamic-update-slice_fusion.21, bf16[2048,1536]{0,1:T(8,128)(2,1)} %pad_maximum_fusion), kind=kOutput, calls=%fused_computation.10 | convolution fusion | flops 12888047616 | bytes 20971520 | tf_op jit(solution)/shard_map/dot_general | solution.py:44
  413.9 8.4 %collective-permute-done.51.b = bf16[128,2048]{1,0:T(8,128)(2,1)S(1)} collective-permute-done((bf16[128,2048]{1,0:T(8,128)(2,1)S(1)}, bf16[128,2048]{1,0:T(8,128)(2,1)S(1)}, u32[]{:S(2)}, u32[]{:S(2)}) %collective-permute-start.51) | collective-permute-done | bytes 524320 | tf_op jit(solution)/shard_map/ppermute | solution.py:428
  426.2 6.3 shard_map.276
  456.4 8.1 %collective-permute-done.52 = bf16[256,2048]{1,0:T(8,128)(2,1)} collective-permute-done((bf16[256,2048]{1,0:T(8,128)(2,1)S(1)}, bf16[256,2048]{1,0:T(8,128)(2,1)}, u32[]{:S(2)}, u32[]{:S(2)}) %collective-permute-start.52) | collective-permute-done | bytes 1048608 | tf_op jit(solution)/shard_map/ppermute | solution.py:428
  490.9 7.6 %multiply_convert_fusion.3 = (bf16[2048,384]{1,0:T(8,128)(2,1)}, f32[2048,384]{1,0:T(8,128)}) fusion(f32[2048,384]{1,0:T(8,128)S(1)} %copy-done.37, f32[2048,384]{1,0:T(8,128)S(1)} %copy-done.33, bf16[2048,2048]{1,0:T(8,128)(2,1)S(1)} %constant_dynamic-update-slice_fusion.30, bf16[2048,64]{1,0:T(8,128)(2,1)S(1)} %copy-done.77, ...), kind=kOutput, calls=%fused_computation.49 | convolution fusion | flops 3241672704 | bytes 20709376 | tf_op jit(solution)/shard_map/dot_general | solution.py:40
  498.4 9.8 %shard_map.277 = (f32[2048,384]{1,0:T(8,128)S(1)}, f32[2048,384]{1,0:T(8,128)}, f32[32,384]{1,0:T(8,128)S(1)}) custom-call(s32[1]{0:T(128)} %bitcast.core_ref, f32[2048,384]{1,0:T(8,128)} %get-tuple-element.159.decay_ref, f32[2048,384]{1,0:T(8,128)} %get-tuple-element.349.grad_ref, f32[2048,384]{1,0:T(8,128)} %copy-done.36), custom_call_target="tpu_custom_call" | custom-call | tf_op jit(solution)/shard_map/pallas_call | solution.py:407
  508.4 8.8 %convolution_convert_fusion.11 = bf16[2048,384]{0,1:T(8,128)(2,1)S(1)} fusion(bf16[2048,2048]{1,0:T(8,128)(2,1)} %shard_map.273, bf16[2048,384]{1,0:T(8,128)(2,1)S(1)} %copy-done.83), kind=kOutput, calls=%fused_computation.60 | convolution fusion | flops 3222011904 | bytes 11534336 | tf_op jit(solution)/shard_map/dot_general | solution.py:44
  543.4 20.7 %shard_map.278 = (bf16[2048,512]{1,0:T(8,128)(2,1)S(1)}, f32[64,512]{1,0:T(8,128)S(1)}, f32[32,512]{1,0:T(8,128)S(1)}, f32[256,512]{1,0:T(8,128)S(1)}, f32[256,256]{1,0:T(8,128)S(1)}, /*index=5*/f32[8,512]{1,0:T(8,128)S(1)}) custom-call(s32[1]{0:T(128)} %bitcast.core_ref, bf16[2048,512]{1,0:T(8,128)(2,1)} %copy-done, bf16[2048,512]{1,0:T(8,128)(2,1)} %copy-done, ...), custom_call_target="tpu_custom_call" | custom-call | tf_op jit(solution)/shard_map/pallas_call | solution.py:407
  576.0 9.7 %convolution_convert_fusion.2 = bf16[2048,512]{1,0:T(8,128)(2,1)} fusion(bf16[2048,2048]{1,0:T(8,128)(2,1)} %shard_map.273, bf16[2048,512]{1,0:T(8,128)(2,1)S(1)} %bitcast.235), kind=kOutput, calls=%fused_computation.50 | convolution fusion | flops 4296015872 | bytes 12582912 | tf_op jit(solution)/shard_map/dot_general | solution.py:44
  642.3 8.6 %all-to-all-start.6 = ((f32[32,1,704]{2,1,0:T(1,128)}), f32[32,1,704]{2,1,0:T(1,128)S(1)}, u32[]{:S(2)}, u32[]{:S(2)}) async-start(f32[32,1,704]{2,1,0:T(1,128)} %copy.120), calls=%async_computation.10 | async-start | bytes 196608 | tf_op jit(solution)/shard_map/all_to_all | solution.py:847
  653.1 5.2 shard_map.281
  684.1 11.8 %all-to-all-done.5 = bf16[8,168,512]{2,1,0:T(8,128)(2,1)S(1)} async-done(((bf16[8,168,512]{2,1,0:T(8,128)(2,1)}), bf16[8,168,512]{2,1,0:T(8,128)(2,1)S(1)}, u32[]{:S(2)}, u32[]{:S(2)}) %all-to-all-start.5) | async-done | bytes 1376288 | tf_op jit(solution)/shard_map/all_to_all | solution.py:520
  (671 shorter events, 353.2 us)
Async XLA Ops:
  7.2 119.8 %all-gather.5.cloned.1.call-start = ((), (), s32[]{:S(2)}) async-start(), calls=%async_computation.11 | async-start | bytes 2621440 | tf_op jit(solution)/shard_map/all_gather | solution.py:530
  24.8 59.0 %collective-permute-start.9 = (bf16[256,2048]{1,0:T(8,128)(2,1)S(1)}, bf16[256,2048]{1,0:T(8,128)(2,1)S(1)}, u32[]{:S(2)}, u32[]{:S(2)}) collective-permute-start(bf16[256,2048]{1,0:T(8,128)(2,1)S(1)} %bitcast.228), channel_id=1, source_target_pairs={{0,16},{8,24},{16,0},{24,8},{1,17},{9,25},{17,1},{25,9},{2,18},{10... | collective-permute-start | bytes 3145736 | tf_op jit(solution)/shard_map/ppermute | solution.py:428
  25.5 58.5 %collective-permute-start.8 = (bf16[256,2048]{1,0:T(8,128)(2,1)S(1)}, bf16[256,2048]{1,0:T(8,128)(2,1)}, u32[]{:S(2)}, u32[]{:S(2)}) collective-permute-start(bf16[256,2048]{1,0:T(8,128)(2,1)S(1)} %bitcast.229), channel_id=1, source_target_pairs={{0,8},{8,0},{16,24},{24,16},{1,9},{9,1},{17,25},{25,17},{2,10},{10... | collective-permute-start | bytes 3145736 | tf_op jit(solution)/shard_map/ppermute | solution.py:428
  56.0 117.1 %all-gather.7.cloned.1.call-start = ((), (), s32[]{:S(2)}) async-start(), calls=%async_computation.12 | async-start | bytes 3276800 | tf_op jit(solution)/shard_map/all_gather | solution.py:530
  62.1 26.4 %collective-permute-start.4 = (bf16[768,256]{1,0:T(8,128)(2,1)}, bf16[768,256]{1,0:T(8,128)(2,1)S(1)}, u32[]{:S(2)}, u32[]{:S(2)}) collective-permute-start(bf16[768,256]{1,0:T(8,128)(2,1)} %all_gather.15), channel_id=1, source_target_pairs={{0,1},{1,0},{2,3},{3,2},{4,5},{5,4},{6,7},{7,6},{8,9},{9,8},{10,11... | collective-permute-start | bytes 1179656 | tf_op jit(solution)/shard_map/ppermute | solution.py:431
  83.8 30.3 %collective-permute-start.12 = (bf16[256,2048]{1,0:T(8,128)(2,1)S(1)}, bf16[256,2048]{1,0:T(8,128)(2,1)}, u32[]{:S(2)}, u32[]{:S(2)}) collective-permute-start(bf16[256,2048]{1,0:T(8,128)(2,1)S(1)} %bitcast.230), channel_id=1, source_target_pairs={{0,1},{1,0},{2,3},{3,2},{4,5},{5,4},{6,7},{7,6},{8,9},{9,8},{10,11... | collective-permute-start | bytes 3145736 | tf_op jit(solution)/shard_map/ppermute | solution.py:431
  106.6 28.9 %all-to-all-start.2 = ((bf16[8,64,1536]{2,1,0:T(8,128)(2,1)}), bf16[8,64,1536]{2,1,0:T(8,128)(2,1)}, u32[]{:S(2)}, u32[]{:S(2)}) async-start(bf16[8,64,1536]{2,1,0:T(8,128)(2,1)} %shard_map.271), calls=%async_computation.2 | async-start | bytes 3145728 | tf_op jit(solution)/shard_map/all_to_all | solution.py:520
  110.9 180.9 %all-gather.9.cloned.1.call-start = ((), (), s32[]{:S(2)}) async-start(), calls=%async_computation.13 | async-start | bytes 7864320 | tf_op jit(solution)/shard_map/all_gather | solution.py:530
  135.5 192.9 %all-gather.11.cloned.1.call-start = ((), (), s32[]{:S(2)}) async-start(), calls=%async_computation.14 | async-start | bytes 3932160 | tf_op jit(solution)/shard_map/all_gather | solution.py:530
  139.7 31.3 %collective-permute-start.20 = (bf16[256,2048]{1,0:T(8,128)(2,1)}, bf16[256,2048]{1,0:T(8,128)(2,1)S(1)}, u32[]{:S(2)}, u32[]{:S(2)}) collective-permute-start(bf16[256,2048]{1,0:T(8,128)(2,1)} %bitcast.1.cot_ref), channel_id=1, source_target_pairs={{0,8},{8,0},{16,24},{24,16},{1,9},{9,1},{17,25},{25,17},{2,10},{10... | collective-permute-start | bytes 3145736 | tf_op jit(solution)/shard_map/ppermute | solution.py:428
  141.6 29.4 %collective-permute-start.21 = (bf16[256,2048]{1,0:T(8,128)(2,1)}, bf16[256,2048]{1,0:T(8,128)(2,1)S(1)}, u32[]{:S(2)}, u32[]{:S(2)}) collective-permute-start(bf16[256,2048]{1,0:T(8,128)(2,1)} %bitcast.1.cot_ref), channel_id=1, source_target_pairs={{0,16},{8,24},{16,0},{24,8},{1,17},{9,25},{17,1},{25,9},{2,18},{10... | collective-permute-start | bytes 3145736 | tf_op jit(solution)/shard_map/ppermute | solution.py:428
  147.5 50.1 %collective-permute-start.24 = (bf16[256,2048]{1,0:T(8,128)(2,1)}, bf16[256,2048]{1,0:T(8,128)(2,1)}, u32[]{:S(2)}, u32[]{:S(2)}) collective-permute-start(bf16[256,2048]{1,0:T(8,128)(2,1)} %bitcast.1.cot_ref), channel_id=1, source_target_pairs={{0,1},{1,0},{2,3},{3,2},{4,5},{5,4},{6,7},{7,6},{8,9},{9,8},{10,11... | collective-permute-start | bytes 3145736 | tf_op jit(solution)/shard_map/ppermute | solution.py:431
  207.3 24.5 %collective-permute-start.33 = (bf16[128,2048]{1,0:T(8,128)(2,1)}, bf16[128,2048]{1,0:T(8,128)(2,1)S(1)}, u32[]{:S(2)}, u32[]{:S(2)}) collective-permute-start(bf16[128,2048]{1,0:T(8,128)(2,1)} %get-tuple-element.304), channel_id=1, source_target_pairs={{0,16},{8,24},{16,0},{24,8},{1,17},{9,25},{17,1},{25,9},{2,18},{10... | collective-permute-start | bytes 1572872 | tf_op jit(solution)/shard_map/ppermute | solution.py:428
  224.0 163.8 %reduce-scatter.5.cloned.1.call-start = ((), (), s32[]{:S(2)}) async-start(), calls=%async_computation.15 | async-start | bytes 3932160 | tf_op jit(solution)/shard_map/reduce_scatter | solution.py:527
  247.6 24.3 %collective-permute-start.36 = (bf16[256,2048]{1,0:T(8,128)(2,1)S(1)}, bf16[256,2048]{1,0:T(8,128)(2,1)S(1)}, u32[]{:S(2)}, u32[]{:S(2)}) collective-permute-start(bf16[256,2048]{1,0:T(8,128)(2,1)S(1)} %get-tuple-element.165), channel_id=1, source_target_pairs={{0,8},{8,0},{16,24},{24,16},{1,9},{9,1},{17,25},{25,17},{2,10},{10... | collective-permute-start | bytes 3145736 | tf_op jit(solution)/shard_map/ppermute | solution.py:428
  328.2 194.8 %reduce-scatter.7.cloned.1.call-start = ((), (), s32[]{:S(2)}) async-start(), calls=%async_computation.16 | async-start | bytes 7864320 | tf_op jit(solution)/shard_map/reduce_scatter | solution.py:527
  384.9 24.7 %collective-permute-start.47 = (bf16[128,2048]{1,0:T(8,128)(2,1)}, bf16[128,2048]{1,0:T(8,128)(2,1)}, u32[]{:S(2)}, u32[]{:S(2)}) collective-permute-start(bf16[128,2048]{1,0:T(8,128)(2,1)} %get-tuple-element.302), channel_id=1, source_target_pairs={{0,8},{8,0},{16,24},{24,16},{1,9},{9,1},{17,25},{25,17},{2,10},{10... | collective-permute-start | bytes 1572872 | tf_op jit(solution)/shard_map/ppermute | solution.py:428
  385.4 26.9 %collective-permute-start.49 = (bf16[128,2048]{1,0:T(8,128)(2,1)}, bf16[128,2048]{1,0:T(8,128)(2,1)S(1)}, u32[]{:S(2)}, u32[]{:S(2)}) collective-permute-start(bf16[128,2048]{1,0:T(8,128)(2,1)} %get-tuple-element.301), channel_id=1, source_target_pairs={{0,16},{8,24},{16,0},{24,8},{1,17},{9,25},{17,1},{25,9},{2,18},{10... | collective-permute-start | bytes 1572872 | tf_op jit(solution)/shard_map/ppermute | solution.py:428
  386.4 26.7 %collective-permute-start.45 = (bf16[128,2048]{1,0:T(8,128)(2,1)}, bf16[128,2048]{1,0:T(8,128)(2,1)S(1)}, u32[]{:S(2)}, u32[]{:S(2)}) collective-permute-start(bf16[128,2048]{1,0:T(8,128)(2,1)} %slice.1071), channel_id=1, source_target_pairs={{0,8},{8,0},{16,24},{24,16},{1,9},{9,1},{17,25},{25,17},{2,10},{10... | collective-permute-start | bytes 1572872 | tf_op jit(solution)/shard_map/ppermute | solution.py:428
  407.1 168.9 %reduce-scatter.9.cloned.1.call-start = ((), (), s32[]{:S(2)}) async-start(), calls=%async_computation.17 | async-start | bytes 3276800 | tf_op jit(solution)/shard_map/reduce_scatter | solution.py:527
  439.3 25.2 %collective-permute-start.52 = (bf16[256,2048]{1,0:T(8,128)(2,1)S(1)}, bf16[256,2048]{1,0:T(8,128)(2,1)}, u32[]{:S(2)}, u32[]{:S(2)}) collective-permute-start(bf16[256,2048]{1,0:T(8,128)(2,1)S(1)} %get-tuple-element.182), channel_id=1, source_target_pairs={{0,8},{8,0},{16,24},{24,16},{1,9},{9,1},{17,25},{25,17},{2,10},{10... | collective-permute-start | bytes 3145736 | tf_op jit(solution)/shard_map/ppermute | solution.py:428
  440.8 24.9 %collective-permute-start.53 = (bf16[256,2048]{1,0:T(8,128)(2,1)S(1)}, bf16[256,2048]{1,0:T(8,128)(2,1)}, u32[]{:S(2)}, u32[]{:S(2)}) collective-permute-start(bf16[256,2048]{1,0:T(8,128)(2,1)S(1)} %get-tuple-element.182), channel_id=1, source_target_pairs={{0,16},{8,24},{16,0},{24,8},{1,17},{9,25},{17,1},{25,9},{2,18},{10... | collective-permute-start | bytes 3145736 | tf_op jit(solution)/shard_map/ppermute | solution.py:428
  479.5 28.8 %collective-permute-start.66 = (bf16[128,2048]{1,0:T(8,128)(2,1)}, bf16[128,2048]{1,0:T(8,128)(2,1)S(1)}, u32[]{:S(2)}, u32[]{:S(2)}) collective-permute-start(bf16[128,2048]{1,0:T(8,128)(2,1)} %slice.823), channel_id=1, source_target_pairs={{0,16},{8,24},{16,0},{24,8},{1,17},{9,25},{17,1},{25,9},{2,18},{10... | collective-permute-start | bytes 1572872 | tf_op jit(solution)/shard_map/ppermute | solution.py:428
  481.8 26.4 %collective-permute-start.65 = (bf16[128,2048]{1,0:T(8,128)(2,1)}, bf16[128,2048]{1,0:T(8,128)(2,1)S(1)}, u32[]{:S(2)}, u32[]{:S(2)}) collective-permute-start(bf16[128,2048]{1,0:T(8,128)(2,1)} %slice.1070), channel_id=1, source_target_pairs={{0,8},{8,0},{16,24},{24,16},{1,9},{9,1},{17,25},{25,17},{2,10},{10... | collective-permute-start | bytes 1572872 | tf_op jit(solution)/shard_map/ppermute | solution.py:428
  538.9 46.8 %all-to-all-start.3 = ((bf16[8,64,1536]{2,1,0:T(8,128)(2,1)}), bf16[8,64,1536]{2,1,0:T(8,128)(2,1)}, u32[]{:S(2)}, u32[]{:S(2)}) async-start(bf16[8,64,1536]{2,1,0:T(8,128)(2,1)} %bitcast.260), calls=%async_computation.6 | async-start | bytes 3145728 | tf_op jit(solution)/shard_map/all_to_all | solution.py:520
  543.2 126.8 %reduce-scatter.11.cloned.1.call-start = ((), (), s32[]{:S(2)}) async-start(), calls=%async_computation.18 | async-start | bytes 3645440 | tf_op jit(solution)/shard_map/reduce_scatter | solution.py:527
  616.1 26.2 %all-to-all-start.4 = ((bf16[8,64,640]{2,1,0:T(8,128)(2,1)}), bf16[8,64,640]{2,1,0:T(8,128)(2,1)}, u32[]{:S(2)}, u32[]{:S(2)}) async-start(bf16[8,64,640]{2,1,0:T(8,128)(2,1)} %bitcast.253), calls=%async_computation.7 | async-start | bytes 1310720 | tf_op jit(solution)/shard_map/all_to_all | solution.py:520
  620.4 30.5 %collective-permute-start.77 = (bf16[128,2048]{1,0:T(8,128)(2,1)}, bf16[128,2048]{1,0:T(8,128)(2,1)}, u32[]{:S(2)}, u32[]{:S(2)}) collective-permute-start(bf16[128,2048]{1,0:T(8,128)(2,1)} %get-tuple-element.296), channel_id=1, source_target_pairs={{0,16},{8,24},{16,0},{24,8},{1,17},{9,25},{17,1},{25,9},{2,18},{10... | collective-permute-start | bytes 1572872 | tf_op jit(solution)/shard_map/ppermute | solution.py:428
  622.3 28.6 %collective-permute-start.73 = (bf16[128,2048]{1,0:T(8,128)(2,1)}, bf16[128,2048]{1,0:T(8,128)(2,1)}, u32[]{:S(2)}, u32[]{:S(2)}) collective-permute-start(bf16[128,2048]{1,0:T(8,128)(2,1)} %slice.1069), channel_id=1, source_target_pairs={{0,8},{8,0},{16,24},{24,16},{1,9},{9,1},{17,25},{25,17},{2,10},{10... | collective-permute-start | bytes 1572872 | tf_op jit(solution)/shard_map/ppermute | solution.py:428
  626.0 27.1 %collective-permute-start.79 = (bf16[128,2048]{1,0:T(8,128)(2,1)}, bf16[128,2048]{1,0:T(8,128)(2,1)}, u32[]{:S(2)}, u32[]{:S(2)}) collective-permute-start(bf16[128,2048]{1,0:T(8,128)(2,1)} %fusion.35), channel_id=1, source_target_pairs={{0,8},{8,0},{16,24},{24,16},{1,9},{9,1},{17,25},{25,17},{2,10},{10... | collective-permute-start | bytes 1572872 | tf_op jit(solution)/shard_map/ppermute | solution.py:428
  628.7 24.4 %collective-permute-start.76 = (bf16[128,2048]{1,0:T(8,128)(2,1)}, bf16[128,2048]{1,0:T(8,128)(2,1)}, u32[]{:S(2)}, u32[]{:S(2)}) collective-permute-start(bf16[128,2048]{1,0:T(8,128)(2,1)} %add_convert_fusion.6), channel_id=1, source_target_pairs={{0,16},{8,24},{16,0},{24,8},{1,17},{9,25},{17,1},{25,9},{2,18},{10... | collective-permute-start | bytes 1572872 | tf_op jit(solution)/shard_map/ppermute | solution.py:428
  642.3 24.7 %all-to-all-start.6 = ((f32[32,1,704]{2,1,0:T(1,128)}), f32[32,1,704]{2,1,0:T(1,128)S(1)}, u32[]{:S(2)}, u32[]{:S(2)}) async-start(f32[32,1,704]{2,1,0:T(1,128)} %copy.120), calls=%async_computation.10 | async-start | bytes 196608 | tf_op jit(solution)/shard_map/all_to_all | solution.py:847
  (168 other events, 1780.3 us)
Sparse Core Ops, SparseCore 0:
  24.9 51.6 all-gather.4
  83.9 53.8 all-gather.6
  139.4 114.1 all-gather.8
  255.0 62.5 all-gather.10
  328.3 58.3 reduce-scatter.4
  407.2 109.6 reduce-scatter.6
  523.1 52.3 reduce-scatter.8
  595.0 60.4 reduce-scatter.10
